TPU v7x, 32 devices: a whole 2x2x4 slice. The times are simulated.
32 devices in a mesh: leg: 2 (over y), ping: 8 (over z, core), rng: 2 (over x).
Axes of the slice: x: 2, y: 2, z: 4, core: 2. Of those that a mesh axis runs over, the one named last changes fastest.
Arguments:
- echo: bfloat16 [2, 16384, 256], P(None, ('leg', 'ping'), 'rng'), parts along dimension 1, may hold values from -6 to 6
- steer: bfloat16 [2, 16384, 8192], P(None, ('leg', 'rng'), 'ping'), parts along dimension 1, may hold values from -0.046875 to 0.046875
- offsets: int32 [256], P(('leg', 'ping')), parts along dimension 0, may hold values from 0 to 15
- taps: float32 [256, 4], P(('leg', 'ping')), parts along dimension 0, may hold values from 0.1 to 1
- centers: int32 [512], P(('leg', 'ping', 'rng')), parts along dimension 0, may hold values from 0 to 8191
- halves: int32 [512], P(('leg', 'ping', 'rng')), parts along dimension 0, may hold values from 128 to 1024
Outputs:
- focused: float32 [2, 512, 8192], P(None, ('leg', 'ping', 'rng')), parts along dimension 1
- phase_error: float32 [16384], P('leg'), parts along dimension 0
There are 2 independent parts, one for each index of `leg`. A program takes and returns all parts, laid end to end along the dimension named above; each array names one. Nothing has to cross between parts.
All inputs are finite; a program needn't handle non-finite values.
Results may differ from a plain program's by a relative error of at most 0.0049.
Values may be sent and summed in bfloat16 or wider, within the bound.
No kernel may reach another device: no remote copies, remote signals or barrier semaphores. Data moves between devices by JAX's collectives and lax.ppermute only.
A program may use at most 64 MiB of HBM per device.

v0:
```python
import math

import jax
import jax.numpy as jnp
from jax import lax
from jax.sharding import PartitionSpec as P

PBLK = 64
NTAP = 4
MAXOFF = 16


epsilon = 1e-06


def from_behind(value, axis, steps):
    count = lax.axis_size(axis)
    initial, last = (max(0, -steps), min(count, count - steps))
    return lax.ppermute(value, axis, [(source, source + steps) for source in range(initial, last)])


def shift_segment(segment, offset, weights, length):
    margin = MAXOFF + NTAP - 1
    first_col = margin - offset - (NTAP - 1)
    window = lax.dynamic_slice_in_dim(segment, first_col, length + NTAP - 1, axis=2)
    result = jnp.zeros(segment.shape[:2] + (length,), jnp.float32)
    for tap_index in range(NTAP):
        lead_cols = NTAP - 1 - tap_index
        result = result + weights[tap_index] * window[:, :, lead_cols : lead_cols + length]
    return result


def split_length(length):
    factor_low = 1
    candidate = 1
    while candidate * candidate <= length:
        if length % candidate == 0:
            factor_low = candidate
        candidate = candidate + 1
    return factor_low


def table(rows_count, cols_count, modulus, direction):
    row_ids = jnp.arange(rows_count, dtype=jnp.int32)
    col_ids = jnp.arange(cols_count, dtype=jnp.int32)
    product = row_ids[:, None] * col_ids[None, :] % modulus
    angle = direction * 2.0 * math.pi / modulus * product.astype(jnp.float32)
    return (jnp.cos(angle), jnp.sin(angle))


def transform(real_part, imag_part, direction):
    length = real_part.shape[-1]
    size_low = split_length(length)
    size_high = length // size_low
    lead_shape = real_part.shape[:-1]
    highest = lax.Precision.HIGHEST
    real_grid = real_part.reshape(lead_shape + (size_low, size_high))
    imag_grid = imag_part.reshape(lead_shape + (size_low, size_high))
    first_cos, first_sin = table(size_low, size_low, size_low, direction)
    section_real = jnp.einsum(
        "kn,...nm->...km", first_cos, real_grid, precision=highest
    ) - jnp.einsum("kn,...nm->...km", first_sin, imag_grid, precision=highest)
    section_imag = jnp.einsum(
        "kn,...nm->...km", first_cos, imag_grid, precision=highest
    ) + jnp.einsum("kn,...nm->...km", first_sin, real_grid, precision=highest)
    twist_cos, twist_sin = table(size_low, size_high, length, direction)
    twisted_real = section_real * twist_cos - section_imag * twist_sin
    twisted_imag = section_real * twist_sin + section_imag * twist_cos
    second_cos, second_sin = table(size_high, size_high, size_high, direction)
    final_real = jnp.einsum(
        "bm,...km->...bk", second_cos, twisted_real, precision=highest
    ) - jnp.einsum("bm,...km->...bk", second_sin, twisted_imag, precision=highest)
    final_imag = jnp.einsum(
        "bm,...km->...bk", second_cos, twisted_imag, precision=highest
    ) + jnp.einsum("bm,...km->...bk", second_sin, twisted_real, precision=highest)
    return (final_real.reshape(lead_shape + (length,)), final_imag.reshape(lead_shape + (length,)))


def on_device(echo, steer, offsets, taps, centers, halves):
    margin = MAXOFF + NTAP - 1
    ping_rows = echo.shape[1]
    columns = echo.shape[2]
    lower_rim = from_behind(echo[:, :, columns - margin :], "rng", 1)
    padded = jnp.concatenate([lower_rim, echo], axis=2).astype(jnp.float32)
    blocks = padded.reshape(2, ping_rows // PBLK, PBLK, margin + columns)
    shifted = jax.vmap(
        lambda segment, offset, weights: shift_segment(segment, offset, weights, columns),
        in_axes=(1, 0, 0),
        out_axes=1,
    )(blocks, offsets, taps)
    interp = shifted.reshape(2, ping_rows, columns).astype(jnp.bfloat16)
    echo_piece = lax.all_gather(interp, "rng", axis=2, tiled=True)
    part_real = jnp.einsum(
        "pr,ap->ra", echo_piece[0], steer[0], preferred_element_type=jnp.float32
    ) - jnp.einsum("pr,ap->ra", echo_piece[1], steer[1], preferred_element_type=jnp.float32)
    part_imag = jnp.einsum(
        "pr,ap->ra", echo_piece[0], steer[1], preferred_element_type=jnp.float32
    ) + jnp.einsum("pr,ap->ra", echo_piece[1], steer[0], preferred_element_type=jnp.float32)
    partial_value = jnp.stack([part_real, part_imag])
    reduced = lax.psum_scatter(partial_value, "ping", scatter_dimension=1, tiled=True)
    lines_image = lax.all_to_all(reduced, "rng", split_axis=1, concat_axis=2, tiled=True)
    length = lines_image.shape[2]
    cells = jnp.arange(length, dtype=jnp.int32)
    distance = (cells[None, :] - centers[:, None]) % length
    distance = jnp.minimum(distance, (length - distance) % length)
    inside = (distance <= halves[:, None]).astype(jnp.float32)
    stacked_real = jnp.stack([lines_image[0], lines_image[0] * inside])
    stacked_imag = jnp.stack([lines_image[1], lines_image[1] * inside])
    spec_real, spec_imag = transform(stacked_real, stacked_imag, -1.0)
    window_real = spec_real[1]
    window_imag = spec_imag[1]
    next_real = jnp.roll(window_real, -1, axis=1)
    next_imag = jnp.roll(window_imag, -1, axis=1)
    cross_real = window_real * next_real + window_imag * next_imag
    cross_imag = window_real * next_imag - window_imag * next_real
    angle = 2.0 * math.pi / length * centers.astype(jnp.float32)
    numer_local = jnp.sum(
        cross_real * jnp.sin(angle)[:, None] + cross_imag * jnp.cos(angle)[:, None], axis=0
    )
    denom_local = jnp.sum(window_real * window_real + window_imag * window_imag, axis=0)
    numer, denom = lax.psum((numer_local, denom_local), ("ping", "rng"))
    slope = numer / (denom + epsilon)
    phase_error = (
        jnp.cumsum(slope)
        - slope
        - jnp.arange(length, dtype=jnp.float32) * (jnp.sum(slope) / length)
    )
    cos_phase = jnp.cos(phase_error)[None, :]
    sin_phase = jnp.sin(phase_error)[None, :]
    full_real = spec_real[0]
    full_imag = spec_imag[0]
    fixed_real = full_real * cos_phase + full_imag * sin_phase
    fixed_imag = full_imag * cos_phase - full_real * sin_phase
    out_real, out_imag = transform(fixed_real, fixed_imag, 1.0)
    focused = jnp.stack([out_real, out_imag]) / length
    return (focused, phase_error)


def solution(mesh):
    in_specs = (
        P(None, ("leg", "ping"), "rng"),
        P(None, ("leg", "rng"), "ping"),
        P(("leg", "ping")),
        P(("leg", "ping"), None),
        P(("leg", "ping", "rng")),
        P(("leg", "ping", "rng")),
    )
    out_specs = (P(None, ("leg", "ping", "rng"), None), P("leg"))
    return jax.shard_map(
        on_device, mesh=mesh, in_specs=in_specs, out_specs=out_specs, check_vma=False
    )
```

profile of v0, /device:TPU:8, one launch (start us, length us, event | category | flops | bytes accessed | tf_op | source)
XLA Modules:
  0.0 358.4 jit_solution(16416869152356131206)
XLA Ops:
  7.2 1.2 slice.91
  8.5 3.4 collective-permute-start
  11.9 0.8 slice_bitcast_fusion.9
  12.7 0.7 fusion.111
  13.4 2.5 copy.46
  15.9 7.1 %collective-permute-done = bf16[2,1024,19]{2,1,0:T(8,128)(2,1)S(1)} collective-permute-done((bf16[2,1024,19]{2,1,0:T(8,128)(2,1)S(1)}, bf16[2,1024,19]{2,1,0:T(8,128)(2,1)S(1)}, u32[]{:S(2)}, u32[]{:S(2)}) %collective-permute-start) | collective-permute-done | bytes 77856 | tf_op jit(solution)/shard_map/ppermute | solution.py:19
  23.4 3.0 convert_bitcast_fusion
  26.4 5.5 %gather_fusion = f32[16,2,64,131]{2,1,3,0:T(2,128)S(1)} fusion(f32[16,2,64,147]{2,1,0,3:T(2,128)} %convert_bitcast_fusion, s32[16]{0:T(128)S(1)} %fusion.111), kind=kCustom, calls=%fused_computation | custom fusion | bytes 2146560 | tf_op jit(solution)/shard_map/vmap()/gather | solution.py:25
  31.9 3.5 fusion.184
  35.3 2.8 copy.72
  38.1 3.9 %copy.73 = f32[16,2,64,128]{3,2,1,0:T(8,128)} copy(f32[16,2,64,128]{2,1,3,0:T(2,128)} %get-tuple-element.12) | data formatting | bytes 2097152
  42.0 3.9 %copy.74 = f32[16,2,64,128]{3,2,1,0:T(8,128)} copy(f32[16,2,64,128]{2,1,3,0:T(2,128)} %get-tuple-element.11) | data formatting | bytes 2097152
  45.9 2.1 copy.75
  48.0 2.3 fusion.38
  50.3 0.8 copy.51
  51.4 23.3 %all-gather.2.cloned.1.call-done = bf16[2,1024,256]{2,1,0:T(8,128)(2,1)} async-done(((bf16[2,1024,128]{2,1,0:T(8,128)(2,1)}), bf16[2,1024,256]{2,1,0:T(8,128)(2,1)}) %all-gather.2.cloned.1.call-update) | async-done | bytes 1048592 | tf_op jit(solution)/shard_map/all_gather | solution.py:92
  74.7 8.0 %fusion.2 = f32[256,4096]{1,0:T(8,128)} fusion(bf16[2,4096,1024]{2,1,0:T(8,128)(2,1)} %param.7, bf16[2,1024,256]{2,1,0:T(8,128)(2,1)} %all-gather.2.cloned.1.call-done), kind=kOutput, calls=%fused_computation.4 | convolution fusion | flops 2147483648 | bytes 13107200 | tf_op jit(solution)/shard_map/pr,ap->ra/dot_general | solution.py:95
  82.8 7.9 %fusion = f32[256,4096]{1,0:T(8,128)} fusion(bf16[2,4096,1024]{2,1,0:T(8,128)(2,1)} %param.7, bf16[2,1024,256]{2,1,0:T(8,128)(2,1)S(1)} %copy-done.7), kind=kOutput, calls=%fused_computation.2 | convolution fusion | flops 2147483648 | bytes 13107200 | tf_op jit(solution)/shard_map/pr,ap->ra/dot_general | solution.py:96
  90.8 4.7 %fusion.15 = f32[1,256,4096]{2,1,0:T(8,128)S(1)} fusion(f32[256,4096]{1,0:T(8,128)} %fusion.2, bf16[2,4096,1024]{2,1,0:T(8,128)(2,1)S(1)} %bitcast.144, bf16[2,1024,256]{2,1,0:T(8,128)(2,1)S(1)} %copy-done.7), kind=kOutput, calls=%fused_computation.15 | convolution fusion | flops 2148532224 | bytes 17301504 | tf_op jit(solution)/shard_map/pr,ap->ra/dot_general | solution.py:93
  95.5 7.0 %fusion.21 = f32[1,256,4096]{2,1,0:T(8,128)S(1)} fusion(f32[256,4096]{1,0:T(8,128)} %fusion, bf16[2,4096,1024]{2,1,0:T(8,128)(2,1)} %param.7, bf16[2,1024,256]{2,1,0:T(8,128)(2,1)S(1)} %copy-done.7), kind=kOutput, calls=%fused_computation.17 | convolution fusion | flops 2148532224 | bytes 17301504 | tf_op jit(solution)/shard_map/pr,ap->ra/dot_general | solution.py:98
  102.5 3.8 %pad_maximum_fusion = f32[2,256,4096]{2,1,0:T(8,128)} fusion(f32[1,256,4096]{2,1,0:T(8,128)S(1)} %fusion.21, f32[1,256,4096]{2,1,0:T(8,128)S(1)} %fusion.15), kind=kLoop, calls=%fused_computation.1 | loop fusion | flops 2097152 | bytes 16777216 | tf_op jit(solution)/shard_map/stack | solution.py:99
  106.3 86.9 %reduce-scatter.2.cloned.1.call-done = f32[2,32,4096]{2,1,0:T(8,128)} async-done(((f32[2,256,4096]{2,1,0:T(8,128)}), f32[2,32,4096]{2,1,0:T(8,128)}) %reduce-scatter.2.cloned.1.call-update) | async-done | bytes 1048592 | tf_op jit(solution)/shard_map/reduce_scatter | solution.py:100
  193.2 3.0 copy.52
  196.2 3.7 %all-to-all-start = ((f32[2,32,4096]{2,0,1:T(2,128)}), f32[2,32,4096]{2,0,1:T(2,128)S(1)}, u32[]{:S(2)}, u32[]{:S(2)}) async-start(f32[2,32,4096]{2,0,1:T(2,128)} %copy.52), calls=%async_computation.1 | async-start | bytes 2097152 | tf_op jit(solution)/shard_map/all_to_all | solution.py:101
  200.6 14.1 %all-to-all-done = f32[2,32,4096]{2,0,1:T(2,128)S(1)} async-done(((f32[2,32,4096]{2,0,1:T(2,128)}), f32[2,32,4096]{2,0,1:T(2,128)S(1)}, u32[]{:S(2)}, u32[]{:S(2)}) %all-to-all-start) | async-done | bytes 1048608 | tf_op jit(solution)/shard_map/all_to_all | solution.py:101
  214.7 0.8 copy.77
  216.5 0.6 broadcast_select_fusion.1
  217.1 1.2 fusion.33
  218.3 1.2 fusion.32
  219.4 1.2 fusion.27
  220.6 1.2 fusion.26
  221.8 1.2 fusion.41
  223.0 1.2 fusion.24
  224.3 0.8 slice.134
  225.1 2.4 copy.57
  227.5 2.4 squeeze.40
  229.9 2.1 slice.135
  231.9 1.2 fusion.40
  233.2 1.4 fusion.25
  234.6 1.0 copy-done.1
  236.3 1.0 slice.132
  237.3 0.9 pad_maximum_fusion.8
  238.2 1.5 concatenate.32
  239.7 1.1 copy.58
  240.8 1.9 pad_maximum_fusion.7
  242.7 1.5 concatenate.30
  244.2 1.1 copy.56
  245.3 2.3 add_reduce_fusion
  247.8 0.7 reduce_sum.32
  248.5 0.7 reduce_sum.34
  250.0 1.4 copy.63
  251.6 84.6 %all-reduce.4.cloned.1.call-done = (f32[8192]{0:T(1024)}, f32[8192]{0:T(1024)}) async-done(((f32[8192]{0:T(1024)}, f32[8192]{0:T(1024)}), (f32[8192]{0:T(1024)}, f32[8192]{0:T(1024)})) %all-reduce.4.cloned.1.call-update) | async-done | bytes 65552 | tf_op jit(solution)/shard_map/psum | solution.py:121
  336.1 1.4 fusion.183
  339.1 0.8 fusion.42
  339.9 0.8 fusion.43
  340.7 0.8 fusion.31
  341.5 0.8 fusion.30
  342.3 0.8 fusion.44
  343.1 0.8 fusion.45
  343.9 1.6 fusion.29
  345.6 1.4 copy.64
  347.3 1.6 fusion.28
  348.9 1.4 copy.65
  350.7 1.0 maximum_multiply_fusion
  (57 shorter events, 5.8 us)
Async XLA Ops:
  7.2 67.6 %all-gather.2.cloned.1.call-start = ((), (), s32[]{:S(2)}) async-start(), calls=%async_computation.2 | async-start | bytes 1572864 | tf_op jit(solution)/shard_map/all_gather | solution.py:92
  8.5 14.6 %collective-permute-start = (bf16[2,1024,19]{2,1,0:T(8,128)(2,1)S(1)}, bf16[2,1024,19]{2,1,0:T(8,128)(2,1)S(1)}, u32[]{:S(2)}, u32[]{:S(2)}) collective-permute-start(bf16[2,1024,19]{2,1,0:T(8,128)(2,1)S(1)} %slice.91), channel_id=1, source_target_pairs={{0,1},{2,3},{4,5},{6,7},{8,9},{10,11},{12,13},{14,15},{16,17},{18,... | collective-permute-start | bytes 233480 | tf_op jit(solution)/shard_map/ppermute | solution.py:19
  35.3 10.6 %copy-start = (f32[16,2,64,128]{2,1,3,0:T(2,128)S(1)}, f32[16,2,64,128]{2,1,3,0:T(2,128)}, u32[]{:S(2)}) copy-start(f32[16,2,64,128]{2,1,3,0:T(2,128)} %get-tuple-element.13) | copy-start | bytes 3145732
  51.2 142.0 %reduce-scatter.2.cloned.1.call-start = ((), (), s32[]{:S(2)}) async-start(), calls=%async_computation.3 | async-start | bytes 9437184 | tf_op jit(solution)/shard_map/reduce_scatter | solution.py:100
  74.7 8.1 %copy-start.7 = (bf16[2,1024,256]{2,1,0:T(8,128)(2,1)S(1)}, bf16[2,1024,256]{2,1,0:T(8,128)(2,1)}, u32[]{:S(2)}) copy-start(bf16[2,1024,256]{2,1,0:T(8,128)(2,1)} %all-gather.2.cloned.1.call-done) | copy-start | bytes 3145732
  74.7 16.0 %slice-start.1 = ((s8[16777216]{0:T(1024)(128)(4,1)}), s8[4194304]{0:T(1024)(128)(4,1)S(1)}, s32[]{:S(2)}) async-start(s8[16777216]{0:T(1024)(128)(4,1)} %bitcast.143), calls=%async_computation.6 | async-start | bytes 8388608
  74.7 16.0 %slice-start.2 = ((s8[16777216]{0:T(1024)(128)(4,1)}), s8[4194304]{0:T(1024)(128)(4,1)S(1)}, s32[]{:S(2)}) async-start(s8[16777216]{0:T(1024)(128)(4,1)} %bitcast.143), calls=%async_computation.7 | async-start | bytes 8388608
  74.7 16.0 %slice-start.3 = ((s8[16777216]{0:T(1024)(128)(4,1)}), s8[4194304]{0:T(1024)(128)(4,1)S(1)}, s32[]{:S(2)}) async-start(s8[16777216]{0:T(1024)(128)(4,1)} %bitcast.143), calls=%async_computation.8 | async-start | bytes 8388608
  82.8 8.0 %slice-start.4 = ((s8[16777216]{0:T(1024)(128)(4,1)}), s8[4194304]{0:T(1024)(128)(4,1)S(1)}, s32[]{:S(2)}) async-start(s8[16777216]{0:T(1024)(128)(4,1)} %bitcast.143), calls=%async_computation.9 | async-start | bytes 8388608
  106.3 94.3 %copy-start.6 = (s32[16]{0:T(128)S(1)}, s32[16]{0:T(128)}, u32[]{:S(2)}) copy-start(s32[16]{0:T(128)} %param.10) | copy-start | bytes 196
  196.2 20.3 %copy-start.5 = (s32[16]{0:T(128)S(1)}, s32[16]{0:T(128)}, u32[]{:S(2)}) copy-start(s32[16]{0:T(128)} %param.11) | copy-start | bytes 196
  196.2 18.5 %all-to-all-start = ((f32[2,32,4096]{2,0,1:T(2,128)}), f32[2,32,4096]{2,0,1:T(2,128)S(1)}, u32[]{:S(2)}, u32[]{:S(2)}) async-start(f32[2,32,4096]{2,0,1:T(2,128)} %copy.52), calls=%async_computation.1 | async-start | bytes 2097152 | tf_op jit(solution)/shard_map/all_to_all | solution.py:101
  199.9 136.2 %all-reduce.4.cloned.1.call-start = ((), (), s32[]{:S(2)}) async-start(), calls=%async_computation.4 | async-start | bytes 131072 | tf_op jit(solution)/shard_map/psum | solution.py:121
  233.2 4.2 %slice-start = ((f32[16,8192]{1,0:T(8,128)}), f32[16,1]{1,0:T(8,128)S(1)}, s32[]{:S(2)}) async-start(f32[16,8192]{1,0:T(8,128)} %squeeze.40), calls=%async_computation.5 | async-start | bytes 16384 | tf_op jit(solution)/shard_map/jit(_roll_static)/slice | solution.py:113
  234.6 1.0 copy-start.1
  235.6 1.8 copy-start.3
  237.3 8.0 %copy-start.2 = (f32[2,16,128,64]{2,3,1,0:T(8,128)S(1)}, f32[2,16,128,64]{2,3,1,0:T(8,128)}, u32[]{:S(2)}) copy-start(f32[2,16,128,64]{2,3,1,0:T(8,128)} %copy-done.1) | copy-start | bytes 3145732
  339.0 4.1 %copy-start.4 = (f32[8192]{0:T(1024)}, f32[8192]{0:T(1024)S(1)}, u32[]{:S(2)}) copy-start(f32[8192]{0:T(1024)S(1)} %get-tuple-element.7) | copy-start | bytes 98308
Sparse Core Ops, SparseCore 0:
  51.3 23.4 all-gather.1
  106.4 86.7 reduce-scatter.1
  249.4 86.7 all-reduce.3
where the time goes:
time: 365 us; the launch traced here: 358 us
  waiting for transfers between devices  216 us (59%)
  local copies, waits for them, and re-layouts  55.2 us (15%)
  matrix products  45.5 us (12%)
  other arithmetic  18.8 us (5%)
  between operations  15 us (4%)
  starting transfers between devices  7.84 us (2%)
    reduce_scatter x1, waiting for transfers between devices, on_device(): lax.psum_scatter(partial_value, 'ping', scatter_dimension=1, tiled=True)  86.9 us
    psum x1, waiting for transfers between devices, on_device(): numer, denom = lax.psum((numer_local, denom_local), ('ping', 'rng'))  84.6 us
    all_gather x1, waiting for transfers between devices, on_device(): echo_piece = lax.all_gather(interp, 'rng', axis=2, tiled=True)  23.3 us
    all_to_all x1, waiting for transfers between devices, on_device(): lax.all_to_all(reduced, 'rng', split_axis=1, concat_axis=2, tiled=True)  14.1 us
    unnamed x28, local copies, waits for them, and re-layouts  13.7 us
    dot_general x1, matrix products, on_device(): jnp.einsum('pr,ap->ra', echo_piece[1], steer[1], preferred_element_type=j...  8.04 us
    dot_general x1, matrix products, on_device(): jnp.einsum('pr,ap->ra', echo_piece[0], steer[1], preferred_element_type=j...  7.94 us
  transfers between devices with their start and end apart: 5, of which 5 were waited for; matrix products, arithmetic and copies ran while one was open for 2% of the time, Pallas kernels for 0%

commit v1 on v0

v1 whole, which is shorter than its diff:
```python
import functools
import math

import jax
import jax.numpy as jnp
import numpy as np
from jax import lax
from jax.experimental import pallas as pl
from jax.experimental.pallas import tpu as pltpu
from jax.sharding import PartitionSpec as P

PBLK = 64
NTAP = 4
LANES = 128
CHUNKS = 4
EPSILON = 1e-06
BF16 = jnp.bfloat16
F32 = jnp.float32
SENT = jnp.float16


def two_terms(table):
    high = table.astype(np.float32).astype(jnp.bfloat16)
    low = (table - high.astype(np.float64)).astype(np.float32).astype(jnp.bfloat16)
    return high, low


def dft_tables(length, direction):
    rows = length // LANES

    def waves(count, other, modulus):
        grid = np.outer(np.arange(count), np.arange(other)) % modulus
        angle = direction * 2.0 * math.pi / modulus * grid
        return np.cos(angle), np.sin(angle)

    scale = 1.0 if direction < 0 else 1.0 / length
    cos, sin = waves(rows, rows, rows)
    high, low = two_terms(scale * np.block([[cos, -sin], [sin, cos]]))
    over_rows = np.concatenate([high, high, low], axis=1)
    cos, sin = waves(LANES, LANES, LANES)
    high, low = two_terms(np.block([[cos, sin], [-sin, cos]]))
    over_lanes = np.concatenate([high, high, low], axis=0)
    cos, sin = waves(rows, LANES, length)
    twist = np.stack([cos, sin]).astype(np.float32)
    return over_rows, over_lanes, twist


def sum_tables(length):
    rows = length // LANES
    below = np.tril(np.ones((rows, rows)), -1)
    before = np.triu(np.ones((LANES, LANES)), 1)
    across = np.concatenate([before, np.ones((LANES, LANES))], axis=1)
    return (
        np.concatenate([below] * 3, axis=1).astype(jnp.bfloat16),
        np.concatenate([across] * 3, axis=0).astype(jnp.bfloat16),
    )


def interp_kernel(starts_ref, offsets_ref, taps_ref, echo_ref, left_ref):
    step = pl.program_id(0)
    lines = echo_ref.shape[2]
    sets = starts_ref.shape[0]
    size = lines // sets
    column = lax.broadcasted_iota(jnp.int32, (PBLK, lines), 1)
    sides = []
    for part in range(2):
        pieces = []
        for sub in range(LANES // PBLK):
            block = step * (LANES // PBLK) + sub
            offset = offsets_ref[block]
            value = echo_ref[part, sub * PBLK : (sub + 1) * PBLK, :].astype(F32)
            moved = pltpu.roll(value, offset, 1)
            moved = jnp.where(column >= offset, moved, 0.0)
            total = taps_ref[block * NTAP] * moved
            for tap in range(1, NTAP):
                moved = jnp.where(column >= 1, pltpu.roll(moved, 1, 1), 0.0)
                total = total + taps_ref[block * NTAP + tap] * moved
            pieces.append(total)
        both = jnp.concatenate(pieces, axis=0).astype(BF16).astype(F32)
        sides.append(jnp.transpose(both))
    real, imag = (side.astype(BF16) for side in sides)
    minus = (-sides[1]).astype(BF16)
    for at in range(sets):
        rows = slice(at * size, (at + 1) * size)
        first = pl.multiple_of(starts_ref[at], size)
        left_ref[0, pl.ds(first, size), :] = real[rows]
        left_ref[1, pl.ds(first, size), :] = minus[rows]
        first = pl.multiple_of(first + size, size)
        left_ref[0, pl.ds(first, size), :] = imag[rows]
        left_ref[1, pl.ds(first, size), :] = real[rows]


def interpolate(starts, offsets, taps, echo):
    pings, lines = echo.shape[1:]
    scalars = pl.BlockSpec(memory_space=pltpu.SMEM)
    return pl.pallas_call(
        interp_kernel,
        grid=(pings // LANES,),
        out_shape=jax.ShapeDtypeStruct((2, 2 * lines, pings), BF16),
        in_specs=[
            scalars,
            scalars,
            scalars,
            pl.BlockSpec((2, LANES, lines), lambda i: (0, i, 0)),
        ],
        out_specs=pl.BlockSpec((2, 2 * lines, LANES), lambda i: (0, 0, i)),
        compiler_params=pltpu.CompilerParams(vmem_limit_bytes=48 * 2**20),
        cost_estimate=pl.CostEstimate(flops=16 * pings * lines, bytes_accessed=12 * pings * lines, transcendentals=0),
        name="interp",
    )(starts, offsets, taps.reshape(-1), echo)


def image_kernel(left_ref, steer_ref, mine_ref, theirs_ref):
    contract = (((1,), (1,)), ((), ()))
    half = mine_ref.shape[0]
    for rows, out_ref in ((slice(half, None), theirs_ref), (slice(0, half), mine_ref)):
        total = lax.dot_general(left_ref[0, rows, :], steer_ref[0], contract, preferred_element_type=F32)
        total = total + lax.dot_general(left_ref[1, rows, :], steer_ref[1], contract, preferred_element_type=F32)
        out_ref[...] = total


def partial_image(left, steer, chunk):
    _, rows, pings = left.shape
    cells = steer.shape[1] // CHUNKS
    tile = math.gcd(cells, 512 if rows <= 512 else 128)
    steps = cells // tile
    half = rows // 2
    return pl.pallas_call(
        image_kernel,
        grid=(steps,),
        out_shape=(jax.ShapeDtypeStruct((half, cells), F32),) * 2,
        in_specs=[
            pl.BlockSpec((2, rows, pings), lambda i: (0, 0, 0)),
            pl.BlockSpec((2, tile, pings), lambda i: (0, chunk * steps + i, 0)),
        ],
        out_specs=(pl.BlockSpec((half, tile), lambda i: (0, i)),) * 2,
        compiler_params=pltpu.CompilerParams(vmem_limit_bytes=56 * 2**20),
        cost_estimate=pl.CostEstimate(
            flops=4 * rows * cells * pings, bytes_accessed=4 * cells * pings + 8 * half * cells, transcendentals=0
        ),
        name="image",
    )(left, steer)


def split_terms(value):
    high = value.astype(BF16)
    low = (value - high.astype(F32)).astype(BF16)
    return high, low


def forward(lines_pair, over_rows_ref, over_lanes_ref, twist_ref):
    rows = lines_pair[0][0].shape[0]
    grid = jnp.concatenate([jnp.concatenate(line, axis=0) for line in lines_pair], axis=1)
    high, low = split_terms(grid)
    first = jnp.dot(
        over_rows_ref[...], jnp.concatenate([high, low, high], axis=0), preferred_element_type=F32
    )
    twisted = []
    for at in range(len(lines_pair)):
        real = first[:rows, at * LANES : (at + 1) * LANES]
        imag = first[rows:, at * LANES : (at + 1) * LANES]
        cos, sin = twist_ref[0], twist_ref[1]
        twisted.append(jnp.concatenate([real * cos - imag * sin, real * sin + imag * cos], axis=1))
    high, low = split_terms(jnp.concatenate(twisted, axis=0))
    second = jnp.dot(
        jnp.concatenate([high, low, high], axis=1), over_lanes_ref[...], preferred_element_type=F32
    )
    return [second[at * rows : (at + 1) * rows] for at in range(len(lines_pair))]


def gradient_kernel(
    count,
    tile_ref,
    centers_ref,
    halves_ref,
    turn_ref,
    over_rows_ref,
    over_lanes_ref,
    twist_ref,
    *refs,
):
    own_refs, far_refs, (grid_ref, sums_ref) = refs[:CHUNKS], refs[CHUNKS:-2], refs[-2:]
    lines = own_refs[0].shape[0] // 2
    chunk_rows = own_refs[0].shape[1] // LANES
    rows = grid_ref.shape[1] // lines
    length = rows * LANES
    for chunk in range(CHUNKS):
        for piece in range(count):
            source = own_refs[chunk] if piece == 0 else far_refs[chunk].at[piece - 1]
            base = (tile_ref[piece] * CHUNKS + chunk) * chunk_rows
            for row in range(chunk_rows):
                first = pl.multiple_of((base + row) * lines, lines)
                for part in range(2):
                    grid_ref[part, pl.ds(first, lines), :] = source[
                        part * lines : (part + 1) * lines, row * LANES : (row + 1) * LANES
                    ]
    cell = lax.broadcasted_iota(jnp.int32, (rows, LANES), 0) * LANES + lax.broadcasted_iota(
        jnp.int32, (rows, LANES), 1
    )
    bottom = lax.broadcasted_iota(jnp.int32, (rows, LANES), 0) == rows - 1
    numer = jnp.zeros((rows, LANES), F32)
    denom = jnp.zeros((rows, LANES), F32)
    for pair in range(0, lines, 2):
        windowed = []
        for line in (pair, pair + 1):
            away = cell - centers_ref[line]
            away = jnp.where(away < 0, away + length, away)
            inside = jnp.minimum(away, length - away) <= halves_ref[line]
            windowed.append(
                [jnp.where(inside, grid_ref[part, pl.ds(line, rows, stride=lines), :], 0.0) for part in range(2)]
            )
        bins = forward(windowed, over_rows_ref, over_lanes_ref, twist_ref)
        for line, value in zip((pair, pair + 1), bins):
            real, imag = value[:, :LANES], value[:, LANES:]
            turned = []
            for side in (real, imag):
                up = pltpu.roll(side, rows - 1, 0)
                turned.append(jnp.where(bottom, pltpu.roll(up, LANES - 1, 1), up))
            next_real, next_imag = turned
            cross_real = real * next_real + imag * next_imag
            cross_imag = real * next_imag - imag * next_real
            numer = numer + (cross_real * turn_ref[1, line] + cross_imag * turn_ref[0, line])
            denom = denom + (real * real + imag * imag)
    sums_ref[0] = numer
    sums_ref[1] = denom


def gradient(tiles, centers, halves, turn, tables, own, far):
    count = tiles.shape[0]
    lines, cells = own[0].shape[0] // 2, own[0].shape[1]
    length = count * cells * CHUNKS
    scalars = pl.BlockSpec(memory_space=pltpu.SMEM)
    whole = pl.BlockSpec(memory_space=pltpu.VMEM)
    return pl.pallas_call(
        functools.partial(gradient_kernel, count),
        out_shape=(
            jax.ShapeDtypeStruct((2, length // LANES * lines, LANES), F32),
            jax.ShapeDtypeStruct((2, length // LANES, LANES), F32),
        ),
        in_specs=[scalars] * 4 + [whole] * (3 + 2 * CHUNKS),
        out_specs=(whole, whole),
        compiler_params=pltpu.CompilerParams(vmem_limit_bytes=40 * 2**20),
        cost_estimate=pl.CostEstimate(flops=2400 * lines * length, bytes_accessed=16 * lines * length, transcendentals=0),
        name="gradient",
    )(tiles, centers, halves, turn, *tables, *own, *far)


def spectrum_kernel(lines, over_rows_ref, over_lanes_ref, twist_ref, grid_ref, bins_ref):
    rows = grid_ref.shape[1] // lines
    for pair in range(0, lines, 2):
        both = [
            [grid_ref[part, pl.ds(line, rows, stride=lines), :] for part in range(2)] for line in (pair, pair + 1)
        ]
        for line, value in zip((pair, pair + 1), forward(both, over_rows_ref, over_lanes_ref, twist_ref)):
            bins_ref[line * rows : (line + 1) * rows, :] = value


def spectrum(tables, grid, lines):
    whole = pl.BlockSpec(memory_space=pltpu.VMEM)
    rows = grid.shape[1] // lines
    return pl.pallas_call(
        functools.partial(spectrum_kernel, lines),
        out_shape=jax.ShapeDtypeStruct((lines * rows, 2 * LANES), F32),
        in_specs=[whole] * 4,
        out_specs=whole,
        compiler_params=pltpu.CompilerParams(vmem_limit_bytes=40 * 2**20),
        cost_estimate=pl.CostEstimate(
            flops=2400 * lines * rows * LANES, bytes_accessed=16 * lines * rows * LANES, transcendentals=0
        ),
        name="spectrum",
    )(*tables, grid)


def three_terms(value):
    high, rest = value.astype(BF16), value
    rest = value - high.astype(F32)
    middle = rest.astype(BF16)
    low = (rest - middle.astype(F32)).astype(BF16)
    return [high, middle, low]


def focus_kernel(
    over_rows_ref, over_lanes_ref, twist_ref, below_ref, across_ref, sums_ref, bins_ref, out_ref, phase_ref, grid_ref
):
    rows = twist_ref.shape[1]
    lines = out_ref.shape[1]
    length = rows * LANES
    slope = sums_ref[0] / (sums_ref[1] + EPSILON)
    inner = jnp.dot(below_ref[...], jnp.concatenate(three_terms(slope), axis=0), preferred_element_type=F32)
    column = inner[rows - 8 :] + slope[rows - 8 :]
    outer = jnp.dot(jnp.concatenate(three_terms(column), axis=1), across_ref[...], preferred_element_type=F32)
    prefix = inner + outer[7:8, :LANES]
    place = lax.broadcasted_iota(jnp.int32, (rows, LANES), 0) + rows * lax.broadcasted_iota(
        jnp.int32, (rows, LANES), 1
    )
    phase = prefix - place.astype(F32) * (outer[7:8, LANES:] * (1.0 / length))
    phase_ref[...] = phase
    cos, sin = jnp.cos(phase), jnp.sin(phase)
    for pair in range(0, lines, 2):
        fixed = []
        for line in (pair, pair + 1):
            real = bins_ref[line * rows : (line + 1) * rows, :LANES]
            imag = bins_ref[line * rows : (line + 1) * rows, LANES:]
            fixed.append(jnp.concatenate([real * cos + imag * sin, imag * cos - real * sin], axis=1))
        high, low = split_terms(jnp.concatenate(fixed, axis=0))
        first = jnp.dot(
            jnp.concatenate([high, low, high], axis=1), over_lanes_ref[...], preferred_element_type=F32
        )
        twisted = []
        for at in range(2):
            real = first[at * rows : (at + 1) * rows, :LANES]
            imag = first[at * rows : (at + 1) * rows, LANES:]
            turn_cos, turn_sin = twist_ref[0], twist_ref[1]
            twisted.append(
                jnp.concatenate([real * turn_cos - imag * turn_sin, real * turn_sin + imag * turn_cos], axis=0)
            )
        high, low = split_terms(jnp.concatenate(twisted, axis=1))
        second = jnp.dot(
            over_rows_ref[...], jnp.concatenate([high, low, high], axis=0), preferred_element_type=F32
        )
        for at in range(2):
            for part in range(2):
                grid_ref[part, pl.ds(pair + at, rows, stride=lines), :] = second[
                    part * rows : (part + 1) * rows, at * LANES : (at + 1) * LANES
                ]
    for row in range(rows):
        for part in range(2):
            out_ref[part, :, row * LANES : (row + 1) * LANES] = grid_ref[part, row * lines : (row + 1) * lines, :]


def focus(tables, prefix_tables, sums, bins, lines):
    whole = pl.BlockSpec(memory_space=pltpu.VMEM)
    rows = sums.shape[1]
    return pl.pallas_call(
        focus_kernel,
        out_shape=(
            jax.ShapeDtypeStruct((2, lines, rows * LANES), F32),
            jax.ShapeDtypeStruct((rows, LANES), F32),
        ),
        in_specs=[whole] * 7,
        out_specs=(whole, whole),
        scratch_shapes=[pltpu.VMEM((2, rows * lines, LANES), F32)],
        compiler_params=pltpu.CompilerParams(vmem_limit_bytes=40 * 2**20),
        cost_estimate=pl.CostEstimate(
            flops=2400 * lines * rows * LANES, bytes_accessed=16 * lines * rows * LANES, transcendentals=0
        ),
        name="focus",
    )(*tables, *prefix_tables, sums, bins)


def swap(value, axis, bit):
    count = lax.axis_size(axis)
    return lax.ppermute(value, axis, [(at, at ^ bit) for at in range(count)])


def total_over(value, axis):
    count = lax.axis_size(axis)
    bit = 1
    while bit < count:
        value = value + swap(value, axis, bit)
        bit *= 2
    return value


def gather_lines(value, axis):
    if lax.axis_size(axis) != 2:
        return lax.all_gather(value, axis, axis=2, tiled=True)
    other = swap(value, axis, 1)
    first = lax.axis_index(axis) == 0
    return jnp.concatenate([jnp.where(first, value, other), jnp.where(first, other, value)], axis=2)


def largest(value):
    return jnp.max(jnp.abs(value)).astype(F32)


def common_scale(echo, taps, steer):
    local = jnp.stack([largest(echo), largest(taps), largest(steer)])
    local = jnp.broadcast_to(local[:, None, None], (3, 8, LANES))
    for axis in ("ping", "rng"):
        local = functools.reduce(jnp.maximum, [local] + [swap(local, axis, at) for at in range(1, lax.axis_size(axis))])
    most = local[:, 0, 0]
    terms = 2 * NTAP * steer.shape[2] * lax.axis_size("ping")
    bound = jnp.clip(terms * most[0] * most[1] * most[2], 1e-30, 1e30)
    power = jnp.clip(jnp.floor(jnp.log2(2.0**15 / bound)), -100.0, 100.0)
    return jnp.exp2(power), jnp.exp2(-power)


def start_rows(pings, tiles, lines):
    me, tile = lax.axis_index("ping"), lax.axis_index("rng")
    owner = jnp.arange(pings * tiles, dtype=jnp.int32)
    apart = (owner // tiles) ^ me
    slot = jnp.zeros_like(apart)
    bit = 1
    while bit < pings:
        slot = 2 * slot + (apart & bit) // bit
        bit *= 2
    return (slot * tiles + (owner % tiles - tile) % tiles) * (2 * lines)


def scatter_sum(mine, theirs, scale):
    up, down = scale
    count = lax.axis_size("ping")
    value = mine + swap(theirs, "ping", 1)
    bit = 2
    while bit < count:
        half = value.shape[0] // 2
        got = swap((value[half:] * up).astype(SENT), "ping", bit)
        value = value[:half] + got.astype(F32) * down
        bit *= 2
    return value


def on_device(echo, steer, offsets, taps, centers, halves):
    pings = lax.axis_size("ping")
    tiles = lax.axis_size("rng")
    tile = lax.axis_index("rng")
    lines = centers.shape[0]
    length = steer.shape[1] * tiles

    echo_lines = gather_lines(echo, "rng")
    scale = common_scale(echo, taps, steer)
    left = interpolate(start_rows(pings, tiles, lines), offsets, taps, echo_lines)
    own, far = [], []
    for chunk in range(CHUNKS):
        total = scatter_sum(*partial_image(left, steer, chunk), scale)
        own.append(total[: 2 * lines])
        pieces = []
        for step in range(1, tiles):
            send = (total[2 * lines * step : 2 * lines * (step + 1)] * scale[0]).astype(SENT)
            got = lax.ppermute(send, "rng", [(at, (at + step) % tiles) for at in range(tiles)])
            pieces.append(got.astype(F32) * scale[1])
        far.append(jnp.stack(pieces))

    angle = 2.0 * math.pi / length * centers.astype(F32)
    turn = jnp.stack([jnp.cos(angle), jnp.sin(angle)])
    owners = (tile - jnp.arange(tiles, dtype=jnp.int32)) % tiles
    tables = [jnp.asarray(table) for table in dft_tables(length, -1.0)]
    grid, sums = gradient(owners, centers, halves, turn, tables, own, far)
    sums = total_over(total_over(sums, "ping"), "rng")
    bins = spectrum(tables, grid, lines)
    tables = [jnp.asarray(table) for table in dft_tables(length, 1.0)]
    prefix_tables = [jnp.asarray(table) for table in sum_tables(length)]
    focused, phase = focus(tables, prefix_tables, sums, bins, lines)
    return (focused, phase.T.reshape(-1))


def solution(mesh):
    in_specs = (
        P(None, ("leg", "ping"), "rng"),
        P(None, ("leg", "rng"), "ping"),
        P(("leg", "ping")),
        P(("leg", "ping"), None),
        P(("leg", "ping", "rng")),
        P(("leg", "ping", "rng")),
    )
    out_specs = (P(None, ("leg", "ping", "rng"), None), P("leg"))
    return jax.shard_map(
        on_device, mesh=mesh, in_specs=in_specs, out_specs=out_specs, check_vma=False
    )
```

time: 365 us -> 136 us (0.37)
  the two profiles are of different devices: /device:TPU:8 before, /device:TPU:0 now
where the time goes in v1:
time: 136 us
  waiting for transfers between devices  48.1 us (35%)
  Pallas kernels  36.2 us (27%)
  starting transfers between devices  31.4 us (23%)
  other arithmetic  11.7 us (9%)
  between operations  4.52 us (3%)
  local copies, waits for them, and re-layouts  3.71 us (3%)
    ppermute x25, waiting for transfers between devices, swap(): return lax.ppermute(value, axis, [(at, at ^ bit) for at in range(count)])  45.2 us
    ppermute x25, starting transfers between devices, swap(): return lax.ppermute(value, axis, [(at, at ^ bit) for at in range(count)])  26.3 us
    pallas_call x4, Pallas kernels, partial_image(): pl.pallas_call(image_kernel, grid=(steps,), out_shape=(jax.ShapeDtypeStru...  22.6 us
    reduce_max x2, other arithmetic, largest(): return jnp.max(jnp.abs(value)).astype(F32)  8.34 us
    pallas_call x1, Pallas kernels, interpolate(): pl.pallas_call(interp_kernel, grid=(pings // LANES,), out_shape=jax.Shape...  5.43 us
    ppermute x4, starting transfers between devices, on_device(): lax.ppermute(send, 'rng', [(at, (at + step) % tiles) for at in range(tile...  5.15 us
    pallas_call x1, Pallas kernels, focus(): pl.pallas_call(focus_kernel, out_shape=(jax.ShapeDtypeStruct((2, lines, r...  4.07 us
    ppermute x4, waiting for transfers between devices, on_device(): lax.ppermute(send, 'rng', [(at, (at + step) % tiles) for at in range(tile...  2.89 us
  transfers between devices with their start and end apart: 29, of which 15 were waited for; matrix products, arithmetic and copies ran while one was open for 9% of the time, Pallas kernels for 22%

profile of v1, /device:TPU:0, one launch (start us, length us, event | category | flops | bytes accessed | tf_op | source)
XLA Modules:
  0.0 135.6 jit_solution(16157642070092935547)
XLA Ops:
  0.6 3.0 %collective-permute-start = (bf16[2,1024,128]{2,1,0:T(8,128)(2,1)}, bf16[2,1024,128]{2,1,0:T(8,128)(2,1)S(1)}, u32[]{:S(2)}, u32[]{:S(2)}) collective-permute-start(bf16[2,1024,128]{2,1,0:T(8,128)(2,1)} %param.14), channel_id=1, source_target_pairs={{0,1},{1,0},{2,3},{3,2},{4,5},{5,4},{6,7},{7,6},{8,9},{9,8},{10,11... | collective-permute-start | bytes 1572872 | tf_op jit(solution)/shard_map/ppermute | solution.py:353
  3.6 0.8 copy.17
  4.5 7.7 %abs_reduce_fusion = bf16[]{:T(256)} fusion(bf16[2,4096,1024]{2,1,0:T(8,128)(2,1)} %steer_ref.7), kind=kLoop, calls=%fused_computation | loop fusion | flops 16777215 | bytes 16777218 | tf_op jit(solution)/shard_map/reduce_max | solution.py:374
  13.0 0.6 abs_reduce_fusion.2
  13.6 2.1 %collective-permute-done = bf16[2,1024,128]{2,1,0:T(8,128)(2,1)S(1)} collective-permute-done((bf16[2,1024,128]{2,1,0:T(8,128)(2,1)}, bf16[2,1024,128]{2,1,0:T(8,128)(2,1)S(1)}, u32[]{:S(2)}, u32[]{:S(2)}) %collective-permute-start) | collective-permute-done | bytes 524320 | tf_op jit(solution)/shard_map/ppermute | solution.py:353
  15.8 0.8 broadcast_select_fusion.1
  17.2 0.7 pad_maximum_fusion.2
  18.0 2.4 %collective-permute-start.8 = (f32[3,8,128]{2,1,0:T(8,128)S(1)}, f32[3,8,128]{2,1,0:T(8,128)S(1)}, u32[]{:S(2)}, u32[]{:S(2)}) collective-permute-start(f32[3,8,128]{2,1,0:T(8,128)S(1)} %broadcast_in_dim.2), channel_id=1, source_target_pairs={{0,14},{2,12},{4,10},{6,8},{8,6},{10,4},{12,2},{14,0},{1,15},{3,13... | collective-permute-start | bytes 36872 | tf_op jit(solution)/shard_map/ppermute | solution.py:353
  20.5 1.5 %collective-permute-start.7 = (f32[3,8,128]{2,1,0:T(8,128)S(1)}, f32[3,8,128]{2,1,0:T(8,128)S(1)}, u32[]{:S(2)}, u32[]{:S(2)}) collective-permute-start(f32[3,8,128]{2,1,0:T(8,128)S(1)} %broadcast_in_dim.2), channel_id=1, source_target_pairs={{0,12},{2,14},{4,8},{6,10},{8,4},{10,6},{12,0},{14,2},{1,13},{3,15... | collective-permute-start | bytes 36872 | tf_op jit(solution)/shard_map/ppermute | solution.py:353
  21.9 0.4 collective-permute-start.6
  22.4 2.2 %collective-permute-start.5 = (f32[3,8,128]{2,1,0:T(8,128)S(1)}, f32[3,8,128]{2,1,0:T(8,128)S(1)}, u32[]{:S(2)}, u32[]{:S(2)}) collective-permute-start(f32[3,8,128]{2,1,0:T(8,128)S(1)} %broadcast_in_dim.2), channel_id=1, source_target_pairs={{0,8},{2,10},{4,12},{6,14},{8,0},{10,2},{12,4},{14,6},{1,9},{3,11}... | collective-permute-start | bytes 36872 | tf_op jit(solution)/shard_map/ppermute | solution.py:353
  24.5 0.1 pad_maximum_fusion.echo_ref
  24.7 5.4 %interp.1.left_ref = bf16[2,512,1024]{2,1,0:T(8,128)(2,1)S(1)} custom-call(s32[16]{0:T(128)S(1)} %fusion.17.starts_ref, s32[16]{0:T(128)S(1)} %copy-done.9, f32[64]{0:T(128)S(1)} %reshape.23.taps_ref, bf16[2,1024,256]{2,1,0:T(8,128)(2,1)S(1)} %pad_maximum_fusion.echo_ref), custom_call_target="tpu_custom_call" | custom-call | flops 4194304 | bytes 3145728 | tf_op jit(solution)/shard_map/interp/pallas_call | solution.py:96
  30.1 1.3 copy-done
  31.5 5.6 %image.4 = (f32[256,1024]{1,0:T(8,128)}, f32[256,1024]{1,0:T(8,128)}) custom-call(bf16[2,512,1024]{2,1,0:T(8,128)(2,1)} %copy-done, bf16[2,4096,1024]{2,1,0:T(8,128)(2,1)} %steer_ref.7), custom_call_target="tpu_custom_call" | custom-call | flops 2147483648 | bytes 6291456 | tf_op jit(solution)/shard_map/image/pallas_call | solution.py:128
  37.1 0.2 collective-permute-start.1
  37.2 5.6 %image.5 = (f32[256,1024]{1,0:T(8,128)}, f32[256,1024]{1,0:T(8,128)}) custom-call(bf16[2,512,1024]{2,1,0:T(8,128)(2,1)} %copy-done, bf16[2,4096,1024]{2,1,0:T(8,128)(2,1)} %steer_ref.7), custom_call_target="tpu_custom_call" | custom-call | flops 2147483648 | bytes 6291456 | tf_op jit(solution)/shard_map/image/pallas_call | solution.py:128
  42.9 1.1 collective-permute-start.4
  44.0 0.2 collective-permute-start.12
  44.2 5.6 %image.6 = (f32[256,1024]{1,0:T(8,128)}, f32[256,1024]{1,0:T(8,128)}) custom-call(bf16[2,512,1024]{2,1,0:T(8,128)(2,1)} %copy-done, bf16[2,4096,1024]{2,1,0:T(8,128)(2,1)} %steer_ref.7), custom_call_target="tpu_custom_call" | custom-call | flops 2147483648 | bytes 6291456 | tf_op jit(solution)/shard_map/image/pallas_call | solution.py:128
  49.8 0.8 collective-permute-start.3
  50.7 0.4 collective-permute-start.15
  51.2 5.7 %image.7 = (f32[256,1024]{1,0:T(8,128)}, f32[256,1024]{1,0:T(8,128)}) custom-call(bf16[2,512,1024]{2,1,0:T(8,128)(2,1)} %copy-done, bf16[2,4096,1024]{2,1,0:T(8,128)(2,1)} %steer_ref.7), custom_call_target="tpu_custom_call" | custom-call | flops 2147483648 | bytes 6291456 | tf_op jit(solution)/shard_map/image/pallas_call | solution.py:128
  56.9 0.2 collective-permute-start.18
  57.2 1.5 %collective-permute-start.9 = (f32[3,8,128]{2,1,0:T(8,128)S(1)}, f32[3,8,128]{2,1,0:T(8,128)S(1)}, u32[]{:S(2)}, u32[]{:S(2)}) collective-permute-start(f32[3,8,128]{2,1,0:T(8,128)S(1)} %maximum_maximum_fusion), channel_id=1, source_target_pairs={{0,1},{1,0},{2,3},{3,2},{4,5},{5,4},{6,7},{7,6},{8,9},{9,8},{10,11... | collective-permute-start | bytes 36872 | tf_op jit(solution)/shard_map/ppermute | solution.py:353
  58.7 2.2 %collective-permute-done.9 = f32[3,8,128]{2,1,0:T(8,128)S(1)} collective-permute-done((f32[3,8,128]{2,1,0:T(8,128)S(1)}, f32[3,8,128]{2,1,0:T(8,128)S(1)}, u32[]{:S(2)}, u32[]{:S(2)}) %collective-permute-start.9) | collective-permute-done | bytes 12320 | tf_op jit(solution)/shard_map/ppermute | solution.py:353
  60.9 0.6 fusion.18
  63.5 0.1 add.83
  63.8 1.3 collective-permute-start.10
  65.0 0.1 add.86
  65.2 0.9 collective-permute-start.13
  66.2 0.1 add.89
  66.4 1.2 collective-permute-start.16
  67.6 0.2 add.92
  67.8 0.9 collective-permute-start.19
  68.7 4.3 %collective-permute-done.10 = f16[128,1024]{1,0:T(8,128)(2,1)S(1)} collective-permute-done((f16[128,1024]{1,0:T(8,128)(2,1)S(1)}, f16[128,1024]{1,0:T(8,128)(2,1)S(1)}, u32[]{:S(2)}, u32[]{:S(2)}) %collective-permute-start.10) | collective-permute-done | bytes 262176 | tf_op jit(solution)/shard_map/ppermute | solution.py:353
  73.1 0.1 slice_add_fusion.3
  73.2 2.5 %collective-permute-start.11 = (f16[64,1024]{1,0:T(8,128)(2,1)S(1)}, f16[64,1024]{1,0:T(8,128)(2,1)S(1)}, u32[]{:S(2)}, u32[]{:S(2)}) collective-permute-start(f16[64,1024]{1,0:T(8,128)(2,1)S(1)} %fusion.7), channel_id=1, source_target_pairs={{0,8},{2,10},{4,12},{6,14},{8,0},{10,2},{12,4},{14,6},{1,9},{3,11}... | collective-permute-start | bytes 393224 | tf_op jit(solution)/shard_map/ppermute | solution.py:353
  75.7 7.2 %collective-permute-done.13 = f16[128,1024]{1,0:T(8,128)(2,1)S(1)} collective-permute-done((f16[128,1024]{1,0:T(8,128)(2,1)S(1)}, f16[128,1024]{1,0:T(8,128)(2,1)S(1)}, u32[]{:S(2)}, u32[]{:S(2)}) %collective-permute-start.13) | collective-permute-done | bytes 262176 | tf_op jit(solution)/shard_map/ppermute | solution.py:353
  83.0 1.7 %collective-permute-start.14 = (f16[64,1024]{1,0:T(8,128)(2,1)S(1)}, f16[64,1024]{1,0:T(8,128)(2,1)S(1)}, u32[]{:S(2)}, u32[]{:S(2)}) collective-permute-start(f16[64,1024]{1,0:T(8,128)(2,1)S(1)} %fusion.6), channel_id=1, source_target_pairs={{0,8},{2,10},{4,12},{6,14},{8,0},{10,2},{12,4},{14,6},{1,9},{3,11}... | collective-permute-start | bytes 393224 | tf_op jit(solution)/shard_map/ppermute | solution.py:353
  84.7 5.2 %collective-permute-done.16 = f16[128,1024]{1,0:T(8,128)(2,1)S(1)} collective-permute-done((f16[128,1024]{1,0:T(8,128)(2,1)S(1)}, f16[128,1024]{1,0:T(8,128)(2,1)S(1)}, u32[]{:S(2)}, u32[]{:S(2)}) %collective-permute-start.16) | collective-permute-done | bytes 262176 | tf_op jit(solution)/shard_map/ppermute | solution.py:353
  90.1 0.7 collective-permute-start.17
  90.8 3.9 %collective-permute-done.19 = f16[128,1024]{1,0:T(8,128)(2,1)S(1)} collective-permute-done((f16[128,1024]{1,0:T(8,128)(2,1)S(1)}, f16[128,1024]{1,0:T(8,128)(2,1)S(1)}, u32[]{:S(2)}, u32[]{:S(2)}) %collective-permute-start.19) | collective-permute-done | bytes 262176 | tf_op jit(solution)/shard_map/ppermute | solution.py:353
  94.9 0.1 collective-permute-start.20
  95.1 1.6 %collective-permute-start.21 = (f16[32,1024]{1,0:T(8,128)(2,1)S(1)}, f16[32,1024]{1,0:T(8,128)(2,1)S(1)}, u32[]{:S(2)}, u32[]{:S(2)}) collective-permute-start(f16[32,1024]{1,0:T(8,128)(2,1)S(1)} %get-tuple-element.35), channel_id=1, source_target_pairs={{0,1},{1,0},{2,3},{3,2},{4,5},{5,4},{6,7},{7,6},{8,9},{9,8},{10,11... | collective-permute-start | bytes 196616 | tf_op jit(solution)/shard_map/ppermute | solution.py:431
  96.7 7.4 %collective-permute-done.17 = f16[64,1024]{1,0:T(8,128)(2,1)S(1)} collective-permute-done((f16[64,1024]{1,0:T(8,128)(2,1)S(1)}, f16[64,1024]{1,0:T(8,128)(2,1)S(1)}, u32[]{:S(2)}, u32[]{:S(2)}) %collective-permute-start.17) | collective-permute-done | bytes 131104 | tf_op jit(solution)/shard_map/ppermute | solution.py:353
  104.2 1.6 %collective-permute-done.20 = f16[64,1024]{1,0:T(8,128)(2,1)S(1)} collective-permute-done((f16[64,1024]{1,0:T(8,128)(2,1)S(1)}, f16[64,1024]{1,0:T(8,128)(2,1)S(1)}, u32[]{:S(2)}, u32[]{:S(2)}) %collective-permute-start.20) | collective-permute-done | bytes 131104 | tf_op jit(solution)/shard_map/ppermute | solution.py:353
  105.9 1.6 %collective-permute-start.22 = (f16[32,1024]{1,0:T(8,128)(2,1)S(1)}, f16[32,1024]{1,0:T(8,128)(2,1)S(1)}, u32[]{:S(2)}, u32[]{:S(2)}) collective-permute-start(f16[32,1024]{1,0:T(8,128)(2,1)S(1)} %get-tuple-element.33), channel_id=1, source_target_pairs={{0,1},{1,0},{2,3},{3,2},{4,5},{5,4},{6,7},{7,6},{8,9},{9,8},{10,11... | collective-permute-start | bytes 196616 | tf_op jit(solution)/shard_map/ppermute | solution.py:431
  107.5 0.5 collective-permute-start.23
  108.0 1.5 %collective-permute-start.24 = (f16[32,1024]{1,0:T(8,128)(2,1)S(1)}, f16[32,1024]{1,0:T(8,128)(2,1)S(1)}, u32[]{:S(2)}, u32[]{:S(2)}) collective-permute-start(f16[32,1024]{1,0:T(8,128)(2,1)S(1)} %get-tuple-element.29), channel_id=1, source_target_pairs={{0,1},{1,0},{2,3},{3,2},{4,5},{5,4},{6,7},{7,6},{8,9},{9,8},{10,11... | collective-permute-start | bytes 196616 | tf_op jit(solution)/shard_map/ppermute | solution.py:431
  109.5 1.4 %collective-permute-done.22 = f16[32,1024]{1,0:T(8,128)(2,1)S(1)} collective-permute-done((f16[32,1024]{1,0:T(8,128)(2,1)S(1)}, f16[32,1024]{1,0:T(8,128)(2,1)S(1)}, u32[]{:S(2)}, u32[]{:S(2)}) %collective-permute-start.22) | collective-permute-done | bytes 65568 | tf_op jit(solution)/shard_map/ppermute | solution.py:431
  110.9 0.8 collective-permute-done.23
  111.8 0.7 collective-permute-done.24
  112.5 2.5 %gradient.1 = (f32[2,1024,128]{2,1,0:T(8,128)S(1)}, f32[2,64,128]{2,1,0:T(8,128)S(1)}) custom-call(s32[2]{0:T(128)S(1)} %and_select_fusion.5.tile_ref, s32[16]{0:T(128)S(1)} %copy-done.10, s32[16]{0:T(128)S(1)} %copy-done.11, f32[2,16]{1,0:T(2,128)S(1)} %pad_maximum_fusion.1.turn_ref, bf16[128,384]{1,0:T(8,128)(2,1)S(1)} %copy-done.3, ...), custom_call_target="tpu_custom_call" | custom-call | flops 314572800 | bytes 2097152 | tf_op jit(solution)/shard_map/gradient/pallas_call | solution.py:234
  115.2 1.2 collective-permute-done.25
  116.5 4.3 %collective-permute-done.26 = f32[2,64,128]{2,1,0:T(8,128)S(1)} collective-permute-done((f32[2,64,128]{2,1,0:T(8,128)S(1)}, f32[2,64,128]{2,1,0:T(8,128)S(1)}, u32[]{:S(2)}, u32[]{:S(2)}) %collective-permute-start.26) | collective-permute-done | bytes 65568 | tf_op jit(solution)/shard_map/ppermute | solution.py:353
  120.8 1.4 %collective-permute-start.27 = (f32[2,64,128]{2,1,0:T(8,128)S(1)}, f32[2,64,128]{2,1,0:T(8,128)S(1)}, u32[]{:S(2)}, u32[]{:S(2)}) collective-permute-start(f32[2,64,128]{2,1,0:T(8,128)S(1)} %add.96), channel_id=1, source_target_pairs={{0,8},{2,10},{4,12},{6,14},{8,0},{10,2},{12,4},{14,6},{1,9},{3,11}... | collective-permute-start | bytes 196616 | tf_op jit(solution)/shard_map/ppermute | solution.py:353
  122.1 4.2 %collective-permute-done.27 = f32[2,64,128]{2,1,0:T(8,128)S(1)} collective-permute-done((f32[2,64,128]{2,1,0:T(8,128)S(1)}, f32[2,64,128]{2,1,0:T(8,128)S(1)}, u32[]{:S(2)}, u32[]{:S(2)}) %collective-permute-start.27) | collective-permute-done | bytes 65568 | tf_op jit(solution)/shard_map/ppermute | solution.py:353
  126.4 1.4 %collective-permute-start.28 = (f32[2,64,128]{2,1,0:T(8,128)S(1)}, f32[2,64,128]{2,1,0:T(8,128)S(1)}, u32[]{:S(2)}, u32[]{:S(2)}) collective-permute-start(f32[2,64,128]{2,1,0:T(8,128)S(1)} %add.97), channel_id=1, source_target_pairs={{0,1},{1,0},{2,3},{3,2},{4,5},{5,4},{6,7},{7,6},{8,9},{9,8},{10,11... | collective-permute-start | bytes 196616 | tf_op jit(solution)/shard_map/ppermute | solution.py:353
  127.8 1.6 %spectrum.1.bins_ref = f32[1024,256]{1,0:T(8,128)S(1)} custom-call(bf16[128,384]{1,0:T(8,128)(2,1)S(1)} %copy-done.3, bf16[768,256]{1,0:T(8,128)(2,1)S(1)} %copy-done.1, f32[2,64,128]{2,1,0:T(8,128)S(1)} %copy-done.4, f32[2,1024,128]{2,1,0:T(8,128)S(1)} %get-tuple-element.23.grid_ref), custom_call_target="tpu_custom_call" | custom-call | flops 314572800 | bytes 2097152 | tf_op jit(solution)/shard_map/spectrum/pallas_call | solution.py:261
  129.3 1.4 %collective-permute-done.28 = f32[2,64,128]{2,1,0:T(8,128)S(1)} collective-permute-done((f32[2,64,128]{2,1,0:T(8,128)S(1)}, f32[2,64,128]{2,1,0:T(8,128)S(1)}, u32[]{:S(2)}, u32[]{:S(2)}) %collective-permute-start.28) | collective-permute-done | bytes 65568 | tf_op jit(solution)/shard_map/ppermute | solution.py:353
  130.8 4.1 %focus.1 = (f32[2,16,8192]{2,1,0:T(8,128)}, f32[64,128]{1,0:T(8,128)S(1)}) custom-call(bf16[128,384]{1,0:T(8,128)(2,1)S(1)} %copy-done.6, bf16[768,256]{1,0:T(8,128)(2,1)S(1)} %copy-done.2, f32[2,64,128]{2,1,0:T(8,128)S(1)} %copy-done.7, bf16[64,192]{1,0:T(8,128)(2,1)S(1)} %copy-done.8, bf16[384,256]{1,0:T(8,128)(2,1)S(1)} %copy-done.5, ...), custom_call_target="tpu_custom_call" | custom-call | flops 314572800 | bytes 2097152 | tf_op jit(solution)/shard_map/focus/pallas_call | solution.py:334
  134.8 0.1 copy.18
  134.9 0.7 reshape.24
  (87 shorter events, 1.5 us)
Async XLA Ops:
  0.6 15.1 %collective-permute-start = (bf16[2,1024,128]{2,1,0:T(8,128)(2,1)}, bf16[2,1024,128]{2,1,0:T(8,128)(2,1)S(1)}, u32[]{:S(2)}, u32[]{:S(2)}) collective-permute-start(bf16[2,1024,128]{2,1,0:T(8,128)(2,1)} %param.14), channel_id=1, source_target_pairs={{0,1},{1,0},{2,3},{3,2},{4,5},{5,4},{6,7},{7,6},{8,9},{9,8},{10,11... | collective-permute-start | bytes 1572872 | tf_op jit(solution)/shard_map/ppermute | solution.py:353
  4.5 8.5 %copy-start.10 = (s32[16]{0:T(128)S(1)}, s32[16]{0:T(128)}, u32[]{:S(2)}) copy-start(s32[16]{0:T(128)} %centers_ref.1) | copy-start | bytes 196
  4.5 8.5 %copy-start.17 = (f32[16,4]{0,1:T(4,128)S(1)}, f32[16,4]{0,1:T(4,128)}, u32[]{:S(2)}) copy-start(f32[16,4]{0,1:T(4,128)} %param.17) | copy-start | bytes 772
  4.5 11.3 %copy-start.16 = (bf16[2,1024,128]{2,1,0:T(8,128)(2,1)S(1)}, bf16[2,1024,128]{2,1,0:T(8,128)(2,1)}, u32[]{:S(2)}) copy-start(bf16[2,1024,128]{2,1,0:T(8,128)(2,1)} %param.14) | copy-start | bytes 1572868
  13.6 11.0 %copy-start.9 = (s32[16]{0:T(128)S(1)}, s32[16]{0:T(128)}, u32[]{:S(2)}) copy-start(s32[16]{0:T(128)} %offsets_ref.1) | copy-start | bytes 196
  18.0 24.8 %collective-permute-start.8 = (f32[3,8,128]{2,1,0:T(8,128)S(1)}, f32[3,8,128]{2,1,0:T(8,128)S(1)}, u32[]{:S(2)}, u32[]{:S(2)}) collective-permute-start(f32[3,8,128]{2,1,0:T(8,128)S(1)} %broadcast_in_dim.2), channel_id=1, source_target_pairs={{0,14},{2,12},{4,10},{6,8},{8,6},{10,4},{12,2},{14,0},{1,15},{3,13... | collective-permute-start | bytes 36872 | tf_op jit(solution)/shard_map/ppermute | solution.py:353
  20.5 23.5 %collective-permute-start.7 = (f32[3,8,128]{2,1,0:T(8,128)S(1)}, f32[3,8,128]{2,1,0:T(8,128)S(1)}, u32[]{:S(2)}, u32[]{:S(2)}) collective-permute-start(f32[3,8,128]{2,1,0:T(8,128)S(1)} %broadcast_in_dim.2), channel_id=1, source_target_pairs={{0,12},{2,14},{4,8},{6,10},{8,4},{10,6},{12,0},{14,2},{1,13},{3,15... | collective-permute-start | bytes 36872 | tf_op jit(solution)/shard_map/ppermute | solution.py:353
  21.9 27.9 %collective-permute-start.6 = (f32[3,8,128]{2,1,0:T(8,128)S(1)}, f32[3,8,128]{2,1,0:T(8,128)S(1)}, u32[]{:S(2)}, u32[]{:S(2)}) collective-permute-start(f32[3,8,128]{2,1,0:T(8,128)S(1)} %broadcast_in_dim.2), channel_id=1, source_target_pairs={{0,10},{2,8},{4,14},{6,12},{8,2},{10,0},{12,6},{14,4},{1,11},{3,9}... | collective-permute-start | bytes 36872 | tf_op jit(solution)/shard_map/ppermute | solution.py:353
  22.4 28.3 %collective-permute-start.5 = (f32[3,8,128]{2,1,0:T(8,128)S(1)}, f32[3,8,128]{2,1,0:T(8,128)S(1)}, u32[]{:S(2)}, u32[]{:S(2)}) collective-permute-start(f32[3,8,128]{2,1,0:T(8,128)S(1)} %broadcast_in_dim.2), channel_id=1, source_target_pairs={{0,8},{2,10},{4,12},{6,14},{8,0},{10,2},{12,4},{14,6},{1,9},{3,11}... | collective-permute-start | bytes 36872 | tf_op jit(solution)/shard_map/ppermute | solution.py:353
  30.1 1.3 copy-start
  37.1 26.5 %collective-permute-start.1 = (f32[256,1024]{1,0:T(8,128)}, f32[256,1024]{1,0:T(8,128)S(1)}, u32[]{:S(2)}, u32[]{:S(2)}) collective-permute-start(f32[256,1024]{1,0:T(8,128)} %get-tuple-element.15), channel_id=1, source_target_pairs={{0,2},{2,0},{4,6},{6,4},{8,10},{10,8},{12,14},{14,12},{1,3},{3,1},... | collective-permute-start | bytes 3145736 | tf_op jit(solution)/shard_map/ppermute | solution.py:353
  42.9 7.9 %collective-permute-start.4 = (f32[3,8,128]{2,1,0:T(8,128)S(1)}, f32[3,8,128]{2,1,0:T(8,128)S(1)}, u32[]{:S(2)}, u32[]{:S(2)}) collective-permute-start(f32[3,8,128]{2,1,0:T(8,128)S(1)} %broadcast_in_dim.2), channel_id=1, source_target_pairs={{0,6},{2,4},{4,2},{6,0},{8,14},{10,12},{12,10},{14,8},{1,7},{3,5},... | collective-permute-start | bytes 36872 | tf_op jit(solution)/shard_map/ppermute | solution.py:353
  44.0 21.0 %collective-permute-start.12 = (f32[256,1024]{1,0:T(8,128)}, f32[256,1024]{1,0:T(8,128)S(1)}, u32[]{:S(2)}, u32[]{:S(2)}) collective-permute-start(f32[256,1024]{1,0:T(8,128)} %get-tuple-element.17), channel_id=1, source_target_pairs={{0,2},{2,0},{4,6},{6,4},{8,10},{10,8},{12,14},{14,12},{1,3},{3,1},... | collective-permute-start | bytes 3145736 | tf_op jit(solution)/shard_map/ppermute | solution.py:353
  49.8 7.1 %collective-permute-start.3 = (f32[3,8,128]{2,1,0:T(8,128)S(1)}, f32[3,8,128]{2,1,0:T(8,128)S(1)}, u32[]{:S(2)}, u32[]{:S(2)}) collective-permute-start(f32[3,8,128]{2,1,0:T(8,128)S(1)} %broadcast_in_dim.2), channel_id=1, source_target_pairs={{0,4},{2,6},{4,0},{6,2},{8,12},{10,14},{12,8},{14,10},{1,5},{3,7},... | collective-permute-start | bytes 36872 | tf_op jit(solution)/shard_map/ppermute | solution.py:353
  50.6 6.4 %collective-permute-start.2 = (f32[3,8,128]{2,1,0:T(8,128)S(1)}, f32[3,8,128]{2,1,0:T(8,128)S(1)}, u32[]{:S(2)}, u32[]{:S(2)}) collective-permute-start(f32[3,8,128]{2,1,0:T(8,128)S(1)} %broadcast_in_dim.2), channel_id=1, source_target_pairs={{0,2},{2,0},{4,6},{6,4},{8,10},{10,8},{12,14},{14,12},{1,3},{3,1},... | collective-permute-start | bytes 36872 | tf_op jit(solution)/shard_map/ppermute | solution.py:353
  50.7 12.8 %copy-start.14 = (f32[256,1024]{1,0:T(8,128)S(1)}, f32[256,1024]{1,0:T(8,128)}, u32[]{:S(2)}) copy-start(f32[256,1024]{1,0:T(8,128)} %get-tuple-element.14) | copy-start | bytes 3145732
  50.7 15.4 %collective-permute-start.15 = (f32[256,1024]{1,0:T(8,128)}, f32[256,1024]{1,0:T(8,128)S(1)}, u32[]{:S(2)}, u32[]{:S(2)}) collective-permute-start(f32[256,1024]{1,0:T(8,128)} %get-tuple-element.19), channel_id=1, source_target_pairs={{0,2},{2,0},{4,6},{6,4},{8,10},{10,8},{12,14},{14,12},{1,3},{3,1},... | collective-permute-start | bytes 3145736 | tf_op jit(solution)/shard_map/ppermute | solution.py:353
  56.9 8.2 %copy-start.12 = (f32[256,1024]{1,0:T(8,128)S(1)}, f32[256,1024]{1,0:T(8,128)}, u32[]{:S(2)}) copy-start(f32[256,1024]{1,0:T(8,128)} %get-tuple-element.16) | copy-start | bytes 3145732
  56.9 10.7 %collective-permute-start.18 = (f32[256,1024]{1,0:T(8,128)}, f32[256,1024]{1,0:T(8,128)S(1)}, u32[]{:S(2)}, u32[]{:S(2)}) collective-permute-start(f32[256,1024]{1,0:T(8,128)} %get-tuple-element.21), channel_id=1, source_target_pairs={{0,2},{2,0},{4,6},{6,4},{8,10},{10,8},{12,14},{14,12},{1,3},{3,1},... | collective-permute-start | bytes 3145736 | tf_op jit(solution)/shard_map/ppermute | solution.py:353
  57.2 3.7 %collective-permute-start.9 = (f32[3,8,128]{2,1,0:T(8,128)S(1)}, f32[3,8,128]{2,1,0:T(8,128)S(1)}, u32[]{:S(2)}, u32[]{:S(2)}) collective-permute-start(f32[3,8,128]{2,1,0:T(8,128)S(1)} %maximum_maximum_fusion), channel_id=1, source_target_pairs={{0,1},{1,0},{2,3},{3,2},{4,5},{5,4},{6,7},{7,6},{8,9},{9,8},{10,11... | collective-permute-start | bytes 36872 | tf_op jit(solution)/shard_map/ppermute | solution.py:353
  63.7 2.4 %copy-start.13 = (f32[256,1024]{1,0:T(8,128)S(1)}, f32[256,1024]{1,0:T(8,128)}, u32[]{:S(2)}) copy-start(f32[256,1024]{1,0:T(8,128)} %get-tuple-element.18) | copy-start | bytes 3145732
  63.8 9.3 %collective-permute-start.10 = (f16[128,1024]{1,0:T(8,128)(2,1)S(1)}, f16[128,1024]{1,0:T(8,128)(2,1)S(1)}, u32[]{:S(2)}, u32[]{:S(2)}) collective-permute-start(f16[128,1024]{1,0:T(8,128)(2,1)S(1)} %fusion.3), channel_id=1, source_target_pairs={{0,4},{2,6},{4,0},{6,2},{8,12},{10,14},{12,8},{14,10},{1,5},{3,7},... | collective-permute-start | bytes 786440 | tf_op jit(solution)/shard_map/ppermute | solution.py:353
  65.2 2.4 %copy-start.15 = (f32[256,1024]{1,0:T(8,128)S(1)}, f32[256,1024]{1,0:T(8,128)}, u32[]{:S(2)}) copy-start(f32[256,1024]{1,0:T(8,128)} %get-tuple-element.20) | copy-start | bytes 3145732
  65.2 17.7 %collective-permute-start.13 = (f16[128,1024]{1,0:T(8,128)(2,1)S(1)}, f16[128,1024]{1,0:T(8,128)(2,1)S(1)}, u32[]{:S(2)}, u32[]{:S(2)}) collective-permute-start(f16[128,1024]{1,0:T(8,128)(2,1)S(1)} %fusion.2), channel_id=1, source_target_pairs={{0,4},{2,6},{4,0},{6,2},{8,12},{10,14},{12,8},{14,10},{1,5},{3,7},... | collective-permute-start | bytes 786440 | tf_op jit(solution)/shard_map/ppermute | solution.py:353
  66.4 23.6 %collective-permute-start.16 = (f16[128,1024]{1,0:T(8,128)(2,1)S(1)}, f16[128,1024]{1,0:T(8,128)(2,1)S(1)}, u32[]{:S(2)}, u32[]{:S(2)}) collective-permute-start(f16[128,1024]{1,0:T(8,128)(2,1)S(1)} %fusion.1), channel_id=1, source_target_pairs={{0,4},{2,6},{4,0},{6,2},{8,12},{10,14},{12,8},{14,10},{1,5},{3,7},... | collective-permute-start | bytes 786440 | tf_op jit(solution)/shard_map/ppermute | solution.py:353
  67.8 26.9 %collective-permute-start.19 = (f16[128,1024]{1,0:T(8,128)(2,1)S(1)}, f16[128,1024]{1,0:T(8,128)(2,1)S(1)}, u32[]{:S(2)}, u32[]{:S(2)}) collective-permute-start(f16[128,1024]{1,0:T(8,128)(2,1)S(1)} %fusion), channel_id=1, source_target_pairs={{0,4},{2,6},{4,0},{6,2},{8,12},{10,14},{12,8},{14,10},{1,5},{3,7},... | collective-permute-start | bytes 786440 | tf_op jit(solution)/shard_map/ppermute | solution.py:353
  73.2 21.8 %collective-permute-start.11 = (f16[64,1024]{1,0:T(8,128)(2,1)S(1)}, f16[64,1024]{1,0:T(8,128)(2,1)S(1)}, u32[]{:S(2)}, u32[]{:S(2)}) collective-permute-start(f16[64,1024]{1,0:T(8,128)(2,1)S(1)} %fusion.7), channel_id=1, source_target_pairs={{0,8},{2,10},{4,12},{6,14},{8,0},{10,2},{12,4},{14,6},{1,9},{3,11}... | collective-permute-start | bytes 393224 | tf_op jit(solution)/shard_map/ppermute | solution.py:353
  83.0 13.6 %collective-permute-start.14 = (f16[64,1024]{1,0:T(8,128)(2,1)S(1)}, f16[64,1024]{1,0:T(8,128)(2,1)S(1)}, u32[]{:S(2)}, u32[]{:S(2)}) collective-permute-start(f16[64,1024]{1,0:T(8,128)(2,1)S(1)} %fusion.6), channel_id=1, source_target_pairs={{0,8},{2,10},{4,12},{6,14},{8,0},{10,2},{12,4},{14,6},{1,9},{3,11}... | collective-permute-start | bytes 393224 | tf_op jit(solution)/shard_map/ppermute | solution.py:353
  90.1 14.0 %collective-permute-start.17 = (f16[64,1024]{1,0:T(8,128)(2,1)S(1)}, f16[64,1024]{1,0:T(8,128)(2,1)S(1)}, u32[]{:S(2)}, u32[]{:S(2)}) collective-permute-start(f16[64,1024]{1,0:T(8,128)(2,1)S(1)} %fusion.5), channel_id=1, source_target_pairs={{0,8},{2,10},{4,12},{6,14},{8,0},{10,2},{12,4},{14,6},{1,9},{3,11}... | collective-permute-start | bytes 393224 | tf_op jit(solution)/shard_map/ppermute | solution.py:353
  94.9 11.0 %collective-permute-start.20 = (f16[64,1024]{1,0:T(8,128)(2,1)S(1)}, f16[64,1024]{1,0:T(8,128)(2,1)S(1)}, u32[]{:S(2)}, u32[]{:S(2)}) collective-permute-start(f16[64,1024]{1,0:T(8,128)(2,1)S(1)} %fusion.4), channel_id=1, source_target_pairs={{0,8},{2,10},{4,12},{6,14},{8,0},{10,2},{12,4},{14,6},{1,9},{3,11}... | collective-permute-start | bytes 393224 | tf_op jit(solution)/shard_map/ppermute | solution.py:353
  95.1 17.4 %copy-start.1 = (bf16[768,256]{1,0:T(8,128)(2,1)S(1)}, bf16[768,256]{1,0:T(8,128)(2,1)}, u32[]{:S(2)}) copy-start(bf16[768,256]{1,0:T(8,128)(2,1)} %constant.124.clone.over_lanes_ref) | copy-start | bytes 1179652
  95.1 17.4 %copy-start.3 = (bf16[128,384]{1,0:T(8,128)(2,1)S(1)}, bf16[128,384]{1,0:T(8,128)(2,1)}, u32[]{:S(2)}) copy-start(bf16[128,384]{1,0:T(8,128)(2,1)} %constant.123.clone.over_rows_ref) | copy-start | bytes 294916
  95.1 17.4 %copy-start.4 = (f32[2,64,128]{2,1,0:T(8,128)S(1)}, f32[2,64,128]{2,1,0:T(8,128)}, u32[]{:S(2)}) copy-start(f32[2,64,128]{2,1,0:T(8,128)} %constant.125.clone.twist_ref) | copy-start | bytes 196612
  95.1 17.4 %copy-start.11 = (s32[16]{0:T(128)S(1)}, s32[16]{0:T(128)}, u32[]{:S(2)}) copy-start(s32[16]{0:T(128)} %halves_ref.1) | copy-start | bytes 196
  95.1 14.4 %collective-permute-start.21 = (f16[32,1024]{1,0:T(8,128)(2,1)S(1)}, f16[32,1024]{1,0:T(8,128)(2,1)S(1)}, u32[]{:S(2)}, u32[]{:S(2)}) collective-permute-start(f16[32,1024]{1,0:T(8,128)(2,1)S(1)} %get-tuple-element.35), channel_id=1, source_target_pairs={{0,1},{1,0},{2,3},{3,2},{4,5},{5,4},{6,7},{7,6},{8,9},{9,8},{10,11... | collective-permute-start | bytes 196616 | tf_op jit(solution)/shard_map/ppermute | solution.py:431
  105.9 5.0 %collective-permute-start.22 = (f16[32,1024]{1,0:T(8,128)(2,1)S(1)}, f16[32,1024]{1,0:T(8,128)(2,1)S(1)}, u32[]{:S(2)}, u32[]{:S(2)}) collective-permute-start(f16[32,1024]{1,0:T(8,128)(2,1)S(1)} %get-tuple-element.33), channel_id=1, source_target_pairs={{0,1},{1,0},{2,3},{3,2},{4,5},{5,4},{6,7},{7,6},{8,9},{9,8},{10,11... | collective-permute-start | bytes 196616 | tf_op jit(solution)/shard_map/ppermute | solution.py:431
  107.5 4.3 %collective-permute-start.23 = (f16[32,1024]{1,0:T(8,128)(2,1)S(1)}, f16[32,1024]{1,0:T(8,128)(2,1)S(1)}, u32[]{:S(2)}, u32[]{:S(2)}) collective-permute-start(f16[32,1024]{1,0:T(8,128)(2,1)S(1)} %get-tuple-element.31), channel_id=1, source_target_pairs={{0,1},{1,0},{2,3},{3,2},{4,5},{5,4},{6,7},{7,6},{8,9},{9,8},{10,11... | collective-permute-start | bytes 196616 | tf_op jit(solution)/shard_map/ppermute | solution.py:431
  108.0 4.4 %collective-permute-start.24 = (f16[32,1024]{1,0:T(8,128)(2,1)S(1)}, f16[32,1024]{1,0:T(8,128)(2,1)S(1)}, u32[]{:S(2)}, u32[]{:S(2)}) collective-permute-start(f16[32,1024]{1,0:T(8,128)(2,1)S(1)} %get-tuple-element.29), channel_id=1, source_target_pairs={{0,1},{1,0},{2,3},{3,2},{4,5},{5,4},{6,7},{7,6},{8,9},{9,8},{10,11... | collective-permute-start | bytes 196616 | tf_op jit(solution)/shard_map/ppermute | solution.py:431
  115.0 15.7 %copy-start.2 = (bf16[768,256]{1,0:T(8,128)(2,1)S(1)}, bf16[768,256]{1,0:T(8,128)(2,1)}, u32[]{:S(2)}) copy-start(bf16[768,256]{1,0:T(8,128)(2,1)} %constant.127.clone.over_lanes_ref) | copy-start | bytes 1179652
  115.0 15.7 %copy-start.5 = (bf16[384,256]{1,0:T(8,128)(2,1)S(1)}, bf16[384,256]{1,0:T(8,128)(2,1)}, u32[]{:S(2)}) copy-start(bf16[384,256]{1,0:T(8,128)(2,1)} %constant.130.clone.across_ref) | copy-start | bytes 589828
  115.0 15.7 %copy-start.6 = (bf16[128,384]{1,0:T(8,128)(2,1)S(1)}, bf16[128,384]{1,0:T(8,128)(2,1)}, u32[]{:S(2)}) copy-start(bf16[128,384]{1,0:T(8,128)(2,1)} %constant.126.clone.over_rows_ref) | copy-start | bytes 294916
  115.1 15.7 %copy-start.7 = (f32[2,64,128]{2,1,0:T(8,128)S(1)}, f32[2,64,128]{2,1,0:T(8,128)}, u32[]{:S(2)}) copy-start(f32[2,64,128]{2,1,0:T(8,128)} %constant.128.clone.twist_ref) | copy-start | bytes 196612
  115.1 15.7 %copy-start.8 = (bf16[64,192]{1,0:T(8,128)(2,1)S(1)}, bf16[64,192]{1,0:T(8,128)(2,1)}, u32[]{:S(2)}) copy-start(bf16[64,192]{1,0:T(8,128)(2,1)} %constant.129.clone.below_ref) | copy-start | bytes 73732
  115.1 1.3 collective-permute-start.25
  116.4 4.3 %collective-permute-start.26 = (f32[2,64,128]{2,1,0:T(8,128)S(1)}, f32[2,64,128]{2,1,0:T(8,128)S(1)}, u32[]{:S(2)}, u32[]{:S(2)}) collective-permute-start(f32[2,64,128]{2,1,0:T(8,128)S(1)} %add.95), channel_id=1, source_target_pairs={{0,4},{2,6},{4,0},{6,2},{8,12},{10,14},{12,8},{14,10},{1,5},{3,7},... | collective-permute-start | bytes 196616 | tf_op jit(solution)/shard_map/ppermute | solution.py:353
  120.8 5.6 %collective-permute-start.27 = (f32[2,64,128]{2,1,0:T(8,128)S(1)}, f32[2,64,128]{2,1,0:T(8,128)S(1)}, u32[]{:S(2)}, u32[]{:S(2)}) collective-permute-start(f32[2,64,128]{2,1,0:T(8,128)S(1)} %add.96), channel_id=1, source_target_pairs={{0,8},{2,10},{4,12},{6,14},{8,0},{10,2},{12,4},{14,6},{1,9},{3,11}... | collective-permute-start | bytes 196616 | tf_op jit(solution)/shard_map/ppermute | solution.py:353
  126.4 4.3 %collective-permute-start.28 = (f32[2,64,128]{2,1,0:T(8,128)S(1)}, f32[2,64,128]{2,1,0:T(8,128)S(1)}, u32[]{:S(2)}, u32[]{:S(2)}) collective-permute-start(f32[2,64,128]{2,1,0:T(8,128)S(1)} %add.97), channel_id=1, source_target_pairs={{0,1},{1,0},{2,3},{3,2},{4,5},{5,4},{6,7},{7,6},{8,9},{9,8},{10,11... | collective-permute-start | bytes 196616 | tf_op jit(solution)/shard_map/ppermute | solution.py:353

commit v2 on v1

--- a/solution.py
+++ b/solution.py
@@ -11,12 +11,26 @@
 
 PBLK = 64
 NTAP = 4
+MARGIN = 24
 LANES = 128
-CHUNKS = 4
+SHARES = (12, 12, 8)
 EPSILON = 1e-06
 BF16 = jnp.bfloat16
 F32 = jnp.float32
 SENT = jnp.float16
+
+
+def cuts_of(cells):
+    units, total = cells // LANES, sum(SHARES)
+    sizes = [units * share // total for share in SHARES]
+    if units % total:
+        count = math.gcd(units, len(SHARES))
+        sizes = [units // count] * count
+    cuts, first = [], 0
+    for size in sizes:
+        cuts.append((first * LANES, size * LANES))
+        first += size
+    return cuts
 
 
 def two_terms(table):
@@ -56,38 +70,42 @@
     )
 
 
-def interp_kernel(starts_ref, offsets_ref, taps_ref, echo_ref, left_ref):
+def interp_kernel(starts_ref, offsets_ref, taps_ref, echo_ref, left_ref, turned_ref):
     step = pl.program_id(0)
     lines = echo_ref.shape[2]
     sets = starts_ref.shape[0]
     size = lines // sets
-    column = lax.broadcasted_iota(jnp.int32, (PBLK, lines), 1)
-    sides = []
+    blocks = LANES // PBLK
+    lane = lax.broadcasted_iota(jnp.int32, (size, LANES), 1)
+    weights, rows_back = [], []
+    for sub in range(blocks):
+        block = step * blocks + sub
+        here = lane // PBLK == sub
+        weights.append([jnp.where(here, taps_ref[tap, block], 0.0) for tap in range(NTAP)])
+        rows_back.append(MARGIN - offsets_ref[block])
+
     for part in range(2):
-        pieces = []
-        for sub in range(LANES // PBLK):
-            block = step * (LANES // PBLK) + sub
-            offset = offsets_ref[block]
-            value = echo_ref[part, sub * PBLK : (sub + 1) * PBLK, :].astype(F32)
-            moved = pltpu.roll(value, offset, 1)
-            moved = jnp.where(column >= offset, moved, 0.0)
-            total = taps_ref[block * NTAP] * moved
-            for tap in range(1, NTAP):
-                moved = jnp.where(column >= 1, pltpu.roll(moved, 1, 1), 0.0)
-                total = total + taps_ref[block * NTAP + tap] * moved
-            pieces.append(total)
-        both = jnp.concatenate(pieces, axis=0).astype(BF16).astype(F32)
-        sides.append(jnp.transpose(both))
-    real, imag = (side.astype(BF16) for side in sides)
-    minus = (-sides[1]).astype(BF16)
+        turned_ref[part, :MARGIN, :] = jnp.zeros((MARGIN, LANES), F32)
+        turned_ref[part, MARGIN:, :] = jnp.transpose(echo_ref[part].astype(F32))
+
+    def line_set(at, first):
+        sides = []
+        for part in range(2):
+            total = None
+            for tap in range(NTAP):
+                for sub in range(blocks):
+                    rows = turned_ref[part, pl.ds(rows_back[sub] + (at * size - tap), size), :]
+                    term = weights[sub][tap] * rows
+                    total = term if total is None else total + term
+            sides.append(total)
+        real, imag = sides
+        left_ref[0, pl.ds(first, size), :] = real.astype(BF16)
+        left_ref[1, pl.ds(first, size), :] = (-imag).astype(BF16)
+        left_ref[0, pl.ds(first + size, size), :] = imag.astype(BF16)
+        left_ref[1, pl.ds(first + size, size), :] = real.astype(BF16)
+
     for at in range(sets):
-        rows = slice(at * size, (at + 1) * size)
-        first = pl.multiple_of(starts_ref[at], size)
-        left_ref[0, pl.ds(first, size), :] = real[rows]
-        left_ref[1, pl.ds(first, size), :] = minus[rows]
-        first = pl.multiple_of(first + size, size)
-        left_ref[0, pl.ds(first, size), :] = imag[rows]
-        left_ref[1, pl.ds(first, size), :] = real[rows]
+        line_set(at, pl.multiple_of(starts_ref[at], size))
 
 
 def interpolate(starts, offsets, taps, echo):
@@ -104,10 +122,47 @@
             pl.BlockSpec((2, LANES, lines), lambda i: (0, i, 0)),
         ],
         out_specs=pl.BlockSpec((2, 2 * lines, LANES), lambda i: (0, 0, i)),
+        scratch_shapes=[pltpu.VMEM((2, MARGIN + lines, LANES), F32)],
         compiler_params=pltpu.CompilerParams(vmem_limit_bytes=48 * 2**20),
         cost_estimate=pl.CostEstimate(flops=16 * pings * lines, bytes_accessed=12 * pings * lines, transcendentals=0),
         name="interp",
-    )(starts, offsets, taps.reshape(-1), echo)
+    )(starts, offsets, taps, echo)
+
+
+def largest_kernel(echo_ref, taps_ref, steer_ref, most_ref, here_ref, sems):
+    pieces, sets, rows, width = here_ref.shape
+    copies = [
+        pltpu.make_async_copy(steer_ref.at[:, pl.ds(at * rows, rows), :], here_ref.at[at], sems.at[at])
+        for at in range(pieces)
+    ]
+    for copy in copies:
+        copy.start()
+    for at, ref in enumerate((echo_ref, taps_ref)):
+        most_ref[at] = jnp.full(most_ref.shape[1:], jnp.max(jnp.abs(ref[...]).astype(F32)), F32)
+    most = jnp.zeros((16, width), here_ref.dtype)
+    for at, copy in enumerate(copies):
+        copy.wait()
+        most = jnp.maximum(most, jnp.max(jnp.abs(here_ref[at]).reshape(sets * rows // 16, 16, width), axis=0))
+    most_ref[2] = jnp.full(most_ref.shape[1:], jnp.max(most.astype(F32)), F32)
+
+
+def largest(echo, taps, steer):
+    sets, rows, width = steer.shape
+    pieces = max(1, rows // 512)
+    whole = pl.BlockSpec(memory_space=pltpu.VMEM)
+    return pl.pallas_call(
+        largest_kernel,
+        out_shape=jax.ShapeDtypeStruct((3, 8, LANES), F32),
+        in_specs=[whole, whole, pl.BlockSpec(memory_space=pl.ANY)],
+        out_specs=whole,
+        scratch_shapes=[
+            pltpu.VMEM((pieces, sets, rows // pieces, width), steer.dtype),
+            pltpu.SemaphoreType.DMA((pieces,)),
+        ],
+        compiler_params=pltpu.CompilerParams(vmem_limit_bytes=56 * 2**20),
+        cost_estimate=pl.CostEstimate(flops=steer.size, bytes_accessed=2 * steer.size, transcendentals=0),
+        name="largest",
+    )(echo, taps, steer)
 
 
 def image_kernel(left_ref, steer_ref, mine_ref, theirs_ref):
@@ -119,25 +174,21 @@
         out_ref[...] = total
 
 
-def partial_image(left, steer, chunk):
+def partial_image(left, steer, first, cells):
     _, rows, pings = left.shape
-    cells = steer.shape[1] // CHUNKS
-    tile = math.gcd(cells, 512 if rows <= 512 else 128)
-    steps = cells // tile
+    tile = math.gcd(math.gcd(first, cells), 512 if rows <= 512 else 128)
     half = rows // 2
     return pl.pallas_call(
         image_kernel,
-        grid=(steps,),
+        grid=(cells // tile,),
         out_shape=(jax.ShapeDtypeStruct((half, cells), F32),) * 2,
         in_specs=[
-            pl.BlockSpec((2, rows, pings), lambda i: (0, 0, 0)),
-            pl.BlockSpec((2, tile, pings), lambda i: (0, chunk * steps + i, 0)),
+            pl.BlockSpec(memory_space=pltpu.VMEM),
+            pl.BlockSpec((2, tile, pings), lambda i: (0, first // tile + i, 0)),
         ],
         out_specs=(pl.BlockSpec((half, tile), lambda i: (0, i)),) * 2,
-        compiler_params=pltpu.CompilerParams(vmem_limit_bytes=56 * 2**20),
-        cost_estimate=pl.CostEstimate(
-            flops=4 * rows * cells * pings, bytes_accessed=4 * cells * pings + 8 * half * cells, transcendentals=0
-        ),
+        compiler_params=pltpu.CompilerParams(vmem_limit_bytes=40 * 2**20),
+        cost_estimate=pl.CostEstimate(flops=cells, bytes_accessed=cells, transcendentals=0),
         name="image",
     )(left, steer)
 
@@ -170,30 +221,31 @@
 
 def gradient_kernel(
     count,
+    cuts,
     tile_ref,
     centers_ref,
     halves_ref,
     turn_ref,
+    down_ref,
     over_rows_ref,
     over_lanes_ref,
     twist_ref,
     *refs,
 ):
-    own_refs, far_refs, (grid_ref, sums_ref) = refs[:CHUNKS], refs[CHUNKS:-2], refs[-2:]
+    own_refs, far_refs, (grid_ref, sums_ref) = refs[: len(cuts)], refs[len(cuts) : -2], refs[-2:]
     lines = own_refs[0].shape[0] // 2
-    chunk_rows = own_refs[0].shape[1] // LANES
     rows = grid_ref.shape[1] // lines
     length = rows * LANES
-    for chunk in range(CHUNKS):
+    down = jnp.concatenate([down_ref[...]] * (lines // 8), axis=0)
+    for (start, cells), own_ref, far_ref in zip(cuts, own_refs, far_refs):
         for piece in range(count):
-            source = own_refs[chunk] if piece == 0 else far_refs[chunk].at[piece - 1]
-            base = (tile_ref[piece] * CHUNKS + chunk) * chunk_rows
-            for row in range(chunk_rows):
+            source = own_ref if piece == 0 else far_ref.at[piece - 1]
+            base = tile_ref[piece] * (rows // count) + start // LANES
+            for row in range(cells // LANES):
                 first = pl.multiple_of((base + row) * lines, lines)
                 for part in range(2):
-                    grid_ref[part, pl.ds(first, lines), :] = source[
-                        part * lines : (part + 1) * lines, row * LANES : (row + 1) * LANES
-                    ]
+                    value = source[part * lines : (part + 1) * lines, row * LANES : (row + 1) * LANES]
+                    grid_ref[part, pl.ds(first, lines), :] = value * down
     cell = lax.broadcasted_iota(jnp.int32, (rows, LANES), 0) * LANES + lax.broadcasted_iota(
         jnp.int32, (rows, LANES), 1
     )
@@ -225,24 +277,24 @@
     sums_ref[1] = denom
 
 
-def gradient(tiles, centers, halves, turn, tables, own, far):
+def gradient(tiles, cuts, centers, halves, turn, down, tables, own, far):
     count = tiles.shape[0]
-    lines, cells = own[0].shape[0] // 2, own[0].shape[1]
-    length = count * cells * CHUNKS
+    lines = own[0].shape[0] // 2
+    length = count * sum(cells for _, cells in cuts)
     scalars = pl.BlockSpec(memory_space=pltpu.SMEM)
     whole = pl.BlockSpec(memory_space=pltpu.VMEM)
     return pl.pallas_call(
-        functools.partial(gradient_kernel, count),
+        functools.partial(gradient_kernel, count, cuts),
         out_shape=(
             jax.ShapeDtypeStruct((2, length // LANES * lines, LANES), F32),
             jax.ShapeDtypeStruct((2, length // LANES, LANES), F32),
         ),
-        in_specs=[scalars] * 4 + [whole] * (3 + 2 * CHUNKS),
+        in_specs=[scalars] * 4 + [whole] * (4 + 2 * len(cuts)),
         out_specs=(whole, whole),
         compiler_params=pltpu.CompilerParams(vmem_limit_bytes=40 * 2**20),
         cost_estimate=pl.CostEstimate(flops=2400 * lines * length, bytes_accessed=16 * lines * length, transcendentals=0),
         name="gradient",
-    )(tiles, centers, halves, turn, *tables, *own, *far)
+    )(tiles, centers, halves, turn, down, *tables, *own, *far)
 
 
 def spectrum_kernel(lines, over_rows_ref, over_lanes_ref, twist_ref, grid_ref, bins_ref):
@@ -280,7 +332,7 @@
 
 
 def focus_kernel(
-    over_rows_ref, over_lanes_ref, twist_ref, below_ref, across_ref, sums_ref, bins_ref, out_ref, phase_ref, grid_ref
+    over_rows_ref, over_lanes_ref, twist_ref, below_ref, across_ref, sums_ref, bins_ref, out_ref, phase_ref, grid_ref, turned_ref
 ):
     rows = twist_ref.shape[1]
     lines = out_ref.shape[1]
@@ -294,7 +346,11 @@
         jnp.int32, (rows, LANES), 1
     )
     phase = prefix - place.astype(F32) * (outer[7:8, LANES:] * (1.0 / length))
-    phase_ref[...] = phase
+    turned_ref[...] = jnp.transpose(phase)
+    runs = LANES // rows
+    phase_ref[...] = jnp.concatenate(
+        [turned_ref[pl.ds(at, rows, stride=runs), :] for at in range(runs)], axis=1
+    )
     cos, sin = jnp.cos(phase), jnp.sin(phase)
     for pair in range(0, lines, 2):
         fixed = []
@@ -339,7 +395,7 @@
         ),
         in_specs=[whole] * 7,
         out_specs=(whole, whole),
-        scratch_shapes=[pltpu.VMEM((2, rows * lines, LANES), F32)],
+        scratch_shapes=[pltpu.VMEM((2, rows * lines, LANES), F32), pltpu.VMEM((LANES, rows), F32)],
         compiler_params=pltpu.CompilerParams(vmem_limit_bytes=40 * 2**20),
         cost_estimate=pl.CostEstimate(
             flops=2400 * lines * rows * LANES, bytes_accessed=16 * lines * rows * LANES, transcendentals=0
@@ -353,12 +409,20 @@
     return lax.ppermute(value, axis, [(at, at ^ bit) for at in range(count)])
 
 
-def total_over(value, axis):
-    count = lax.axis_size(axis)
-    bit = 1
-    while bit < count:
-        value = value + swap(value, axis, bit)
-        bit *= 2
+def total_over(value, pairs):
+    for at in range(0, len(pairs), 2):
+        (axis, bit), *more = sorted(pairs[at : at + 2])
+        first = swap(value, axis, bit)
+        for other, other_bit in more:
+            second = swap(value, other, other_bit)
+            if other == axis:
+                third = swap(value, axis, bit ^ other_bit)
+            else:
+                count, inner = lax.axis_size(axis), lax.axis_size(other)
+                both = [(i, ((i // inner) ^ bit) * inner + ((i % inner) ^ other_bit)) for i in range(count * inner)]
+                third = lax.ppermute(value, (axis, other), both)
+            value, first = value + first, second + third
+        value = value + first
     return value
 
 
@@ -370,20 +434,10 @@
     return jnp.concatenate([jnp.where(first, value, other), jnp.where(first, other, value)], axis=2)
 
 
-def largest(value):
-    return jnp.max(jnp.abs(value)).astype(F32)
-
-
-def common_scale(echo, taps, steer):
-    local = jnp.stack([largest(echo), largest(taps), largest(steer)])
-    local = jnp.broadcast_to(local[:, None, None], (3, 8, LANES))
-    for axis in ("ping", "rng"):
-        local = functools.reduce(jnp.maximum, [local] + [swap(local, axis, at) for at in range(1, lax.axis_size(axis))])
-    most = local[:, 0, 0]
-    terms = 2 * NTAP * steer.shape[2] * lax.axis_size("ping")
-    bound = jnp.clip(terms * most[0] * most[1] * most[2], 1e-30, 1e30)
+def scale_of(known, terms):
+    bound = jnp.clip(terms * known[0] * known[1] * known[2], 1e-30, 1e30)
     power = jnp.clip(jnp.floor(jnp.log2(2.0**15 / bound)), -100.0, 100.0)
-    return jnp.exp2(power), jnp.exp2(-power)
+    return lax.optimization_barrier((jnp.exp2(power), jnp.exp2(-power)))
 
 
 def start_rows(pings, tiles, lines):
@@ -398,17 +452,16 @@
     return (slot * tiles + (owner % tiles - tile) % tiles) * (2 * lines)
 
 
-def scatter_sum(mine, theirs, scale):
-    up, down = scale
-    count = lax.axis_size("ping")
-    value = mine + swap(theirs, "ping", 1)
-    bit = 2
-    while bit < count:
-        half = value.shape[0] // 2
-        got = swap((value[half:] * up).astype(SENT), "ping", bit)
-        value = value[:half] + got.astype(F32) * down
-        bit *= 2
-    return value
+def tie(value, *others):
+    return lax.optimization_barrier((value, *others))[0]
+
+
+def packed(value):
+    return value[value.shape[0] // 2 :].astype(SENT)
+
+
+def merged(value, got):
+    return value[: value.shape[0] // 2] + got.astype(F32)
 
 
 def on_device(echo, steer, offsets, taps, centers, halves):
@@ -417,32 +470,70 @@
     tile = lax.axis_index("rng")
     lines = centers.shape[0]
     length = steer.shape[1] * tiles
+    cuts = cuts_of(steer.shape[1])
 
     echo_lines = gather_lines(echo, "rng")
-    scale = common_scale(echo, taps, steer)
+    taps = taps.T
+    known = largest(echo, taps, steer)
+    known = jnp.maximum(known, swap(known, "ping", 1))
+    bits = [1 << at for at in range(1, pings.bit_length() - 1)]
+    steps = [("ping", bit) for bit in bits] + [("rng", 1 << at) for at in range(tiles.bit_length() - 1)]
+    echo_lines = tie(echo_lines, known)
+    got = swap(known, *steps[0])
     left = interpolate(start_rows(pings, tiles, lines), offsets, taps, echo_lines)
+    known = jnp.maximum(known, tie(got, left))
+
+    count = len(cuts)
+    totals, moving = [None] * count, [None] * count
+
+    def advance(at, stage, gate):
+        got = moving[at] if gate is None else tie(moving[at], gate)
+        totals[at] = (totals[at] + got) * up[0, 0] if stage == 0 else merged(totals[at], got)
+        if stage == len(bits):
+            return totals[at]
+        send = packed(totals[at])
+        moving[at] = swap(send, "ping", bits[stage])
+        return send
+
+    gate = known
+    for at in range(count + 1):
+        if at < count:
+            left = tie(left, gate)
+            totals[at], theirs = partial_image(left, steer, *cuts[at])
+            moving[at] = swap(theirs, "ping", 1)
+            gate = theirs
+        for step in steps[1:] if at == 1 else steps[1:2] if at == 0 else []:
+            if at == 0 or step != steps[1]:
+                known = jnp.maximum(known, tie(swap(known, *step), gate))
+                gate = known
+        if at == 1:
+            up, down = scale_of(known, 2.0 * NTAP * steer.shape[2] * pings)
+        for stage in range(min(at, 2)):
+            gate = advance(at - 1 - stage, stage, gate)
+    waiting = [(count - 1, 1)] + [(at, stage) for at in range(count) for stage in range(2, len(bits) + 1)]
+    for at, stage in sorted(waiting, key=lambda item: (item[0] + 2 * item[1], item[1])):
+        advance(at, stage, gate if stage == 1 else None)
     own, far = [], []
-    for chunk in range(CHUNKS):
-        total = scatter_sum(*partial_image(left, steer, chunk), scale)
+    for total in totals:
         own.append(total[: 2 * lines])
         pieces = []
         for step in range(1, tiles):
-            send = (total[2 * lines * step : 2 * lines * (step + 1)] * scale[0]).astype(SENT)
-            got = lax.ppermute(send, "rng", [(at, (at + step) % tiles) for at in range(tiles)])
-            pieces.append(got.astype(F32) * scale[1])
+            send = total[2 * lines * step : 2 * lines * (step + 1)]
+            pieces.append(lax.ppermute(send, "rng", [(at, (at + step) % tiles) for at in range(tiles)]))
         far.append(jnp.stack(pieces))
 
     angle = 2.0 * math.pi / length * centers.astype(F32)
     turn = jnp.stack([jnp.cos(angle), jnp.sin(angle)])
     owners = (tile - jnp.arange(tiles, dtype=jnp.int32)) % tiles
     tables = [jnp.asarray(table) for table in dft_tables(length, -1.0)]
-    grid, sums = gradient(owners, centers, halves, turn, tables, own, far)
-    sums = total_over(total_over(sums, "ping"), "rng")
+    grid, sums = gradient(owners, cuts, centers, halves, turn, down, tables, own, far)
+    pairs = [("ping", 1)] + [("rng", 1 << at) for at in range(tiles.bit_length() - 1)] + [("ping", bit) for bit in bits]
+    sums = total_over(sums, pairs)
     bins = spectrum(tables, grid, lines)
     tables = [jnp.asarray(table) for table in dft_tables(length, 1.0)]
     prefix_tables = [jnp.asarray(table) for table in sum_tables(length)]
     focused, phase = focus(tables, prefix_tables, sums, bins, lines)
-    return (focused, phase.T.reshape(-1))
+    return (focused, phase.reshape(-1))
 
 
 def solution(mesh):

time: 136 us -> 113 us (0.83)
  waiting for transfers between devices: 48.1 us -> 40.5 us
  other arithmetic: 11.7 us -> 4.25 us
  between operations: 4.52 us -> 1.08 us
  local copies, waits for them, and re-layouts: 3.71 us -> 1.22 us
  starting transfers between devices: 31.4 us -> 30 us
    ppermute x25 -> x19, waiting for transfers between devices: 45.2 us -> 34.3 us  [swap(): return lax.ppermute(value, axis, [(at, at ^ bit) for at in range(count)])]
    reduce_max x2 -> x0, other arithmetic: 8.34 us -> none  [largest(): return jnp.max(jnp.abs(value)).astype(F32)]
    mul x0 -> x3, other arithmetic: none -> 2.57 us  [advance(): (totals[at] + got) * up[0, 0]]
    ppermute x0 -> x1, waiting for transfers between devices: none -> 1.92 us  [total_over(): third = lax.ppermute(value, (axis, other), both)]
    pallas_call x1, Pallas kernels: 5.43 us -> 3.85 us  [interpolate(): pl.pallas_call(interp_kernel, grid=(pings // LANES,), out_shape=jax.Shape...]
    unnamed x37 -> x26, local copies, waits for them, and re-layouts: 2.19 us -> 0.62 us
    ppermute x4 -> x3, starting transfers between devices: 5.15 us -> 3.58 us  [on_device(): lax.ppermute(send, 'rng', [(at, (at + step) % tiles) for at in range(tile...]
    pallas_call x5, Pallas kernels: 25.1 us -> 26.6 us  [the longest x3 16.1 us: partial_image(): pl.pallas_call(image_kernel, grid=(cells // tile,), out_shape=(jax.ShapeD...]
  transfers between devices with their start and end apart: 29 -> 23, of which waited for: 15 -> 16; matrix products, arithmetic and copies ran while one was open for 9% -> 4% of each run, Pallas kernels for 22% -> 21%
where the time goes in v2:
time: 113 us
  waiting for transfers between devices  40.5 us (36%)
  Pallas kernels  36.1 us (32%)
  starting transfers between devices  30 us (27%)
  other arithmetic  4.25 us (4%)
  local copies, waits for them, and re-layouts  1.22 us (1%)
    ppermute x19, waiting for transfers between devices, swap(): return lax.ppermute(value, axis, [(at, at ^ bit) for at in range(count)])  34.3 us
    ppermute x19, starting transfers between devices, swap(): return lax.ppermute(value, axis, [(at, at ^ bit) for at in range(count)])  26.3 us
    pallas_call x3, Pallas kernels, partial_image(): pl.pallas_call(image_kernel, grid=(cells // tile,), out_shape=(jax.ShapeD...  16.1 us
    pallas_call x1, Pallas kernels, largest(): pl.pallas_call(largest_kernel, out_shape=jax.ShapeDtypeStruct((3, 8, LANE...  7.9 us
    ppermute x3, waiting for transfers between devices, on_device(): lax.ppermute(send, 'rng', [(at, (at + step) % tiles) for at in range(tile...  4.36 us
    pallas_call x1, Pallas kernels, focus(): pl.pallas_call(focus_kernel, out_shape=(jax.ShapeDtypeStruct((2, lines, r...  4.09 us
    pallas_call x1, Pallas kernels, interpolate(): pl.pallas_call(interp_kernel, grid=(pings // LANES,), out_shape=jax.Shape...  3.85 us
    ppermute x3, starting transfers between devices, on_device(): lax.ppermute(send, 'rng', [(at, (at + step) % tiles) for at in range(tile...  3.58 us
  transfers between devices with their start and end apart: 23, of which 16 were waited for; matrix products, arithmetic and copies ran while one was open for 4% of the time, Pallas kernels for 21%

profile of v2, /device:TPU:0, one launch (start us, length us, event | category | flops | bytes accessed | tf_op | source)
XLA Modules:
  0.0 113.2 jit_solution(953130985337859632)
XLA Ops:
  0.6 3.0 %collective-permute-start.2 = (bf16[2,1024,128]{2,1,0:T(8,128)(2,1)}, bf16[2,1024,128]{2,1,0:T(8,128)(2,1)S(1)}, u32[]{:S(2)}, u32[]{:S(2)}) collective-permute-start(bf16[2,1024,128]{2,1,0:T(8,128)(2,1)} %echo_ref.1), channel_id=1, source_target_pairs={{0,1},{1,0},{2,3},{3,2},{4,5},{5,4},{6,7},{7,6},{8,9},{9,8},{10,11... | collective-permute-start | bytes 1572872 | tf_op jit(solution)/shard_map/ppermute | solution.py:409
  3.6 7.9 %largest.1 = f32[3,8,128]{2,1,0:T(8,128)} custom-call(bf16[2,1024,128]{2,1,0:T(8,128)(2,1)} %echo_ref.1, f32[4,16]{1,0:T(4,128)} %bitcast.17, bf16[2,4096,1024]{2,1,0:T(8,128)(2,1)} %steer_ref.7), custom_call_target="tpu_custom_call" | custom-call | flops 8388608 | bytes 16777216 | tf_op jit(solution)/shard_map/largest/pallas_call | solution.py:153
  11.5 0.1 collective-permute-start
  11.7 1.3 %collective-permute-done = f32[3,8,128]{2,1,0:T(8,128)S(1)} collective-permute-done((f32[3,8,128]{2,1,0:T(8,128)}, f32[3,8,128]{2,1,0:T(8,128)S(1)}, u32[]{:S(2)}, u32[]{:S(2)}) %collective-permute-start) | collective-permute-done | bytes 12320 | tf_op jit(solution)/shard_map/ppermute | solution.py:409
  13.0 0.7 max.24
  13.7 1.6 %collective-permute-start.1 = (f32[3,8,128]{2,1,0:T(8,128)S(1)}, f32[3,8,128]{2,1,0:T(8,128)S(1)}, u32[]{:S(2)}, u32[]{:S(2)}) collective-permute-start(f32[3,8,128]{2,1,0:T(8,128)S(1)} %max.24), channel_id=1, source_target_pairs={{0,4},{2,6},{4,0},{6,2},{8,12},{10,14},{12,8},{14,10},{1,5},{3,7},... | collective-permute-start | bytes 36872 | tf_op jit(solution)/shard_map/ppermute | solution.py:409
  15.3 0.5 collective-permute-done.2
  15.8 0.1 broadcast_select_fusion.1
  15.9 0.1 pad_maximum_fusion.echo_ref
  16.0 0.5 copy-done.8
  16.5 3.9 %interp.1.left_ref = bf16[2,512,1024]{2,1,0:T(8,128)(2,1)S(1)} custom-call(s32[16]{0:T(128)S(1)} %fusion.11.starts_ref, s32[16]{0:T(128)S(1)} %copy-done.9, f32[4,16]{1,0:T(4,128)S(1)} %bitcast.18, bf16[2,1024,256]{2,1,0:T(8,128)(2,1)S(1)} %pad_maximum_fusion.echo_ref), custom_call_target="tpu_custom_call" | custom-call | flops 4194304 | bytes 3145728 | tf_op jit(solution)/shard_map/interp/pallas_call | solution.py:114
  20.4 5.9 %image.3 = (f32[256,1536]{1,0:T(8,128)S(1)}, f32[256,1536]{1,0:T(8,128)S(1)}) custom-call(bf16[2,512,1024]{2,1,0:T(8,128)(2,1)S(1)} %interp.1.left_ref, bf16[2,4096,1024]{2,1,0:T(8,128)(2,1)} %steer_ref.7), custom_call_target="tpu_custom_call" | custom-call | flops 1536 | bytes 1536 | tf_op jit(solution)/shard_map/image/pallas_call | solution.py:181
  26.3 0.1 collective-permute-start.5
  26.4 2.9 %collective-permute-start.3 = (f32[3,8,128]{2,1,0:T(8,128)S(1)}, f32[3,8,128]{2,1,0:T(8,128)S(1)}, u32[]{:S(2)}, u32[]{:S(2)}) collective-permute-start(f32[3,8,128]{2,1,0:T(8,128)S(1)} %max.25), channel_id=1, source_target_pairs={{0,8},{2,10},{4,12},{6,14},{8,0},{10,2},{12,4},{14,6},{1,9},{3,11}... | collective-permute-start | bytes 36872 | tf_op jit(solution)/shard_map/ppermute | solution.py:409
  29.3 1.8 %collective-permute-done.3 = f32[3,8,128]{2,1,0:T(8,128)S(1)} collective-permute-done((f32[3,8,128]{2,1,0:T(8,128)S(1)}, f32[3,8,128]{2,1,0:T(8,128)S(1)}, u32[]{:S(2)}, u32[]{:S(2)}) %collective-permute-start.3) | collective-permute-done | bytes 12320 | tf_op jit(solution)/shard_map/ppermute | solution.py:409
  31.1 5.9 %image.4 = (f32[256,1536]{1,0:T(8,128)S(1)}, f32[256,1536]{1,0:T(8,128)S(1)}) custom-call(bf16[2,512,1024]{2,1,0:T(8,128)(2,1)S(1)} %interp.1.left_ref, bf16[2,4096,1024]{2,1,0:T(8,128)(2,1)} %steer_ref.7), custom_call_target="tpu_custom_call" | custom-call | flops 1536 | bytes 1536 | tf_op jit(solution)/shard_map/image/pallas_call | solution.py:181
  37.0 0.1 collective-permute-start.7
  37.1 1.8 %collective-permute-start.4 = (f32[3,8,128]{2,1,0:T(8,128)S(1)}, f32[3,8,128]{2,1,0:T(8,128)S(1)}, u32[]{:S(2)}, u32[]{:S(2)}) collective-permute-start(f32[3,8,128]{2,1,0:T(8,128)S(1)} %max.26), channel_id=1, source_target_pairs={{0,1},{1,0},{2,3},{3,2},{4,5},{5,4},{6,7},{7,6},{8,9},{9,8},{10,11... | collective-permute-start | bytes 36872 | tf_op jit(solution)/shard_map/ppermute | solution.py:409
  38.9 2.0 %collective-permute-done.4 = f32[3,8,128]{2,1,0:T(8,128)S(1)} collective-permute-done((f32[3,8,128]{2,1,0:T(8,128)S(1)}, f32[3,8,128]{2,1,0:T(8,128)S(1)}, u32[]{:S(2)}, u32[]{:S(2)}) %collective-permute-start.4) | collective-permute-done | bytes 12320 | tf_op jit(solution)/shard_map/ppermute | solution.py:409
  40.9 0.5 slice.77
  41.4 0.9 add_multiply_fusion.1
  42.3 1.9 %collective-permute-start.6 = (f16[128,1536]{1,0:T(8,128)(2,1)S(1)}, f16[128,1536]{1,0:T(8,128)(2,1)S(1)}, u32[]{:S(2)}, u32[]{:S(2)}) collective-permute-start(f16[128,1536]{1,0:T(8,128)(2,1)S(1)} %slice_convert_fusion.1), channel_id=1, source_target_pairs={{0,4},{2,6},{4,0},{6,2},{8,12},{10,14},{12,8},{14,10},{1,5},{3,7},... | collective-permute-start | bytes 1179656 | tf_op jit(solution)/shard_map/ppermute | solution.py:409
  44.2 4.3 %image.5 = (f32[256,1024]{1,0:T(8,128)S(1)}, f32[256,1024]{1,0:T(8,128)S(1)}) custom-call(bf16[2,512,1024]{2,1,0:T(8,128)(2,1)S(1)} %interp.1.left_ref, bf16[2,4096,1024]{2,1,0:T(8,128)(2,1)} %steer_ref.7), custom_call_target="tpu_custom_call" | custom-call | flops 1024 | bytes 1024 | tf_op jit(solution)/shard_map/image/pallas_call | solution.py:181
  48.6 0.1 collective-permute-start.10
  48.7 0.9 add_multiply_fusion
  49.6 3.2 %collective-permute-done.6 = f16[128,1536]{1,0:T(8,128)(2,1)S(1)} collective-permute-done((f16[128,1536]{1,0:T(8,128)(2,1)S(1)}, f16[128,1536]{1,0:T(8,128)(2,1)S(1)}, u32[]{:S(2)}, u32[]{:S(2)}) %collective-permute-start.6) | collective-permute-done | bytes 393248 | tf_op jit(solution)/shard_map/ppermute | solution.py:409
  52.8 0.1 slice_add_fusion.1
  53.0 2.8 %collective-permute-start.8 = (f16[64,1536]{1,0:T(8,128)(2,1)S(1)}, f16[64,1536]{1,0:T(8,128)(2,1)S(1)}, u32[]{:S(2)}, u32[]{:S(2)}) collective-permute-start(f16[64,1536]{1,0:T(8,128)(2,1)S(1)} %slice_convert_fusion.4), channel_id=1, source_target_pairs={{0,8},{2,10},{4,12},{6,14},{8,0},{10,2},{12,4},{14,6},{1,9},{3,11}... | collective-permute-start | bytes 589832 | tf_op jit(solution)/shard_map/ppermute | solution.py:409
  55.8 1.7 %collective-permute-start.9 = (f16[128,1536]{1,0:T(8,128)(2,1)S(1)}, f16[128,1536]{1,0:T(8,128)(2,1)S(1)}, u32[]{:S(2)}, u32[]{:S(2)}) collective-permute-start(f16[128,1536]{1,0:T(8,128)(2,1)S(1)} %slice_convert_fusion), channel_id=1, source_target_pairs={{0,4},{2,6},{4,0},{6,2},{8,12},{10,14},{12,8},{14,10},{1,5},{3,7},... | collective-permute-start | bytes 1179656 | tf_op jit(solution)/shard_map/ppermute | solution.py:409
  57.5 6.0 %collective-permute-done.8 = f16[64,1536]{1,0:T(8,128)(2,1)S(1)} collective-permute-done((f16[64,1536]{1,0:T(8,128)(2,1)S(1)}, f16[64,1536]{1,0:T(8,128)(2,1)S(1)}, u32[]{:S(2)}, u32[]{:S(2)}) %collective-permute-start.8) | collective-permute-done | bytes 196640 | tf_op jit(solution)/shard_map/ppermute | solution.py:409
  63.6 0.8 add_multiply_fusion.2
  64.4 3.6 %collective-permute-done.9 = f16[128,1536]{1,0:T(8,128)(2,1)S(1)} collective-permute-done((f16[128,1536]{1,0:T(8,128)(2,1)S(1)}, f16[128,1536]{1,0:T(8,128)(2,1)S(1)}, u32[]{:S(2)}, u32[]{:S(2)}) %collective-permute-start.9) | collective-permute-done | bytes 393248 | tf_op jit(solution)/shard_map/ppermute | solution.py:409
  68.1 0.1 slice_add_fusion
  68.2 1.3 %collective-permute-start.11 = (f16[64,1536]{1,0:T(8,128)(2,1)S(1)}, f16[64,1536]{1,0:T(8,128)(2,1)S(1)}, u32[]{:S(2)}, u32[]{:S(2)}) collective-permute-start(f16[64,1536]{1,0:T(8,128)(2,1)S(1)} %slice_convert_fusion.3), channel_id=1, source_target_pairs={{0,8},{2,10},{4,12},{6,14},{8,0},{10,2},{12,4},{14,6},{1,9},{3,11}... | collective-permute-start | bytes 589832 | tf_op jit(solution)/shard_map/ppermute | solution.py:409
  69.6 1.6 %collective-permute-start.14 = (f32[32,1536]{1,0:T(8,128)S(1)}, f32[32,1536]{1,0:T(8,128)S(1)}, u32[]{:S(2)}, u32[]{:S(2)}) collective-permute-start(f32[32,1536]{1,0:T(8,128)S(1)} %get-tuple-element.58), channel_id=1, source_target_pairs={{0,1},{1,0},{2,3},{3,2},{4,5},{5,4},{6,7},{7,6},{8,9},{9,8},{10,11... | collective-permute-start | bytes 589832 | tf_op jit(solution)/shard_map/ppermute | solution.py:522
  71.1 1.8 %collective-permute-start.12 = (f16[128,1024]{1,0:T(8,128)(2,1)S(1)}, f16[128,1024]{1,0:T(8,128)(2,1)S(1)}, u32[]{:S(2)}, u32[]{:S(2)}) collective-permute-start(f16[128,1024]{1,0:T(8,128)(2,1)S(1)} %slice_convert_fusion.2), channel_id=1, source_target_pairs={{0,4},{2,6},{4,0},{6,2},{8,12},{10,14},{12,8},{14,10},{1,5},{3,7},... | collective-permute-start | bytes 786440 | tf_op jit(solution)/shard_map/ppermute | solution.py:409
  73.0 5.4 %collective-permute-done.11 = f16[64,1536]{1,0:T(8,128)(2,1)S(1)} collective-permute-done((f16[64,1536]{1,0:T(8,128)(2,1)S(1)}, f16[64,1536]{1,0:T(8,128)(2,1)S(1)}, u32[]{:S(2)}, u32[]{:S(2)}) %collective-permute-start.11) | collective-permute-done | bytes 196640 | tf_op jit(solution)/shard_map/ppermute | solution.py:409
  78.4 0.0 copy-start
  78.4 0.0 copy-start.2
  78.4 0.0 copy-start.3
  78.4 1.6 %collective-permute-done.12 = f16[128,1024]{1,0:T(8,128)(2,1)S(1)} collective-permute-done((f16[128,1024]{1,0:T(8,128)(2,1)S(1)}, f16[128,1024]{1,0:T(8,128)(2,1)S(1)}, u32[]{:S(2)}, u32[]{:S(2)}) %collective-permute-start.12) | collective-permute-done | bytes 262176 | tf_op jit(solution)/shard_map/ppermute | solution.py:409
  80.1 0.1 slice_add_fusion.2
  80.2 0.9 collective-permute-start.13
  81.2 1.4 %collective-permute-start.15 = (f32[32,1536]{1,0:T(8,128)S(1)}, f32[32,1536]{1,0:T(8,128)S(1)}, u32[]{:S(2)}, u32[]{:S(2)}) collective-permute-start(f32[32,1536]{1,0:T(8,128)S(1)} %get-tuple-element.56), channel_id=1, source_target_pairs={{0,1},{1,0},{2,3},{3,2},{4,5},{5,4},{6,7},{7,6},{8,9},{9,8},{10,11... | collective-permute-start | bytes 589832 | tf_op jit(solution)/shard_map/ppermute | solution.py:522
  82.5 4.9 %collective-permute-done.13 = f16[64,1024]{1,0:T(8,128)(2,1)S(1)} collective-permute-done((f16[64,1024]{1,0:T(8,128)(2,1)S(1)}, f16[64,1024]{1,0:T(8,128)(2,1)S(1)}, u32[]{:S(2)}, u32[]{:S(2)}) %collective-permute-start.13) | collective-permute-done | bytes 131104 | tf_op jit(solution)/shard_map/ppermute | solution.py:409
  87.5 0.6 collective-permute-start.16
  88.1 0.2 collective-permute-done.15
  88.3 4.2 %collective-permute-done.16 = f32[32,1024]{1,0:T(8,128)S(1)} collective-permute-done((f32[32,1024]{1,0:T(8,128)S(1)}, f32[32,1024]{1,0:T(8,128)S(1)}, u32[]{:S(2)}, u32[]{:S(2)}) %collective-permute-start.16) | collective-permute-done | bytes 131104 | tf_op jit(solution)/shard_map/ppermute | solution.py:522
  92.5 2.6 %gradient.1 = (f32[2,1024,128]{2,1,0:T(8,128)S(1)}, f32[2,64,128]{2,1,0:T(8,128)S(1)}) custom-call(s32[2]{0:T(128)S(1)} %and_select_fusion.5.tile_ref, s32[16]{0:T(128)S(1)} %copy-done.10, s32[16]{0:T(128)S(1)} %copy-done.11, f32[2,16]{1,0:T(2,128)S(1)} %pad_maximum_fusion.1.turn_ref, f32[8,128]{1,0:T(8,128)S(1)} %get-tuple-element.35.down_ref, ...), custom_call_target="tpu_custom_call" | custom-call | flops 314572800 | bytes 2097152 | tf_op jit(solution)/shard_map/gradient/pallas_call | solution.py:286
  95.1 0.1 collective-permute-start.19
  95.2 0.6 collective-permute-start.18
  95.8 1.2 %collective-permute-start.17 = (f32[2,64,128]{2,1,0:T(8,128)S(1)}, f32[2,64,128]{2,1,0:T(8,128)S(1)}, u32[]{:S(2)}, u32[]{:S(2)}) collective-permute-start(f32[2,64,128]{2,1,0:T(8,128)S(1)} %get-tuple-element.48), channel_id=1, source_target_pairs={{0,2},{2,0},{4,6},{6,4},{8,10},{10,8},{12,14},{14,12},{1,3},{3,1},... | collective-permute-start | bytes 196616 | tf_op jit(solution)/shard_map/ppermute | solution.py:409
  97.0 1.9 %collective-permute-done.19 = f32[2,64,128]{2,1,0:T(8,128)S(1)} collective-permute-done((f32[2,64,128]{2,1,0:T(8,128)S(1)}, f32[2,64,128]{2,1,0:T(8,128)S(1)}, u32[]{:S(2)}, u32[]{:S(2)}) %collective-permute-start.19) | collective-permute-done | bytes 65568 | tf_op jit(solution)/shard_map/ppermute | solution.py:423
  98.9 1.2 %collective-permute-done.18 = f32[2,64,128]{2,1,0:T(8,128)S(1)} collective-permute-done((f32[2,64,128]{2,1,0:T(8,128)S(1)}, f32[2,64,128]{2,1,0:T(8,128)S(1)}, u32[]{:S(2)}, u32[]{:S(2)}) %collective-permute-start.18) | collective-permute-done | bytes 65568 | tf_op jit(solution)/shard_map/ppermute | solution.py:409
  100.2 0.0 copy-start.4
  100.2 0.0 copy-start.5
  100.2 0.0 copy-start.6
  100.2 0.0 copy-start.7
  100.2 2.3 %collective-permute-start.22 = (f32[2,64,128]{2,1,0:T(8,128)S(1)}, f32[2,64,128]{2,1,0:T(8,128)S(1)}, u32[]{:S(2)}, u32[]{:S(2)}) collective-permute-start(f32[2,64,128]{2,1,0:T(8,128)S(1)} %add_add_fusion.1), channel_id=1, source_target_pairs={{0,12},{2,14},{4,8},{6,10},{8,4},{10,6},{12,0},{14,2},{1,13},{3,15... | collective-permute-start | bytes 196616 | tf_op jit(solution)/shard_map/ppermute | solution.py:409
  102.5 2.1 %collective-permute-start.20 = (f32[2,64,128]{2,1,0:T(8,128)S(1)}, f32[2,64,128]{2,1,0:T(8,128)S(1)}, u32[]{:S(2)}, u32[]{:S(2)}) collective-permute-start(f32[2,64,128]{2,1,0:T(8,128)S(1)} %add_add_fusion.1), channel_id=1, source_target_pairs={{0,4},{2,6},{4,0},{6,2},{8,12},{10,14},{12,8},{14,10},{1,5},{3,7},... | collective-permute-start | bytes 196616 | tf_op jit(solution)/shard_map/ppermute | solution.py:409
  104.7 1.6 %spectrum.1.bins_ref = f32[1024,256]{1,0:T(8,128)S(1)} custom-call(bf16[128,384]{1,0:T(8,128)(2,1)S(1)} %copy-done.2, bf16[768,256]{1,0:T(8,128)(2,1)S(1)} %copy-done, f32[2,64,128]{2,1,0:T(8,128)S(1)} %copy-done.3, f32[2,1024,128]{2,1,0:T(8,128)S(1)} %get-tuple-element.49.grid_ref), custom_call_target="tpu_custom_call" | custom-call | flops 314572800 | bytes 2097152 | tf_op jit(solution)/shard_map/spectrum/pallas_call | solution.py:313
  106.3 0.8 collective-permute-done.22
  107.0 2.0 %collective-permute-done.21 = f32[2,64,128]{2,1,0:T(8,128)S(1)} collective-permute-done((f32[2,64,128]{2,1,0:T(8,128)S(1)}, f32[2,64,128]{2,1,0:T(8,128)S(1)}, u32[]{:S(2)}, u32[]{:S(2)}) %collective-permute-start.21) | collective-permute-done | bytes 65568 | tf_op jit(solution)/shard_map/ppermute | solution.py:409
  109.1 4.1 %focus.1 = (f32[2,16,8192]{2,1,0:T(8,128)}, f32[64,128]{1,0:T(8,128)}) custom-call(bf16[128,384]{1,0:T(8,128)(2,1)S(1)} %copy-done.5, bf16[768,256]{1,0:T(8,128)(2,1)S(1)} %copy-done.1, f32[2,64,128]{2,1,0:T(8,128)S(1)} %copy-done.6, bf16[64,192]{1,0:T(8,128)(2,1)S(1)} %copy-done.7, bf16[384,256]{1,0:T(8,128)(2,1)S(1)} %copy-done.4, ...), custom_call_target="tpu_custom_call" | custom-call | flops 314572800 | bytes 2097152 | tf_op jit(solution)/shard_map/focus/pallas_call | solution.py:390
  (49 shorter events, 0.6 us)
Async XLA Ops:
  0.6 15.1 %collective-permute-start.2 = (bf16[2,1024,128]{2,1,0:T(8,128)(2,1)}, bf16[2,1024,128]{2,1,0:T(8,128)(2,1)S(1)}, u32[]{:S(2)}, u32[]{:S(2)}) collective-permute-start(bf16[2,1024,128]{2,1,0:T(8,128)(2,1)} %echo_ref.1), channel_id=1, source_target_pairs={{0,1},{1,0},{2,3},{3,2},{4,5},{5,4},{6,7},{7,6},{8,9},{9,8},{10,11... | collective-permute-start | bytes 1572872 | tf_op jit(solution)/shard_map/ppermute | solution.py:409
  3.6 12.1 %copy-start.12 = (bf16[2,1024,128]{2,1,0:T(8,128)(2,1)S(1)}, bf16[2,1024,128]{2,1,0:T(8,128)(2,1)}, u32[]{:S(2)}) copy-start(bf16[2,1024,128]{2,1,0:T(8,128)(2,1)} %echo_ref.1) | copy-start | bytes 1572868
  11.5 1.5 %collective-permute-start = (f32[3,8,128]{2,1,0:T(8,128)}, f32[3,8,128]{2,1,0:T(8,128)S(1)}, u32[]{:S(2)}, u32[]{:S(2)}) collective-permute-start(f32[3,8,128]{2,1,0:T(8,128)} %largest.1), channel_id=1, source_target_pairs={{0,2},{2,0},{4,6},{6,4},{8,10},{10,8},{12,14},{14,12},{1,3},{3,1},... | collective-permute-start | bytes 36872 | tf_op jit(solution)/shard_map/ppermute | solution.py:409
  13.7 6.7 %collective-permute-start.1 = (f32[3,8,128]{2,1,0:T(8,128)S(1)}, f32[3,8,128]{2,1,0:T(8,128)S(1)}, u32[]{:S(2)}, u32[]{:S(2)}) collective-permute-start(f32[3,8,128]{2,1,0:T(8,128)S(1)} %max.24), channel_id=1, source_target_pairs={{0,4},{2,6},{4,0},{6,2},{8,12},{10,14},{12,8},{14,10},{1,5},{3,7},... | collective-permute-start | bytes 36872 | tf_op jit(solution)/shard_map/ppermute | solution.py:409
  15.8 0.7 copy-start.8
  15.9 0.7 copy-start.9
  26.3 15.1 %collective-permute-start.5 = (f32[256,1536]{1,0:T(8,128)S(1)}, f32[256,1536]{1,0:T(8,128)S(1)}, u32[]{:S(2)}, u32[]{:S(2)}) collective-permute-start(f32[256,1536]{1,0:T(8,128)S(1)} %get-tuple-element.30), channel_id=1, source_target_pairs={{0,2},{2,0},{4,6},{6,4},{8,10},{10,8},{12,14},{14,12},{1,3},{3,1},... | collective-permute-start | bytes 4718600 | tf_op jit(solution)/shard_map/ppermute | solution.py:409
  26.4 4.7 %collective-permute-start.3 = (f32[3,8,128]{2,1,0:T(8,128)S(1)}, f32[3,8,128]{2,1,0:T(8,128)S(1)}, u32[]{:S(2)}, u32[]{:S(2)}) collective-permute-start(f32[3,8,128]{2,1,0:T(8,128)S(1)} %max.25), channel_id=1, source_target_pairs={{0,8},{2,10},{4,12},{6,14},{8,0},{10,2},{12,4},{14,6},{1,9},{3,11}... | collective-permute-start | bytes 36872 | tf_op jit(solution)/shard_map/ppermute | solution.py:409
  37.0 11.7 %collective-permute-start.7 = (f32[256,1536]{1,0:T(8,128)S(1)}, f32[256,1536]{1,0:T(8,128)S(1)}, u32[]{:S(2)}, u32[]{:S(2)}) collective-permute-start(f32[256,1536]{1,0:T(8,128)S(1)} %get-tuple-element.33), channel_id=1, source_target_pairs={{0,2},{2,0},{4,6},{6,4},{8,10},{10,8},{12,14},{14,12},{1,3},{3,1},... | collective-permute-start | bytes 4718600 | tf_op jit(solution)/shard_map/ppermute | solution.py:409
  37.1 3.8 %collective-permute-start.4 = (f32[3,8,128]{2,1,0:T(8,128)S(1)}, f32[3,8,128]{2,1,0:T(8,128)S(1)}, u32[]{:S(2)}, u32[]{:S(2)}) collective-permute-start(f32[3,8,128]{2,1,0:T(8,128)S(1)} %max.26), channel_id=1, source_target_pairs={{0,1},{1,0},{2,3},{3,2},{4,5},{5,4},{6,7},{7,6},{8,9},{9,8},{10,11... | collective-permute-start | bytes 36872 | tf_op jit(solution)/shard_map/ppermute | solution.py:409
  42.3 10.5 %collective-permute-start.6 = (f16[128,1536]{1,0:T(8,128)(2,1)S(1)}, f16[128,1536]{1,0:T(8,128)(2,1)S(1)}, u32[]{:S(2)}, u32[]{:S(2)}) collective-permute-start(f16[128,1536]{1,0:T(8,128)(2,1)S(1)} %slice_convert_fusion.1), channel_id=1, source_target_pairs={{0,4},{2,6},{4,0},{6,2},{8,12},{10,14},{12,8},{14,10},{1,5},{3,7},... | collective-permute-start | bytes 1179656 | tf_op jit(solution)/shard_map/ppermute | solution.py:409
  48.6 15.0 %collective-permute-start.10 = (f32[256,1024]{1,0:T(8,128)S(1)}, f32[256,1024]{1,0:T(8,128)S(1)}, u32[]{:S(2)}, u32[]{:S(2)}) collective-permute-start(f32[256,1024]{1,0:T(8,128)S(1)} %get-tuple-element.41), channel_id=1, source_target_pairs={{0,2},{2,0},{4,6},{6,4},{8,10},{10,8},{12,14},{14,12},{1,3},{3,1},... | collective-permute-start | bytes 3145736 | tf_op jit(solution)/shard_map/ppermute | solution.py:409
  49.5 6.2 %copy-start.10 = (s32[16]{0:T(128)S(1)}, s32[16]{0:T(128)}, u32[]{:S(2)}) copy-start(s32[16]{0:T(128)} %centers_ref.1) | copy-start | bytes 196
  53.0 10.5 %collective-permute-start.8 = (f16[64,1536]{1,0:T(8,128)(2,1)S(1)}, f16[64,1536]{1,0:T(8,128)(2,1)S(1)}, u32[]{:S(2)}, u32[]{:S(2)}) collective-permute-start(f16[64,1536]{1,0:T(8,128)(2,1)S(1)} %slice_convert_fusion.4), channel_id=1, source_target_pairs={{0,8},{2,10},{4,12},{6,14},{8,0},{10,2},{12,4},{14,6},{1,9},{3,11}... | collective-permute-start | bytes 589832 | tf_op jit(solution)/shard_map/ppermute | solution.py:409
  55.8 12.2 %collective-permute-start.9 = (f16[128,1536]{1,0:T(8,128)(2,1)S(1)}, f16[128,1536]{1,0:T(8,128)(2,1)S(1)}, u32[]{:S(2)}, u32[]{:S(2)}) collective-permute-start(f16[128,1536]{1,0:T(8,128)(2,1)S(1)} %slice_convert_fusion), channel_id=1, source_target_pairs={{0,4},{2,6},{4,0},{6,2},{8,12},{10,14},{12,8},{14,10},{1,5},{3,7},... | collective-permute-start | bytes 1179656 | tf_op jit(solution)/shard_map/ppermute | solution.py:409
  68.2 10.1 %collective-permute-start.11 = (f16[64,1536]{1,0:T(8,128)(2,1)S(1)}, f16[64,1536]{1,0:T(8,128)(2,1)S(1)}, u32[]{:S(2)}, u32[]{:S(2)}) collective-permute-start(f16[64,1536]{1,0:T(8,128)(2,1)S(1)} %slice_convert_fusion.3), channel_id=1, source_target_pairs={{0,8},{2,10},{4,12},{6,14},{8,0},{10,2},{12,4},{14,6},{1,9},{3,11}... | collective-permute-start | bytes 589832 | tf_op jit(solution)/shard_map/ppermute | solution.py:409
  69.6 18.5 %collective-permute-start.14 = (f32[32,1536]{1,0:T(8,128)S(1)}, f32[32,1536]{1,0:T(8,128)S(1)}, u32[]{:S(2)}, u32[]{:S(2)}) collective-permute-start(f32[32,1536]{1,0:T(8,128)S(1)} %get-tuple-element.58), channel_id=1, source_target_pairs={{0,1},{1,0},{2,3},{3,2},{4,5},{5,4},{6,7},{7,6},{8,9},{9,8},{10,11... | collective-permute-start | bytes 589832 | tf_op jit(solution)/shard_map/ppermute | solution.py:522
  71.1 8.9 %collective-permute-start.12 = (f16[128,1024]{1,0:T(8,128)(2,1)S(1)}, f16[128,1024]{1,0:T(8,128)(2,1)S(1)}, u32[]{:S(2)}, u32[]{:S(2)}) collective-permute-start(f16[128,1024]{1,0:T(8,128)(2,1)S(1)} %slice_convert_fusion.2), channel_id=1, source_target_pairs={{0,4},{2,6},{4,0},{6,2},{8,12},{10,14},{12,8},{14,10},{1,5},{3,7},... | collective-permute-start | bytes 786440 | tf_op jit(solution)/shard_map/ppermute | solution.py:409
  78.4 14.1 %copy-start = (bf16[768,256]{1,0:T(8,128)(2,1)S(1)}, bf16[768,256]{1,0:T(8,128)(2,1)}, u32[]{:S(2)}) copy-start(bf16[768,256]{1,0:T(8,128)(2,1)} %constant.118.clone.over_lanes_ref) | copy-start | bytes 1179652
  78.4 14.1 %copy-start.2 = (bf16[128,384]{1,0:T(8,128)(2,1)S(1)}, bf16[128,384]{1,0:T(8,128)(2,1)}, u32[]{:S(2)}) copy-start(bf16[128,384]{1,0:T(8,128)(2,1)} %constant.117.clone.over_rows_ref) | copy-start | bytes 294916
  78.4 14.1 %copy-start.3 = (f32[2,64,128]{2,1,0:T(8,128)S(1)}, f32[2,64,128]{2,1,0:T(8,128)}, u32[]{:S(2)}) copy-start(f32[2,64,128]{2,1,0:T(8,128)} %constant.119.clone.twist_ref) | copy-start | bytes 196612
  78.4 14.1 %copy-start.11 = (s32[16]{0:T(128)S(1)}, s32[16]{0:T(128)}, u32[]{:S(2)}) copy-start(s32[16]{0:T(128)} %halves_ref.1) | copy-start | bytes 196
  80.2 7.2 %collective-permute-start.13 = (f16[64,1024]{1,0:T(8,128)(2,1)S(1)}, f16[64,1024]{1,0:T(8,128)(2,1)S(1)}, u32[]{:S(2)}, u32[]{:S(2)}) collective-permute-start(f16[64,1024]{1,0:T(8,128)(2,1)S(1)} %slice_convert_fusion.5), channel_id=1, source_target_pairs={{0,8},{2,10},{4,12},{6,14},{8,0},{10,2},{12,4},{14,6},{1,9},{3,11}... | collective-permute-start | bytes 393224 | tf_op jit(solution)/shard_map/ppermute | solution.py:409
  81.2 7.1 %collective-permute-start.15 = (f32[32,1536]{1,0:T(8,128)S(1)}, f32[32,1536]{1,0:T(8,128)S(1)}, u32[]{:S(2)}, u32[]{:S(2)}) collective-permute-start(f32[32,1536]{1,0:T(8,128)S(1)} %get-tuple-element.56), channel_id=1, source_target_pairs={{0,1},{1,0},{2,3},{3,2},{4,5},{5,4},{6,7},{7,6},{8,9},{9,8},{10,11... | collective-permute-start | bytes 589832 | tf_op jit(solution)/shard_map/ppermute | solution.py:522
  87.5 5.0 %collective-permute-start.16 = (f32[32,1024]{1,0:T(8,128)S(1)}, f32[32,1024]{1,0:T(8,128)S(1)}, u32[]{:S(2)}, u32[]{:S(2)}) collective-permute-start(f32[32,1024]{1,0:T(8,128)S(1)} %get-tuple-element.60), channel_id=1, source_target_pairs={{0,1},{1,0},{2,3},{3,2},{4,5},{5,4},{6,7},{7,6},{8,9},{9,8},{10,11... | collective-permute-start | bytes 393224 | tf_op jit(solution)/shard_map/ppermute | solution.py:522
  95.1 3.8 %collective-permute-start.19 = (f32[2,64,128]{2,1,0:T(8,128)S(1)}, f32[2,64,128]{2,1,0:T(8,128)S(1)}, u32[]{:S(2)}, u32[]{:S(2)}) collective-permute-start(f32[2,64,128]{2,1,0:T(8,128)S(1)} %get-tuple-element.48), channel_id=1, source_target_pairs={{0,3},{1,2},{2,1},{3,0},{4,7},{5,6},{6,5},{7,4},{8,11},{9,10},{10,... | collective-permute-start | bytes 196616 | tf_op jit(solution)/shard_map/ppermute | solution.py:423
  95.2 5.0 %collective-permute-start.18 = (f32[2,64,128]{2,1,0:T(8,128)S(1)}, f32[2,64,128]{2,1,0:T(8,128)S(1)}, u32[]{:S(2)}, u32[]{:S(2)}) collective-permute-start(f32[2,64,128]{2,1,0:T(8,128)S(1)} %get-tuple-element.48), channel_id=1, source_target_pairs={{0,1},{1,0},{2,3},{3,2},{4,5},{5,4},{6,7},{7,6},{8,9},{9,8},{10,11... | collective-permute-start | bytes 196616 | tf_op jit(solution)/shard_map/ppermute | solution.py:409
  95.8 4.3 %collective-permute-start.17 = (f32[2,64,128]{2,1,0:T(8,128)S(1)}, f32[2,64,128]{2,1,0:T(8,128)S(1)}, u32[]{:S(2)}, u32[]{:S(2)}) collective-permute-start(f32[2,64,128]{2,1,0:T(8,128)S(1)} %get-tuple-element.48), channel_id=1, source_target_pairs={{0,2},{2,0},{4,6},{6,4},{8,10},{10,8},{12,14},{14,12},{1,3},{3,1},... | collective-permute-start | bytes 196616 | tf_op jit(solution)/shard_map/ppermute | solution.py:409
  100.2 8.9 %copy-start.1 = (bf16[768,256]{1,0:T(8,128)(2,1)S(1)}, bf16[768,256]{1,0:T(8,128)(2,1)}, u32[]{:S(2)}) copy-start(bf16[768,256]{1,0:T(8,128)(2,1)} %constant.121.clone.over_lanes_ref) | copy-start | bytes 1179652
  100.2 8.9 %copy-start.4 = (bf16[384,256]{1,0:T(8,128)(2,1)S(1)}, bf16[384,256]{1,0:T(8,128)(2,1)}, u32[]{:S(2)}) copy-start(bf16[384,256]{1,0:T(8,128)(2,1)} %constant.124.clone.across_ref) | copy-start | bytes 589828
  100.2 8.9 %copy-start.5 = (bf16[128,384]{1,0:T(8,128)(2,1)S(1)}, bf16[128,384]{1,0:T(8,128)(2,1)}, u32[]{:S(2)}) copy-start(bf16[128,384]{1,0:T(8,128)(2,1)} %constant.120.clone.over_rows_ref) | copy-start | bytes 294916
  100.2 8.9 %copy-start.6 = (f32[2,64,128]{2,1,0:T(8,128)S(1)}, f32[2,64,128]{2,1,0:T(8,128)}, u32[]{:S(2)}) copy-start(f32[2,64,128]{2,1,0:T(8,128)} %constant.122.clone.twist_ref) | copy-start | bytes 196612
  100.2 8.9 %copy-start.7 = (bf16[64,192]{1,0:T(8,128)(2,1)S(1)}, bf16[64,192]{1,0:T(8,128)(2,1)}, u32[]{:S(2)}) copy-start(bf16[64,192]{1,0:T(8,128)(2,1)} %constant.123.clone.below_ref) | copy-start | bytes 73732
  100.2 6.8 %collective-permute-start.22 = (f32[2,64,128]{2,1,0:T(8,128)S(1)}, f32[2,64,128]{2,1,0:T(8,128)S(1)}, u32[]{:S(2)}, u32[]{:S(2)}) collective-permute-start(f32[2,64,128]{2,1,0:T(8,128)S(1)} %add_add_fusion.1), channel_id=1, source_target_pairs={{0,12},{2,14},{4,8},{6,10},{8,4},{10,6},{12,0},{14,2},{1,13},{3,15... | collective-permute-start | bytes 196616 | tf_op jit(solution)/shard_map/ppermute | solution.py:409
  102.5 6.5 %collective-permute-start.21 = (f32[2,64,128]{2,1,0:T(8,128)S(1)}, f32[2,64,128]{2,1,0:T(8,128)S(1)}, u32[]{:S(2)}, u32[]{:S(2)}) collective-permute-start(f32[2,64,128]{2,1,0:T(8,128)S(1)} %add_add_fusion.1), channel_id=1, source_target_pairs={{0,8},{2,10},{4,12},{6,14},{8,0},{10,2},{12,4},{14,6},{1,9},{3,11}... | collective-permute-start | bytes 196616 | tf_op jit(solution)/shard_map/ppermute | solution.py:409
  102.5 6.5 %collective-permute-start.20 = (f32[2,64,128]{2,1,0:T(8,128)S(1)}, f32[2,64,128]{2,1,0:T(8,128)S(1)}, u32[]{:S(2)}, u32[]{:S(2)}) collective-permute-start(f32[2,64,128]{2,1,0:T(8,128)S(1)} %add_add_fusion.1), channel_id=1, source_target_pairs={{0,4},{2,6},{4,0},{6,2},{8,12},{10,14},{12,8},{14,10},{1,5},{3,7},... | collective-permute-start | bytes 196616 | tf_op jit(solution)/shard_map/ppermute | solution.py:409

commit v3 on v2

--- a/solution.py
+++ b/solution.py
@@ -13,7 +13,8 @@
 NTAP = 4
 MARGIN = 24
 LANES = 128
-SHARES = (12, 12, 8)
+SHARES = (8, 8, 8, 4, 4)
+STAGES = (0, 1, 2)
 EPSILON = 1e-06
 BF16 = jnp.bfloat16
 F32 = jnp.float32
@@ -188,7 +189,9 @@
         ],
         out_specs=(pl.BlockSpec((half, tile), lambda i: (0, i)),) * 2,
         compiler_params=pltpu.CompilerParams(vmem_limit_bytes=40 * 2**20),
-        cost_estimate=pl.CostEstimate(flops=cells, bytes_accessed=cells, transcendentals=0),
+        cost_estimate=pl.CostEstimate(
+            flops=4 * rows * cells * pings, bytes_accessed=4 * cells * pings + 8 * half * cells, transcendentals=0
+        ),
         name="image",
     )(left, steer)
 
@@ -477,11 +480,10 @@
     known = largest(echo, taps, steer)
     known = jnp.maximum(known, swap(known, "ping", 1))
     bits = [1 << at for at in range(1, pings.bit_length() - 1)]
-    steps = [("ping", bit) for bit in bits] + [("rng", 1 << at) for at in range(tiles.bit_length() - 1)]
     echo_lines = tie(echo_lines, known)
-    got = swap(known, *steps[0])
+    others = [swap(known, "ping", 2 * at) for at in range(1, pings // 2)]
     left = interpolate(start_rows(pings, tiles, lines), offsets, taps, echo_lines)
-    known = jnp.maximum(known, tie(got, left))
+    known = functools.reduce(jnp.maximum, lax.optimization_barrier((known, left, *others))[2:], known)
 
     count = len(cuts)
     totals, moving = [None] * count, [None] * count
@@ -496,23 +498,23 @@
         return send
 
     gate = known
-    for at in range(count + 1):
-        if at < count:
+    for turn_at in range(count + 1 + len(bits)):
+        if turn_at < count:
             left = tie(left, gate)
-            totals[at], theirs = partial_image(left, steer, *cuts[at])
-            moving[at] = swap(theirs, "ping", 1)
+            totals[turn_at], theirs = partial_image(left, steer, *cuts[turn_at])
+            moving[turn_at] = swap(theirs, "ping", 1)
             gate = theirs
-        for step in steps[1:] if at == 1 else steps[1:2] if at == 0 else []:
-            if at == 0 or step != steps[1]:
-                known = jnp.maximum(known, tie(swap(known, *step), gate))
-                gate = known
-        if at == 1:
+        if turn_at == 0:
+            bit = 1
+            while bit < tiles:
+                known = jnp.maximum(known, tie(swap(known, "rng", bit), gate))
+                bit *= 2
+            gate = known
             up, down = scale_of(known, 2.0 * NTAP * steer.shape[2] * pings)
-        for stage in range(min(at, 2)):
-            gate = advance(at - 1 - stage, stage, gate)
-    waiting = [(count - 1, 1)] + [(at, stage) for at in range(count) for stage in range(2, len(bits) + 1)]
-    for at, stage in sorted(waiting, key=lambda item: (item[0] + 2 * item[1], item[1])):
-        advance(at, stage, gate if stage == 1 else None)
+        for stage in STAGES:
+            at = turn_at - 1 - stage
+            if 0 <= at < count and stage <= len(bits):
+                gate = advance(at, stage, gate)
     own, far = [], []
     for total in totals:
         own.append(total[: 2 * lines])

time: 113 us -> 106 us (0.938)
  waiting for transfers between devices: 40.5 us -> 25.1 us
  starting transfers between devices: 30 us -> 33.9 us
  Pallas kernels: 36.1 us -> 38.9 us
  other arithmetic: 4.25 us -> 5.72 us
    ppermute x19 -> x26, waiting for transfers between devices: 34.3 us -> 21.2 us  [swap(): return lax.ppermute(value, axis, [(at, at ^ bit) for at in range(count)])]
    pallas_call x3 -> x5, Pallas kernels: 16.1 us -> 19 us  [partial_image(): pl.pallas_call(image_kernel, grid=(cells // tile,), out_shape=(jax.ShapeD...]
    ppermute x3 -> x5, starting transfers between devices: 3.58 us -> 5.78 us  [on_device(): lax.ppermute(send, 'rng', [(at, (at + step) % tiles) for at in range(tile...]
    ppermute x1, waiting for transfers between devices: 1.92 us -> 0.01 us  [total_over(): third = lax.ppermute(value, (axis, other), both)]
    ppermute x19 -> x26, starting transfers between devices: 26.3 us -> 28.1 us  [swap(): return lax.ppermute(value, axis, [(at, at ^ bit) for at in range(count)])]
    mul x3 -> x5, other arithmetic: 2.57 us -> 4.06 us  [advance(): (totals[at] + got) * up[0, 0]]
    ppermute x3 -> x5, waiting for transfers between devices: 4.36 us -> 3.86 us  [on_device(): lax.ppermute(send, 'rng', [(at, (at + step) % tiles) for at in range(tile...]
  transfers between devices with their start and end apart: 23 -> 32, of which waited for: 16 -> 12; matrix products, arithmetic and copies ran while one was open for 4% -> 6% of each run, Pallas kernels for 21% -> 27%
where the time goes in v3:
time: 106 us
  Pallas kernels  38.9 us (37%)
  starting transfers between devices  33.9 us (32%)
  waiting for transfers between devices  25.1 us (24%)
  other arithmetic  5.72 us (5%)
  between operations  1.22 us (1%)
    ppermute x26, starting transfers between devices, swap(): return lax.ppermute(value, axis, [(at, at ^ bit) for at in range(count)])  28.1 us
    ppermute x26, waiting for transfers between devices, swap(): return lax.ppermute(value, axis, [(at, at ^ bit) for at in range(count)])  21.2 us
    pallas_call x5, Pallas kernels, partial_image(): pl.pallas_call(image_kernel, grid=(cells // tile,), out_shape=(jax.ShapeD...  19 us
    pallas_call x1, Pallas kernels, largest(): pl.pallas_call(largest_kernel, out_shape=jax.ShapeDtypeStruct((3, 8, LANE...  7.9 us
    ppermute x5, starting transfers between devices, on_device(): lax.ppermute(send, 'rng', [(at, (at + step) % tiles) for at in range(tile...  5.78 us
    pallas_call x1, Pallas kernels, focus(): pl.pallas_call(focus_kernel, out_shape=(jax.ShapeDtypeStruct((2, lines, r...  4.08 us
    mul x5, other arithmetic, advance(): (totals[at] + got) * up[0, 0]  4.06 us
    pallas_call x1, Pallas kernels, interpolate(): pl.pallas_call(interp_kernel, grid=(pings // LANES,), out_shape=jax.Shape...  3.87 us
  transfers between devices with their start and end apart: 32, of which 12 were waited for; matrix products, arithmetic and copies ran while one was open for 6% of the time, Pallas kernels for 27%

profile of v3, /device:TPU:0, one launch (start us, length us, event | category | flops | bytes accessed | tf_op | source)
XLA Modules:
  0.0 105.5 jit_solution(9692020667321834899)
XLA Ops:
  0.6 3.0 %collective-permute-start.1 = (bf16[2,1024,128]{2,1,0:T(8,128)(2,1)}, bf16[2,1024,128]{2,1,0:T(8,128)(2,1)S(1)}, u32[]{:S(2)}, u32[]{:S(2)}) collective-permute-start(bf16[2,1024,128]{2,1,0:T(8,128)(2,1)} %echo_ref.1), channel_id=1, source_target_pairs={{0,1},{1,0},{2,3},{3,2},{4,5},{5,4},{6,7},{7,6},{8,9},{9,8},{10,11... | collective-permute-start | bytes 1572872 | tf_op jit(solution)/shard_map/ppermute | solution.py:412
  3.6 7.9 %largest.1 = f32[3,8,128]{2,1,0:T(8,128)} custom-call(bf16[2,1024,128]{2,1,0:T(8,128)(2,1)} %echo_ref.1, f32[4,16]{1,0:T(4,128)} %bitcast.21, bf16[2,4096,1024]{2,1,0:T(8,128)(2,1)} %steer_ref.11), custom_call_target="tpu_custom_call" | custom-call | flops 8388608 | bytes 16777216 | tf_op jit(solution)/shard_map/largest/pallas_call | solution.py:154
  11.5 0.1 collective-permute-start
  11.7 1.3 %collective-permute-done = f32[3,8,128]{2,1,0:T(8,128)S(1)} collective-permute-done((f32[3,8,128]{2,1,0:T(8,128)}, f32[3,8,128]{2,1,0:T(8,128)S(1)}, u32[]{:S(2)}, u32[]{:S(2)}) %collective-permute-start) | collective-permute-done | bytes 12320 | tf_op jit(solution)/shard_map/ppermute | solution.py:412
  13.0 0.7 max.27
  13.7 1.6 %collective-permute-start.2 = (f32[3,8,128]{2,1,0:T(8,128)S(1)}, f32[3,8,128]{2,1,0:T(8,128)S(1)}, u32[]{:S(2)}, u32[]{:S(2)}) collective-permute-start(f32[3,8,128]{2,1,0:T(8,128)S(1)} %max.27), channel_id=1, source_target_pairs={{0,4},{2,6},{4,0},{6,2},{8,12},{10,14},{12,8},{14,10},{1,5},{3,7},... | collective-permute-start | bytes 36872 | tf_op jit(solution)/shard_map/ppermute | solution.py:412
  15.3 2.6 %collective-permute-start.3 = (f32[3,8,128]{2,1,0:T(8,128)S(1)}, f32[3,8,128]{2,1,0:T(8,128)S(1)}, u32[]{:S(2)}, u32[]{:S(2)}) collective-permute-start(f32[3,8,128]{2,1,0:T(8,128)S(1)} %max.27), channel_id=1, source_target_pairs={{0,8},{2,10},{4,12},{6,14},{8,0},{10,2},{12,4},{14,6},{1,9},{3,11}... | collective-permute-start | bytes 36872 | tf_op jit(solution)/shard_map/ppermute | solution.py:412
  17.9 0.2 collective-permute-start.4
  18.1 0.1 broadcast_select_fusion.1
  18.2 0.1 pad_maximum_fusion.echo_ref
  18.3 3.9 %interp.1.left_ref = bf16[2,512,1024]{2,1,0:T(8,128)(2,1)S(1)} custom-call(s32[16]{0:T(128)S(1)} %fusion.11.starts_ref, s32[16]{0:T(128)S(1)} %copy-done.9, f32[4,16]{1,0:T(4,128)S(1)} %bitcast.22, bf16[2,1024,256]{2,1,0:T(8,128)(2,1)S(1)} %pad_maximum_fusion.echo_ref), custom_call_target="tpu_custom_call" | custom-call | flops 4194304 | bytes 3145728 | tf_op jit(solution)/shard_map/interp/pallas_call | solution.py:115
  22.2 1.1 %collective-permute-done.4 = f32[3,8,128]{2,1,0:T(8,128)S(1)} collective-permute-done((f32[3,8,128]{2,1,0:T(8,128)S(1)}, f32[3,8,128]{2,1,0:T(8,128)S(1)}, u32[]{:S(2)}, u32[]{:S(2)}) %collective-permute-start.4) | collective-permute-done | bytes 12320 | tf_op jit(solution)/shard_map/ppermute | solution.py:412
  23.4 4.3 %image.5 = (f32[256,1024]{1,0:T(8,128)S(1)}, f32[256,1024]{1,0:T(8,128)S(1)}) custom-call(bf16[2,512,1024]{2,1,0:T(8,128)(2,1)S(1)} %interp.1.left_ref, bf16[2,4096,1024]{2,1,0:T(8,128)(2,1)} %steer_ref.11), custom_call_target="tpu_custom_call" | custom-call | flops 2147483648 | bytes 6291456 | tf_op jit(solution)/shard_map/image/pallas_call | solution.py:182
  27.7 0.1 collective-permute-start.6
  27.9 0.6 collective-permute-start.5
  28.5 3.2 %collective-permute-done.5 = f32[3,8,128]{2,1,0:T(8,128)S(1)} collective-permute-done((f32[3,8,128]{2,1,0:T(8,128)S(1)}, f32[3,8,128]{2,1,0:T(8,128)S(1)}, u32[]{:S(2)}, u32[]{:S(2)}) %collective-permute-start.5) | collective-permute-done | bytes 12320 | tf_op jit(solution)/shard_map/ppermute | solution.py:412
  31.6 4.3 %image.6 = (f32[256,1024]{1,0:T(8,128)S(1)}, f32[256,1024]{1,0:T(8,128)S(1)}) custom-call(bf16[2,512,1024]{2,1,0:T(8,128)(2,1)S(1)} %interp.1.left_ref, bf16[2,4096,1024]{2,1,0:T(8,128)(2,1)} %steer_ref.11), custom_call_target="tpu_custom_call" | custom-call | flops 2147483648 | bytes 6291456 | tf_op jit(solution)/shard_map/image/pallas_call | solution.py:182
  36.0 0.1 collective-permute-start.8
  36.1 0.5 slice.119
  36.6 0.9 add_multiply_fusion.2
  37.5 0.1 collective-permute-start.7
  37.6 4.5 %image.7 = (f32[256,1024]{1,0:T(8,128)S(1)}, f32[256,1024]{1,0:T(8,128)S(1)}) custom-call(bf16[2,512,1024]{2,1,0:T(8,128)(2,1)S(1)} %interp.1.left_ref, bf16[2,4096,1024]{2,1,0:T(8,128)(2,1)} %steer_ref.11), custom_call_target="tpu_custom_call" | custom-call | flops 2147483648 | bytes 6291456 | tf_op jit(solution)/shard_map/image/pallas_call | solution.py:182
  42.2 0.6 collective-permute-start.11
  42.7 0.9 add_multiply_fusion.1
  43.6 1.8 %collective-permute-start.10 = (f16[128,1024]{1,0:T(8,128)(2,1)S(1)}, f16[128,1024]{1,0:T(8,128)(2,1)S(1)}, u32[]{:S(2)}, u32[]{:S(2)}) collective-permute-start(f16[128,1024]{1,0:T(8,128)(2,1)S(1)} %slice_convert_fusion.1), channel_id=1, source_target_pairs={{0,4},{2,6},{4,0},{6,2},{8,12},{10,14},{12,8},{14,10},{1,5},{3,7},... | collective-permute-start | bytes 786440 | tf_op jit(solution)/shard_map/ppermute | solution.py:412
  45.4 0.9 collective-permute-done.7
  46.3 0.1 slice_add_fusion.2
  46.4 1.4 %collective-permute-start.9 = (f16[64,1024]{1,0:T(8,128)(2,1)S(1)}, f16[64,1024]{1,0:T(8,128)(2,1)S(1)}, u32[]{:S(2)}, u32[]{:S(2)}) collective-permute-start(f16[64,1024]{1,0:T(8,128)(2,1)S(1)} %slice_convert_fusion.7), channel_id=1, source_target_pairs={{0,8},{2,10},{4,12},{6,14},{8,0},{10,2},{12,4},{14,6},{1,9},{3,11}... | collective-permute-start | bytes 393224 | tf_op jit(solution)/shard_map/ppermute | solution.py:412
  47.8 2.9 %image.8 = (f32[256,512]{1,0:T(8,128)S(1)}, f32[256,512]{1,0:T(8,128)S(1)}) custom-call(bf16[2,512,1024]{2,1,0:T(8,128)(2,1)S(1)} %interp.1.left_ref, bf16[2,4096,1024]{2,1,0:T(8,128)(2,1)} %steer_ref.11), custom_call_target="tpu_custom_call" | custom-call | flops 1073741824 | bytes 3145728 | tf_op jit(solution)/shard_map/image/pallas_call | solution.py:182
  50.6 0.1 collective-permute-start.14
  50.7 0.9 add_multiply_fusion
  51.6 1.8 %collective-permute-start.13 = (f16[128,1024]{1,0:T(8,128)(2,1)S(1)}, f16[128,1024]{1,0:T(8,128)(2,1)S(1)}, u32[]{:S(2)}, u32[]{:S(2)}) collective-permute-start(f16[128,1024]{1,0:T(8,128)(2,1)S(1)} %slice_convert_fusion), channel_id=1, source_target_pairs={{0,4},{2,6},{4,0},{6,2},{8,12},{10,14},{12,8},{14,10},{1,5},{3,7},... | collective-permute-start | bytes 786440 | tf_op jit(solution)/shard_map/ppermute | solution.py:412
  53.4 1.6 %collective-permute-done.10 = f16[128,1024]{1,0:T(8,128)(2,1)S(1)} collective-permute-done((f16[128,1024]{1,0:T(8,128)(2,1)S(1)}, f16[128,1024]{1,0:T(8,128)(2,1)S(1)}, u32[]{:S(2)}, u32[]{:S(2)}) %collective-permute-start.10) | collective-permute-done | bytes 262176 | tf_op jit(solution)/shard_map/ppermute | solution.py:412
  55.1 0.1 slice_add_fusion.1
  55.2 1.2 %collective-permute-start.12 = (f16[64,1024]{1,0:T(8,128)(2,1)S(1)}, f16[64,1024]{1,0:T(8,128)(2,1)S(1)}, u32[]{:S(2)}, u32[]{:S(2)}) collective-permute-start(f16[64,1024]{1,0:T(8,128)(2,1)S(1)} %slice_convert_fusion.6), channel_id=1, source_target_pairs={{0,8},{2,10},{4,12},{6,14},{8,0},{10,2},{12,4},{14,6},{1,9},{3,11}... | collective-permute-start | bytes 393224 | tf_op jit(solution)/shard_map/ppermute | solution.py:412
  56.4 2.9 %image.9 = (f32[256,512]{1,0:T(8,128)S(1)}, f32[256,512]{1,0:T(8,128)S(1)}) custom-call(bf16[2,512,1024]{2,1,0:T(8,128)(2,1)S(1)} %interp.1.left_ref, bf16[2,4096,1024]{2,1,0:T(8,128)(2,1)} %steer_ref.11), custom_call_target="tpu_custom_call" | custom-call | flops 1073741824 | bytes 3145728 | tf_op jit(solution)/shard_map/image/pallas_call | solution.py:182
  59.3 0.1 collective-permute-start.17
  59.4 0.7 add_multiply_fusion.4
  60.2 2.5 %collective-permute-start.16 = (f16[128,512]{1,0:T(8,128)(2,1)S(1)}, f16[128,512]{1,0:T(8,128)(2,1)S(1)}, u32[]{:S(2)}, u32[]{:S(2)}) collective-permute-start(f16[128,512]{1,0:T(8,128)(2,1)S(1)} %slice_convert_fusion.5), channel_id=1, source_target_pairs={{0,4},{2,6},{4,0},{6,2},{8,12},{10,14},{12,8},{14,10},{1,5},{3,7},... | collective-permute-start | bytes 393224 | tf_op jit(solution)/shard_map/ppermute | solution.py:412
  62.7 0.6 collective-permute-start.21
  63.3 0.1 collective-permute-done.13
  63.5 1.2 %collective-permute-start.15 = (f16[64,1024]{1,0:T(8,128)(2,1)S(1)}, f16[64,1024]{1,0:T(8,128)(2,1)S(1)}, u32[]{:S(2)}, u32[]{:S(2)}) collective-permute-start(f16[64,1024]{1,0:T(8,128)(2,1)S(1)} %slice_convert_fusion.4), channel_id=1, source_target_pairs={{0,8},{2,10},{4,12},{6,14},{8,0},{10,2},{12,4},{14,6},{1,9},{3,11}... | collective-permute-start | bytes 393224 | tf_op jit(solution)/shard_map/ppermute | solution.py:412
  64.8 0.6 collective-permute-start.22
  65.4 0.7 add_multiply_fusion.3
  66.2 2.5 %collective-permute-start.19 = (f16[128,512]{1,0:T(8,128)(2,1)S(1)}, f16[128,512]{1,0:T(8,128)(2,1)S(1)}, u32[]{:S(2)}, u32[]{:S(2)}) collective-permute-start(f16[128,512]{1,0:T(8,128)(2,1)S(1)} %slice_convert_fusion.3), channel_id=1, source_target_pairs={{0,4},{2,6},{4,0},{6,2},{8,12},{10,14},{12,8},{14,10},{1,5},{3,7},... | collective-permute-start | bytes 393224 | tf_op jit(solution)/shard_map/ppermute | solution.py:412
  68.8 0.9 collective-permute-start.18
  69.7 3.6 %collective-permute-done.15 = f16[64,1024]{1,0:T(8,128)(2,1)S(1)} collective-permute-done((f16[64,1024]{1,0:T(8,128)(2,1)S(1)}, f16[64,1024]{1,0:T(8,128)(2,1)S(1)}, u32[]{:S(2)}, u32[]{:S(2)}) %collective-permute-start.15) | collective-permute-done | bytes 131104 | tf_op jit(solution)/shard_map/ppermute | solution.py:412
  73.4 2.0 %collective-permute-start.23 = (f32[32,1024]{1,0:T(8,128)S(1)}, f32[32,1024]{1,0:T(8,128)S(1)}, u32[]{:S(2)}, u32[]{:S(2)}) collective-permute-start(f32[32,1024]{1,0:T(8,128)S(1)} %get-tuple-element.88), channel_id=1, source_target_pairs={{0,1},{1,0},{2,3},{3,2},{4,5},{5,4},{6,7},{7,6},{8,9},{9,8},{10,11... | collective-permute-start | bytes 393224 | tf_op jit(solution)/shard_map/ppermute | solution.py:524
  75.4 0.1 collective-permute-start.20
  75.6 2.1 %collective-permute-start.24 = (f32[32,512]{1,0:T(8,128)S(1)}, f32[32,512]{1,0:T(8,128)S(1)}, u32[]{:S(2)}, u32[]{:S(2)}) collective-permute-start(f32[32,512]{1,0:T(8,128)S(1)} %get-tuple-element.96), channel_id=1, source_target_pairs={{0,1},{1,0},{2,3},{3,2},{4,5},{5,4},{6,7},{7,6},{8,9},{9,8},{10,11... | collective-permute-start | bytes 196616 | tf_op jit(solution)/shard_map/ppermute | solution.py:524
  77.7 2.9 %collective-permute-done.20 = f16[64,512]{1,0:T(8,128)(2,1)S(1)} collective-permute-done((f16[64,512]{1,0:T(8,128)(2,1)S(1)}, f16[64,512]{1,0:T(8,128)(2,1)S(1)}, u32[]{:S(2)}, u32[]{:S(2)}) %collective-permute-start.20) | collective-permute-done | bytes 65568 | tf_op jit(solution)/shard_map/ppermute | solution.py:412
  80.7 0.4 collective-permute-start.25
  81.2 3.9 %collective-permute-done.25 = f32[32,512]{1,0:T(8,128)S(1)} collective-permute-done((f32[32,512]{1,0:T(8,128)S(1)}, f32[32,512]{1,0:T(8,128)S(1)}, u32[]{:S(2)}, u32[]{:S(2)}) %collective-permute-start.25) | collective-permute-done | bytes 65568 | tf_op jit(solution)/shard_map/ppermute | solution.py:524
  85.1 2.5 %gradient.1 = (f32[2,1024,128]{2,1,0:T(8,128)S(1)}, f32[2,64,128]{2,1,0:T(8,128)S(1)}) custom-call(s32[2]{0:T(128)S(1)} %and_select_fusion.5.tile_ref, s32[16]{0:T(128)S(1)} %copy-done.10, s32[16]{0:T(128)S(1)} %copy-done.11, f32[2,16]{1,0:T(2,128)S(1)} %pad_maximum_fusion.1.turn_ref, f32[8,128]{1,0:T(8,128)S(1)} %get-tuple-element.50.down_ref, ...), custom_call_target="tpu_custom_call" | custom-call | flops 314572800 | bytes 2097152 | tf_op jit(solution)/shard_map/gradient/pallas_call | solution.py:289
  87.7 0.4 collective-permute-start.27
  88.1 1.8 %collective-permute-start.26 = (f32[2,64,128]{2,1,0:T(8,128)S(1)}, f32[2,64,128]{2,1,0:T(8,128)S(1)}, u32[]{:S(2)}, u32[]{:S(2)}) collective-permute-start(f32[2,64,128]{2,1,0:T(8,128)S(1)} %get-tuple-element.80), channel_id=1, source_target_pairs={{0,2},{2,0},{4,6},{6,4},{8,10},{10,8},{12,14},{14,12},{1,3},{3,1},... | collective-permute-start | bytes 196616 | tf_op jit(solution)/shard_map/ppermute | solution.py:412
  89.9 2.6 %collective-permute-done.27 = f32[2,64,128]{2,1,0:T(8,128)S(1)} collective-permute-done((f32[2,64,128]{2,1,0:T(8,128)S(1)}, f32[2,64,128]{2,1,0:T(8,128)S(1)}, u32[]{:S(2)}, u32[]{:S(2)}) %collective-permute-start.27) | collective-permute-done | bytes 65568 | tf_op jit(solution)/shard_map/ppermute | solution.py:412
  92.5 0.2 collective-permute-start.30
  92.7 2.0 %collective-permute-start.31 = (f32[2,64,128]{2,1,0:T(8,128)S(1)}, f32[2,64,128]{2,1,0:T(8,128)S(1)}, u32[]{:S(2)}, u32[]{:S(2)}) collective-permute-start(f32[2,64,128]{2,1,0:T(8,128)S(1)} %add_add_fusion.1), channel_id=1, source_target_pairs={{0,12},{2,14},{4,8},{6,10},{8,4},{10,6},{12,0},{14,2},{1,13},{3,15... | collective-permute-start | bytes 196616 | tf_op jit(solution)/shard_map/ppermute | solution.py:412
  94.7 1.4 %collective-permute-start.29 = (f32[2,64,128]{2,1,0:T(8,128)S(1)}, f32[2,64,128]{2,1,0:T(8,128)S(1)}, u32[]{:S(2)}, u32[]{:S(2)}) collective-permute-start(f32[2,64,128]{2,1,0:T(8,128)S(1)} %add_add_fusion.1), channel_id=1, source_target_pairs={{0,4},{2,6},{4,0},{6,2},{8,12},{10,14},{12,8},{14,10},{1,5},{3,7},... | collective-permute-start | bytes 196616 | tf_op jit(solution)/shard_map/ppermute | solution.py:412
  96.1 1.6 %spectrum.1.bins_ref = f32[1024,256]{1,0:T(8,128)S(1)} custom-call(bf16[128,384]{1,0:T(8,128)(2,1)S(1)} %copy-done.2, bf16[768,256]{1,0:T(8,128)(2,1)S(1)} %copy-done, f32[2,64,128]{2,1,0:T(8,128)S(1)} %copy-done.3, f32[2,1024,128]{2,1,0:T(8,128)S(1)} %get-tuple-element.81.grid_ref), custom_call_target="tpu_custom_call" | custom-call | flops 314572800 | bytes 2097152 | tf_op jit(solution)/shard_map/spectrum/pallas_call | solution.py:316
  97.6 2.5 %collective-permute-done.30 = f32[2,64,128]{2,1,0:T(8,128)S(1)} collective-permute-done((f32[2,64,128]{2,1,0:T(8,128)S(1)}, f32[2,64,128]{2,1,0:T(8,128)S(1)}, u32[]{:S(2)}, u32[]{:S(2)}) %collective-permute-start.30) | collective-permute-done | bytes 65568 | tf_op jit(solution)/shard_map/ppermute | solution.py:412
  100.1 1.3 %collective-permute-done.29 = f32[2,64,128]{2,1,0:T(8,128)S(1)} collective-permute-done((f32[2,64,128]{2,1,0:T(8,128)S(1)}, f32[2,64,128]{2,1,0:T(8,128)S(1)}, u32[]{:S(2)}, u32[]{:S(2)}) %collective-permute-start.29) | collective-permute-done | bytes 65568 | tf_op jit(solution)/shard_map/ppermute | solution.py:412
  101.5 4.1 %focus.1 = (f32[2,16,8192]{2,1,0:T(8,128)}, f32[64,128]{1,0:T(8,128)}) custom-call(bf16[128,384]{1,0:T(8,128)(2,1)S(1)} %copy-done.5, bf16[768,256]{1,0:T(8,128)(2,1)S(1)} %copy-done.1, f32[2,64,128]{2,1,0:T(8,128)S(1)} %copy-done.6, bf16[64,192]{1,0:T(8,128)(2,1)S(1)} %copy-done.7, bf16[384,256]{1,0:T(8,128)(2,1)S(1)} %copy-done.4, ...), custom_call_target="tpu_custom_call" | custom-call | flops 314572800 | bytes 2097152 | tf_op jit(solution)/shard_map/focus/pallas_call | solution.py:393
  (80 shorter events, 0.8 us)
Async XLA Ops:
  0.6 17.5 %collective-permute-start.1 = (bf16[2,1024,128]{2,1,0:T(8,128)(2,1)}, bf16[2,1024,128]{2,1,0:T(8,128)(2,1)S(1)}, u32[]{:S(2)}, u32[]{:S(2)}) collective-permute-start(bf16[2,1024,128]{2,1,0:T(8,128)(2,1)} %echo_ref.1), channel_id=1, source_target_pairs={{0,1},{1,0},{2,3},{3,2},{4,5},{5,4},{6,7},{7,6},{8,9},{9,8},{10,11... | collective-permute-start | bytes 1572872 | tf_op jit(solution)/shard_map/ppermute | solution.py:412
  3.6 14.5 %copy-start.12 = (bf16[2,1024,128]{2,1,0:T(8,128)(2,1)S(1)}, bf16[2,1024,128]{2,1,0:T(8,128)(2,1)}, u32[]{:S(2)}) copy-start(bf16[2,1024,128]{2,1,0:T(8,128)(2,1)} %echo_ref.1) | copy-start | bytes 1572868
  11.5 1.5 %collective-permute-start = (f32[3,8,128]{2,1,0:T(8,128)}, f32[3,8,128]{2,1,0:T(8,128)S(1)}, u32[]{:S(2)}, u32[]{:S(2)}) collective-permute-start(f32[3,8,128]{2,1,0:T(8,128)} %largest.1), channel_id=1, source_target_pairs={{0,2},{2,0},{4,6},{6,4},{8,10},{10,8},{12,14},{14,12},{1,3},{3,1},... | collective-permute-start | bytes 36872 | tf_op jit(solution)/shard_map/ppermute | solution.py:412
  13.7 4.6 %copy-start.8 = (f32[16,4]{0,1:T(4,128)S(1)}, f32[16,4]{0,1:T(4,128)}, u32[]{:S(2)}) copy-start(f32[16,4]{0,1:T(4,128)} %param.17) | copy-start | bytes 772
  13.7 4.6 %copy-start.9 = (s32[16]{0:T(128)S(1)}, s32[16]{0:T(128)}, u32[]{:S(2)}) copy-start(s32[16]{0:T(128)} %offsets_ref.1) | copy-start | bytes 196
  13.7 8.5 %collective-permute-start.2 = (f32[3,8,128]{2,1,0:T(8,128)S(1)}, f32[3,8,128]{2,1,0:T(8,128)S(1)}, u32[]{:S(2)}, u32[]{:S(2)}) collective-permute-start(f32[3,8,128]{2,1,0:T(8,128)S(1)} %max.27), channel_id=1, source_target_pairs={{0,4},{2,6},{4,0},{6,2},{8,12},{10,14},{12,8},{14,10},{1,5},{3,7},... | collective-permute-start | bytes 36872 | tf_op jit(solution)/shard_map/ppermute | solution.py:412
  15.3 6.9 %collective-permute-start.3 = (f32[3,8,128]{2,1,0:T(8,128)S(1)}, f32[3,8,128]{2,1,0:T(8,128)S(1)}, u32[]{:S(2)}, u32[]{:S(2)}) collective-permute-start(f32[3,8,128]{2,1,0:T(8,128)S(1)} %max.27), channel_id=1, source_target_pairs={{0,8},{2,10},{4,12},{6,14},{8,0},{10,2},{12,4},{14,6},{1,9},{3,11}... | collective-permute-start | bytes 36872 | tf_op jit(solution)/shard_map/ppermute | solution.py:412
  17.9 5.5 %collective-permute-start.4 = (f32[3,8,128]{2,1,0:T(8,128)S(1)}, f32[3,8,128]{2,1,0:T(8,128)S(1)}, u32[]{:S(2)}, u32[]{:S(2)}) collective-permute-start(f32[3,8,128]{2,1,0:T(8,128)S(1)} %max.27), channel_id=1, source_target_pairs={{0,12},{2,14},{4,8},{6,10},{8,4},{10,6},{12,0},{14,2},{1,13},{3,15... | collective-permute-start | bytes 36872 | tf_op jit(solution)/shard_map/ppermute | solution.py:412
  23.4 4.4 %copy-start.10 = (s32[16]{0:T(128)S(1)}, s32[16]{0:T(128)}, u32[]{:S(2)}) copy-start(s32[16]{0:T(128)} %centers_ref.1) | copy-start | bytes 196
  27.7 8.9 %collective-permute-start.6 = (f32[256,1024]{1,0:T(8,128)S(1)}, f32[256,1024]{1,0:T(8,128)S(1)}, u32[]{:S(2)}, u32[]{:S(2)}) collective-permute-start(f32[256,1024]{1,0:T(8,128)S(1)} %get-tuple-element.48), channel_id=1, source_target_pairs={{0,2},{2,0},{4,6},{6,4},{8,10},{10,8},{12,14},{14,12},{1,3},{3,1},... | collective-permute-start | bytes 3145736 | tf_op jit(solution)/shard_map/ppermute | solution.py:412
  27.9 3.8 %collective-permute-start.5 = (f32[3,8,128]{2,1,0:T(8,128)S(1)}, f32[3,8,128]{2,1,0:T(8,128)S(1)}, u32[]{:S(2)}, u32[]{:S(2)}) collective-permute-start(f32[3,8,128]{2,1,0:T(8,128)S(1)} %maximum_maximum_fusion), channel_id=1, source_target_pairs={{0,1},{1,0},{2,3},{3,2},{4,5},{5,4},{6,7},{7,6},{8,9},{9,8},{10,11... | collective-permute-start | bytes 36872 | tf_op jit(solution)/shard_map/ppermute | solution.py:412
  36.0 6.7 %collective-permute-start.8 = (f32[256,1024]{1,0:T(8,128)S(1)}, f32[256,1024]{1,0:T(8,128)S(1)}, u32[]{:S(2)}, u32[]{:S(2)}) collective-permute-start(f32[256,1024]{1,0:T(8,128)S(1)} %get-tuple-element.53), channel_id=1, source_target_pairs={{0,2},{2,0},{4,6},{6,4},{8,10},{10,8},{12,14},{14,12},{1,3},{3,1},... | collective-permute-start | bytes 3145736 | tf_op jit(solution)/shard_map/ppermute | solution.py:412
  37.5 8.8 %collective-permute-start.7 = (f16[128,1024]{1,0:T(8,128)(2,1)S(1)}, f16[128,1024]{1,0:T(8,128)(2,1)S(1)}, u32[]{:S(2)}, u32[]{:S(2)}) collective-permute-start(f16[128,1024]{1,0:T(8,128)(2,1)S(1)} %slice_convert_fusion.2), channel_id=1, source_target_pairs={{0,4},{2,6},{4,0},{6,2},{8,12},{10,14},{12,8},{14,10},{1,5},{3,7},... | collective-permute-start | bytes 786440 | tf_op jit(solution)/shard_map/ppermute | solution.py:412
  42.2 8.6 %collective-permute-start.11 = (f32[256,1024]{1,0:T(8,128)S(1)}, f32[256,1024]{1,0:T(8,128)S(1)}, u32[]{:S(2)}, u32[]{:S(2)}) collective-permute-start(f32[256,1024]{1,0:T(8,128)S(1)} %get-tuple-element.58), channel_id=1, source_target_pairs={{0,2},{2,0},{4,6},{6,4},{8,10},{10,8},{12,14},{14,12},{1,3},{3,1},... | collective-permute-start | bytes 3145736 | tf_op jit(solution)/shard_map/ppermute | solution.py:412
  43.6 11.5 %collective-permute-start.10 = (f16[128,1024]{1,0:T(8,128)(2,1)S(1)}, f16[128,1024]{1,0:T(8,128)(2,1)S(1)}, u32[]{:S(2)}, u32[]{:S(2)}) collective-permute-start(f16[128,1024]{1,0:T(8,128)(2,1)S(1)} %slice_convert_fusion.1), channel_id=1, source_target_pairs={{0,4},{2,6},{4,0},{6,2},{8,12},{10,14},{12,8},{14,10},{1,5},{3,7},... | collective-permute-start | bytes 786440 | tf_op jit(solution)/shard_map/ppermute | solution.py:412
  46.4 10.0 %collective-permute-start.9 = (f16[64,1024]{1,0:T(8,128)(2,1)S(1)}, f16[64,1024]{1,0:T(8,128)(2,1)S(1)}, u32[]{:S(2)}, u32[]{:S(2)}) collective-permute-start(f16[64,1024]{1,0:T(8,128)(2,1)S(1)} %slice_convert_fusion.7), channel_id=1, source_target_pairs={{0,8},{2,10},{4,12},{6,14},{8,0},{10,2},{12,4},{14,6},{1,9},{3,11}... | collective-permute-start | bytes 393224 | tf_op jit(solution)/shard_map/ppermute | solution.py:412
  50.6 8.7 %collective-permute-start.14 = (f32[256,512]{1,0:T(8,128)S(1)}, f32[256,512]{1,0:T(8,128)S(1)}, u32[]{:S(2)}, u32[]{:S(2)}) collective-permute-start(f32[256,512]{1,0:T(8,128)S(1)} %get-tuple-element.63), channel_id=1, source_target_pairs={{0,2},{2,0},{4,6},{6,4},{8,10},{10,8},{12,14},{14,12},{1,3},{3,1},... | collective-permute-start | bytes 1572872 | tf_op jit(solution)/shard_map/ppermute | solution.py:412
  51.6 11.8 %collective-permute-start.13 = (f16[128,1024]{1,0:T(8,128)(2,1)S(1)}, f16[128,1024]{1,0:T(8,128)(2,1)S(1)}, u32[]{:S(2)}, u32[]{:S(2)}) collective-permute-start(f16[128,1024]{1,0:T(8,128)(2,1)S(1)} %slice_convert_fusion), channel_id=1, source_target_pairs={{0,4},{2,6},{4,0},{6,2},{8,12},{10,14},{12,8},{14,10},{1,5},{3,7},... | collective-permute-start | bytes 786440 | tf_op jit(solution)/shard_map/ppermute | solution.py:412
  55.2 9.5 %collective-permute-start.12 = (f16[64,1024]{1,0:T(8,128)(2,1)S(1)}, f16[64,1024]{1,0:T(8,128)(2,1)S(1)}, u32[]{:S(2)}, u32[]{:S(2)}) collective-permute-start(f16[64,1024]{1,0:T(8,128)(2,1)S(1)} %slice_convert_fusion.6), channel_id=1, source_target_pairs={{0,8},{2,10},{4,12},{6,14},{8,0},{10,2},{12,4},{14,6},{1,9},{3,11}... | collective-permute-start | bytes 393224 | tf_op jit(solution)/shard_map/ppermute | solution.py:412
  59.3 6.1 %collective-permute-start.17 = (f32[256,512]{1,0:T(8,128)S(1)}, f32[256,512]{1,0:T(8,128)S(1)}, u32[]{:S(2)}, u32[]{:S(2)}) collective-permute-start(f32[256,512]{1,0:T(8,128)S(1)} %get-tuple-element.69), channel_id=1, source_target_pairs={{0,2},{2,0},{4,6},{6,4},{8,10},{10,8},{12,14},{14,12},{1,3},{3,1},... | collective-permute-start | bytes 1572872 | tf_op jit(solution)/shard_map/ppermute | solution.py:412
  60.2 8.6 %collective-permute-start.16 = (f16[128,512]{1,0:T(8,128)(2,1)S(1)}, f16[128,512]{1,0:T(8,128)(2,1)S(1)}, u32[]{:S(2)}, u32[]{:S(2)}) collective-permute-start(f16[128,512]{1,0:T(8,128)(2,1)S(1)} %slice_convert_fusion.5), channel_id=1, source_target_pairs={{0,4},{2,6},{4,0},{6,2},{8,12},{10,14},{12,8},{14,10},{1,5},{3,7},... | collective-permute-start | bytes 393224 | tf_op jit(solution)/shard_map/ppermute | solution.py:412
  62.7 18.4 %collective-permute-start.21 = (f32[32,1024]{1,0:T(8,128)S(1)}, f32[32,1024]{1,0:T(8,128)S(1)}, u32[]{:S(2)}, u32[]{:S(2)}) collective-permute-start(f32[32,1024]{1,0:T(8,128)S(1)} %get-tuple-element.92), channel_id=1, source_target_pairs={{0,1},{1,0},{2,3},{3,2},{4,5},{5,4},{6,7},{7,6},{8,9},{9,8},{10,11... | collective-permute-start | bytes 393224 | tf_op jit(solution)/shard_map/ppermute | solution.py:524
  63.5 9.8 %collective-permute-start.15 = (f16[64,1024]{1,0:T(8,128)(2,1)S(1)}, f16[64,1024]{1,0:T(8,128)(2,1)S(1)}, u32[]{:S(2)}, u32[]{:S(2)}) collective-permute-start(f16[64,1024]{1,0:T(8,128)(2,1)S(1)} %slice_convert_fusion.4), channel_id=1, source_target_pairs={{0,8},{2,10},{4,12},{6,14},{8,0},{10,2},{12,4},{14,6},{1,9},{3,11}... | collective-permute-start | bytes 393224 | tf_op jit(solution)/shard_map/ppermute | solution.py:412
  64.8 16.4 %collective-permute-start.22 = (f32[32,1024]{1,0:T(8,128)S(1)}, f32[32,1024]{1,0:T(8,128)S(1)}, u32[]{:S(2)}, u32[]{:S(2)}) collective-permute-start(f32[32,1024]{1,0:T(8,128)S(1)} %get-tuple-element.90), channel_id=1, source_target_pairs={{0,1},{1,0},{2,3},{3,2},{4,5},{5,4},{6,7},{7,6},{8,9},{9,8},{10,11... | collective-permute-start | bytes 393224 | tf_op jit(solution)/shard_map/ppermute | solution.py:524
  66.2 18.9 %copy-start = (bf16[768,256]{1,0:T(8,128)(2,1)S(1)}, bf16[768,256]{1,0:T(8,128)(2,1)}, u32[]{:S(2)}) copy-start(bf16[768,256]{1,0:T(8,128)(2,1)} %constant.118.clone.over_lanes_ref) | copy-start | bytes 1179652
  66.2 18.9 %copy-start.2 = (bf16[128,384]{1,0:T(8,128)(2,1)S(1)}, bf16[128,384]{1,0:T(8,128)(2,1)}, u32[]{:S(2)}) copy-start(bf16[128,384]{1,0:T(8,128)(2,1)} %constant.117.clone.over_rows_ref) | copy-start | bytes 294916
  66.2 18.9 %copy-start.3 = (f32[2,64,128]{2,1,0:T(8,128)S(1)}, f32[2,64,128]{2,1,0:T(8,128)}, u32[]{:S(2)}) copy-start(f32[2,64,128]{2,1,0:T(8,128)} %constant.119.clone.twist_ref) | copy-start | bytes 196612
  66.2 18.9 %copy-start.11 = (s32[16]{0:T(128)S(1)}, s32[16]{0:T(128)}, u32[]{:S(2)}) copy-start(s32[16]{0:T(128)} %halves_ref.1) | copy-start | bytes 196
  66.2 9.2 %collective-permute-start.19 = (f16[128,512]{1,0:T(8,128)(2,1)S(1)}, f16[128,512]{1,0:T(8,128)(2,1)S(1)}, u32[]{:S(2)}, u32[]{:S(2)}) collective-permute-start(f16[128,512]{1,0:T(8,128)(2,1)S(1)} %slice_convert_fusion.3), channel_id=1, source_target_pairs={{0,4},{2,6},{4,0},{6,2},{8,12},{10,14},{12,8},{14,10},{1,5},{3,7},... | collective-permute-start | bytes 393224 | tf_op jit(solution)/shard_map/ppermute | solution.py:412
  68.8 6.7 %collective-permute-start.18 = (f16[64,512]{1,0:T(8,128)(2,1)S(1)}, f16[64,512]{1,0:T(8,128)(2,1)S(1)}, u32[]{:S(2)}, u32[]{:S(2)}) collective-permute-start(f16[64,512]{1,0:T(8,128)(2,1)S(1)} %slice_convert_fusion.9), channel_id=1, source_target_pairs={{0,8},{2,10},{4,12},{6,14},{8,0},{10,2},{12,4},{14,6},{1,9},{3,11}... | collective-permute-start | bytes 196616 | tf_op jit(solution)/shard_map/ppermute | solution.py:412
  73.4 7.8 %collective-permute-start.23 = (f32[32,1024]{1,0:T(8,128)S(1)}, f32[32,1024]{1,0:T(8,128)S(1)}, u32[]{:S(2)}, u32[]{:S(2)}) collective-permute-start(f32[32,1024]{1,0:T(8,128)S(1)} %get-tuple-element.88), channel_id=1, source_target_pairs={{0,1},{1,0},{2,3},{3,2},{4,5},{5,4},{6,7},{7,6},{8,9},{9,8},{10,11... | collective-permute-start | bytes 393224 | tf_op jit(solution)/shard_map/ppermute | solution.py:524
  75.4 5.2 %collective-permute-start.20 = (f16[64,512]{1,0:T(8,128)(2,1)S(1)}, f16[64,512]{1,0:T(8,128)(2,1)S(1)}, u32[]{:S(2)}, u32[]{:S(2)}) collective-permute-start(f16[64,512]{1,0:T(8,128)(2,1)S(1)} %slice_convert_fusion.8), channel_id=1, source_target_pairs={{0,8},{2,10},{4,12},{6,14},{8,0},{10,2},{12,4},{14,6},{1,9},{3,11}... | collective-permute-start | bytes 196616 | tf_op jit(solution)/shard_map/ppermute | solution.py:412
  75.6 5.6 %collective-permute-start.24 = (f32[32,512]{1,0:T(8,128)S(1)}, f32[32,512]{1,0:T(8,128)S(1)}, u32[]{:S(2)}, u32[]{:S(2)}) collective-permute-start(f32[32,512]{1,0:T(8,128)S(1)} %get-tuple-element.96), channel_id=1, source_target_pairs={{0,1},{1,0},{2,3},{3,2},{4,5},{5,4},{6,7},{7,6},{8,9},{9,8},{10,11... | collective-permute-start | bytes 196616 | tf_op jit(solution)/shard_map/ppermute | solution.py:524
  80.7 4.3 %collective-permute-start.25 = (f32[32,512]{1,0:T(8,128)S(1)}, f32[32,512]{1,0:T(8,128)S(1)}, u32[]{:S(2)}, u32[]{:S(2)}) collective-permute-start(f32[32,512]{1,0:T(8,128)S(1)} %get-tuple-element.94), channel_id=1, source_target_pairs={{0,1},{1,0},{2,3},{3,2},{4,5},{5,4},{6,7},{7,6},{8,9},{9,8},{10,11... | collective-permute-start | bytes 196616 | tf_op jit(solution)/shard_map/ppermute | solution.py:524
  85.1 16.3 %copy-start.1 = (bf16[768,256]{1,0:T(8,128)(2,1)S(1)}, bf16[768,256]{1,0:T(8,128)(2,1)}, u32[]{:S(2)}) copy-start(bf16[768,256]{1,0:T(8,128)(2,1)} %constant.121.clone.over_lanes_ref) | copy-start | bytes 1179652
  85.1 16.3 %copy-start.4 = (bf16[384,256]{1,0:T(8,128)(2,1)S(1)}, bf16[384,256]{1,0:T(8,128)(2,1)}, u32[]{:S(2)}) copy-start(bf16[384,256]{1,0:T(8,128)(2,1)} %constant.124.clone.across_ref) | copy-start | bytes 589828
  85.1 16.3 %copy-start.5 = (bf16[128,384]{1,0:T(8,128)(2,1)S(1)}, bf16[128,384]{1,0:T(8,128)(2,1)}, u32[]{:S(2)}) copy-start(bf16[128,384]{1,0:T(8,128)(2,1)} %constant.120.clone.over_rows_ref) | copy-start | bytes 294916
  85.1 16.3 %copy-start.6 = (f32[2,64,128]{2,1,0:T(8,128)S(1)}, f32[2,64,128]{2,1,0:T(8,128)}, u32[]{:S(2)}) copy-start(f32[2,64,128]{2,1,0:T(8,128)} %constant.122.clone.twist_ref) | copy-start | bytes 196612
  85.1 16.3 %copy-start.7 = (bf16[64,192]{1,0:T(8,128)(2,1)S(1)}, bf16[64,192]{1,0:T(8,128)(2,1)}, u32[]{:S(2)}) copy-start(bf16[64,192]{1,0:T(8,128)(2,1)} %constant.123.clone.below_ref) | copy-start | bytes 73732
  87.7 4.8 %collective-permute-start.27 = (f32[2,64,128]{2,1,0:T(8,128)S(1)}, f32[2,64,128]{2,1,0:T(8,128)S(1)}, u32[]{:S(2)}, u32[]{:S(2)}) collective-permute-start(f32[2,64,128]{2,1,0:T(8,128)S(1)} %get-tuple-element.80), channel_id=1, source_target_pairs={{0,1},{1,0},{2,3},{3,2},{4,5},{5,4},{6,7},{7,6},{8,9},{9,8},{10,11... | collective-permute-start | bytes 196616 | tf_op jit(solution)/shard_map/ppermute | solution.py:412
  88.1 4.4 %collective-permute-start.28 = (f32[2,64,128]{2,1,0:T(8,128)S(1)}, f32[2,64,128]{2,1,0:T(8,128)S(1)}, u32[]{:S(2)}, u32[]{:S(2)}) collective-permute-start(f32[2,64,128]{2,1,0:T(8,128)S(1)} %get-tuple-element.80), channel_id=1, source_target_pairs={{0,3},{1,2},{2,1},{3,0},{4,7},{5,6},{6,5},{7,4},{8,11},{9,10},{10,... | collective-permute-start | bytes 196616 | tf_op jit(solution)/shard_map/ppermute | solution.py:426
  88.1 4.4 %collective-permute-start.26 = (f32[2,64,128]{2,1,0:T(8,128)S(1)}, f32[2,64,128]{2,1,0:T(8,128)S(1)}, u32[]{:S(2)}, u32[]{:S(2)}) collective-permute-start(f32[2,64,128]{2,1,0:T(8,128)S(1)} %get-tuple-element.80), channel_id=1, source_target_pairs={{0,2},{2,0},{4,6},{6,4},{8,10},{10,8},{12,14},{14,12},{1,3},{3,1},... | collective-permute-start | bytes 196616 | tf_op jit(solution)/shard_map/ppermute | solution.py:412
  92.5 7.6 %collective-permute-start.30 = (f32[2,64,128]{2,1,0:T(8,128)S(1)}, f32[2,64,128]{2,1,0:T(8,128)S(1)}, u32[]{:S(2)}, u32[]{:S(2)}) collective-permute-start(f32[2,64,128]{2,1,0:T(8,128)S(1)} %add_add_fusion.1), channel_id=1, source_target_pairs={{0,8},{2,10},{4,12},{6,14},{8,0},{10,2},{12,4},{14,6},{1,9},{3,11}... | collective-permute-start | bytes 196616 | tf_op jit(solution)/shard_map/ppermute | solution.py:412
  92.7 7.4 %collective-permute-start.31 = (f32[2,64,128]{2,1,0:T(8,128)S(1)}, f32[2,64,128]{2,1,0:T(8,128)S(1)}, u32[]{:S(2)}, u32[]{:S(2)}) collective-permute-start(f32[2,64,128]{2,1,0:T(8,128)S(1)} %add_add_fusion.1), channel_id=1, source_target_pairs={{0,12},{2,14},{4,8},{6,10},{8,4},{10,6},{12,0},{14,2},{1,13},{3,15... | collective-permute-start | bytes 196616 | tf_op jit(solution)/shard_map/ppermute | solution.py:412
  94.7 6.7 %collective-permute-start.29 = (f32[2,64,128]{2,1,0:T(8,128)S(1)}, f32[2,64,128]{2,1,0:T(8,128)S(1)}, u32[]{:S(2)}, u32[]{:S(2)}) collective-permute-start(f32[2,64,128]{2,1,0:T(8,128)S(1)} %add_add_fusion.1), channel_id=1, source_target_pairs={{0,4},{2,6},{4,0},{6,2},{8,12},{10,14},{12,8},{14,10},{1,5},{3,7},... | collective-permute-start | bytes 196616 | tf_op jit(solution)/shard_map/ppermute | solution.py:412

commit v4 on v3

--- a/solution.py
+++ b/solution.py
@@ -504,12 +504,12 @@
             totals[turn_at], theirs = partial_image(left, steer, *cuts[turn_at])
             moving[turn_at] = swap(theirs, "ping", 1)
             gate = theirs
-        if turn_at == 0:
-            bit = 1
-            while bit < tiles:
+        spread = [1 << at for at in range(tiles.bit_length() - 1)]
+        if turn_at < 2 and turn_at < count:
+            for bit in spread[:-1] if turn_at == 0 else spread[-1:]:
                 known = jnp.maximum(known, tie(swap(known, "rng", bit), gate))
-                bit *= 2
-            gate = known
+            gate = tie(gate, known)
+        if turn_at == 1:
             up, down = scale_of(known, 2.0 * NTAP * steer.shape[2] * pings)
         for stage in STAGES:
             at = turn_at - 1 - stage

time: 106 us -> 104 us (0.981)
  starting transfers between devices: 33.9 us -> 31.6 us
    ppermute x26, starting transfers between devices: 28.1 us -> 26.2 us  [swap(): return lax.ppermute(value, axis, [(at, at ^ bit) for at in range(count)])]
    ppermute x1, waiting for transfers between devices: 0.01 us -> 1.15 us  [total_over(): third = lax.ppermute(value, (axis, other), both)]
  transfers between devices with their start and end apart: 32 -> 32, of which waited for: 12 -> 13; matrix products, arithmetic and copies ran while one was open for 6% -> 6% of each run, Pallas kernels for 27% -> 27%
where the time goes in v4:
time: 104 us; the launch traced here: 103 us
  Pallas kernels  38.9 us (37%)
  starting transfers between devices  31.6 us (30%)
  waiting for transfers between devices  25.3 us (24%)
  other arithmetic  5.72 us (6%)
  between operations  1.2 us (1%)
    ppermute x26, starting transfers between devices, swap(): return lax.ppermute(value, axis, [(at, at ^ bit) for at in range(count)])  26.2 us
    ppermute x26, waiting for transfers between devices, swap(): return lax.ppermute(value, axis, [(at, at ^ bit) for at in range(count)])  21.1 us
    pallas_call x5, Pallas kernels, partial_image(): pl.pallas_call(image_kernel, grid=(cells // tile,), out_shape=(jax.ShapeD...  19 us
    pallas_call x1, Pallas kernels, largest(): pl.pallas_call(largest_kernel, out_shape=jax.ShapeDtypeStruct((3, 8, LANE...  7.9 us
    ppermute x5, starting transfers between devices, on_device(): lax.ppermute(send, 'rng', [(at, (at + step) % tiles) for at in range(tile...  5.46 us
    pallas_call x1, Pallas kernels, focus(): pl.pallas_call(focus_kernel, out_shape=(jax.ShapeDtypeStruct((2, lines, r...  4.08 us
    mul x5, other arithmetic, advance(): (totals[at] + got) * up[0, 0]  4.06 us
    pallas_call x1, Pallas kernels, interpolate(): pl.pallas_call(interp_kernel, grid=(pings // LANES,), out_shape=jax.Shape...  3.87 us
  transfers between devices with their start and end apart: 32, of which 13 were waited for; matrix products, arithmetic and copies ran while one was open for 6% of the time, Pallas kernels for 27%

profile of v4, /device:TPU:0, one launch (start us, length us, event | category | flops | bytes accessed | tf_op | source)
XLA Modules:
  0.0 103.5 jit_solution(2534395551507088022)
XLA Ops:
  0.6 3.0 %collective-permute-start.1 = (bf16[2,1024,128]{2,1,0:T(8,128)(2,1)}, bf16[2,1024,128]{2,1,0:T(8,128)(2,1)S(1)}, u32[]{:S(2)}, u32[]{:S(2)}) collective-permute-start(bf16[2,1024,128]{2,1,0:T(8,128)(2,1)} %echo_ref.1), channel_id=1, source_target_pairs={{0,1},{1,0},{2,3},{3,2},{4,5},{5,4},{6,7},{7,6},{8,9},{9,8},{10,11... | collective-permute-start | bytes 1572872 | tf_op jit(solution)/shard_map/ppermute | solution.py:412
  3.6 7.9 %largest.1 = f32[3,8,128]{2,1,0:T(8,128)} custom-call(bf16[2,1024,128]{2,1,0:T(8,128)(2,1)} %echo_ref.1, f32[4,16]{1,0:T(4,128)} %bitcast.21, bf16[2,4096,1024]{2,1,0:T(8,128)(2,1)} %steer_ref.11), custom_call_target="tpu_custom_call" | custom-call | flops 8388608 | bytes 16777216 | tf_op jit(solution)/shard_map/largest/pallas_call | solution.py:154
  11.5 0.1 collective-permute-start
  11.7 1.3 %collective-permute-done = f32[3,8,128]{2,1,0:T(8,128)S(1)} collective-permute-done((f32[3,8,128]{2,1,0:T(8,128)}, f32[3,8,128]{2,1,0:T(8,128)S(1)}, u32[]{:S(2)}, u32[]{:S(2)}) %collective-permute-start) | collective-permute-done | bytes 12320 | tf_op jit(solution)/shard_map/ppermute | solution.py:412
  13.0 0.7 max.27
  13.7 1.6 %collective-permute-start.2 = (f32[3,8,128]{2,1,0:T(8,128)S(1)}, f32[3,8,128]{2,1,0:T(8,128)S(1)}, u32[]{:S(2)}, u32[]{:S(2)}) collective-permute-start(f32[3,8,128]{2,1,0:T(8,128)S(1)} %max.27), channel_id=1, source_target_pairs={{0,4},{2,6},{4,0},{6,2},{8,12},{10,14},{12,8},{14,10},{1,5},{3,7},... | collective-permute-start | bytes 36872 | tf_op jit(solution)/shard_map/ppermute | solution.py:412
  15.3 2.6 %collective-permute-start.3 = (f32[3,8,128]{2,1,0:T(8,128)S(1)}, f32[3,8,128]{2,1,0:T(8,128)S(1)}, u32[]{:S(2)}, u32[]{:S(2)}) collective-permute-start(f32[3,8,128]{2,1,0:T(8,128)S(1)} %max.27), channel_id=1, source_target_pairs={{0,8},{2,10},{4,12},{6,14},{8,0},{10,2},{12,4},{14,6},{1,9},{3,11}... | collective-permute-start | bytes 36872 | tf_op jit(solution)/shard_map/ppermute | solution.py:412
  17.9 0.2 collective-permute-start.4
  18.1 0.1 broadcast_select_fusion.1
  18.2 0.1 pad_maximum_fusion.echo_ref
  18.3 3.9 %interp.1.left_ref = bf16[2,512,1024]{2,1,0:T(8,128)(2,1)S(1)} custom-call(s32[16]{0:T(128)S(1)} %fusion.11.starts_ref, s32[16]{0:T(128)S(1)} %copy-done.9, f32[4,16]{1,0:T(4,128)S(1)} %bitcast.22, bf16[2,1024,256]{2,1,0:T(8,128)(2,1)S(1)} %pad_maximum_fusion.echo_ref), custom_call_target="tpu_custom_call" | custom-call | flops 4194304 | bytes 3145728 | tf_op jit(solution)/shard_map/interp/pallas_call | solution.py:115
  22.2 1.1 %collective-permute-done.4 = f32[3,8,128]{2,1,0:T(8,128)S(1)} collective-permute-done((f32[3,8,128]{2,1,0:T(8,128)S(1)}, f32[3,8,128]{2,1,0:T(8,128)S(1)}, u32[]{:S(2)}, u32[]{:S(2)}) %collective-permute-start.4) | collective-permute-done | bytes 12320 | tf_op jit(solution)/shard_map/ppermute | solution.py:412
  23.4 4.3 %image.6 = (f32[256,1024]{1,0:T(8,128)S(1)}, f32[256,1024]{1,0:T(8,128)S(1)}) custom-call(bf16[2,512,1024]{2,1,0:T(8,128)(2,1)S(1)} %interp.1.left_ref, bf16[2,4096,1024]{2,1,0:T(8,128)(2,1)} %steer_ref.11), custom_call_target="tpu_custom_call" | custom-call | flops 2147483648 | bytes 6291456 | tf_op jit(solution)/shard_map/image/pallas_call | solution.py:182
  27.7 0.1 collective-permute-start.6
  27.9 0.6 collective-permute-start.5
  28.5 4.3 %image.5 = (f32[256,1024]{1,0:T(8,128)S(1)}, f32[256,1024]{1,0:T(8,128)S(1)}) custom-call(bf16[2,512,1024]{2,1,0:T(8,128)(2,1)S(1)} %interp.1.left_ref, bf16[2,4096,1024]{2,1,0:T(8,128)(2,1)} %steer_ref.11), custom_call_target="tpu_custom_call" | custom-call | flops 2147483648 | bytes 6291456 | tf_op jit(solution)/shard_map/image/pallas_call | solution.py:182
  32.8 0.3 collective-permute-start.8
  33.1 0.5 slice.119
  33.7 0.9 add_multiply_fusion.2
  34.6 0.1 collective-permute-start.7
  34.7 4.5 %image.7 = (f32[256,1024]{1,0:T(8,128)S(1)}, f32[256,1024]{1,0:T(8,128)S(1)}) custom-call(bf16[2,512,1024]{2,1,0:T(8,128)(2,1)S(1)} %interp.1.left_ref, bf16[2,4096,1024]{2,1,0:T(8,128)(2,1)} %steer_ref.11), custom_call_target="tpu_custom_call" | custom-call | flops 2147483648 | bytes 6291456 | tf_op jit(solution)/shard_map/image/pallas_call | solution.py:182
  39.2 0.4 collective-permute-start.11
  39.6 0.9 add_multiply_fusion.1
  40.5 1.8 %collective-permute-start.10 = (f16[128,1024]{1,0:T(8,128)(2,1)S(1)}, f16[128,1024]{1,0:T(8,128)(2,1)S(1)}, u32[]{:S(2)}, u32[]{:S(2)}) collective-permute-start(f16[128,1024]{1,0:T(8,128)(2,1)S(1)} %slice_convert_fusion.1), channel_id=1, source_target_pairs={{0,4},{2,6},{4,0},{6,2},{8,12},{10,14},{12,8},{14,10},{1,5},{3,7},... | collective-permute-start | bytes 786440 | tf_op jit(solution)/shard_map/ppermute | solution.py:412
  42.3 0.9 collective-permute-done.7
  43.2 0.1 slice_add_fusion.2
  43.3 1.4 %collective-permute-start.9 = (f16[64,1024]{1,0:T(8,128)(2,1)S(1)}, f16[64,1024]{1,0:T(8,128)(2,1)S(1)}, u32[]{:S(2)}, u32[]{:S(2)}) collective-permute-start(f16[64,1024]{1,0:T(8,128)(2,1)S(1)} %slice_convert_fusion.7), channel_id=1, source_target_pairs={{0,8},{2,10},{4,12},{6,14},{8,0},{10,2},{12,4},{14,6},{1,9},{3,11}... | collective-permute-start | bytes 393224 | tf_op jit(solution)/shard_map/ppermute | solution.py:412
  44.6 2.9 %image.8 = (f32[256,512]{1,0:T(8,128)S(1)}, f32[256,512]{1,0:T(8,128)S(1)}) custom-call(bf16[2,512,1024]{2,1,0:T(8,128)(2,1)S(1)} %interp.1.left_ref, bf16[2,4096,1024]{2,1,0:T(8,128)(2,1)} %steer_ref.11), custom_call_target="tpu_custom_call" | custom-call | flops 1073741824 | bytes 3145728 | tf_op jit(solution)/shard_map/image/pallas_call | solution.py:182
  47.5 0.1 collective-permute-start.14
  47.6 0.9 add_multiply_fusion
  48.5 1.8 %collective-permute-start.13 = (f16[128,1024]{1,0:T(8,128)(2,1)S(1)}, f16[128,1024]{1,0:T(8,128)(2,1)S(1)}, u32[]{:S(2)}, u32[]{:S(2)}) collective-permute-start(f16[128,1024]{1,0:T(8,128)(2,1)S(1)} %slice_convert_fusion), channel_id=1, source_target_pairs={{0,4},{2,6},{4,0},{6,2},{8,12},{10,14},{12,8},{14,10},{1,5},{3,7},... | collective-permute-start | bytes 786440 | tf_op jit(solution)/shard_map/ppermute | solution.py:412
  50.3 2.0 %collective-permute-done.10 = f16[128,1024]{1,0:T(8,128)(2,1)S(1)} collective-permute-done((f16[128,1024]{1,0:T(8,128)(2,1)S(1)}, f16[128,1024]{1,0:T(8,128)(2,1)S(1)}, u32[]{:S(2)}, u32[]{:S(2)}) %collective-permute-start.10) | collective-permute-done | bytes 262176 | tf_op jit(solution)/shard_map/ppermute | solution.py:412
  52.4 0.8 collective-permute-start.12
  53.2 2.9 %image.9 = (f32[256,512]{1,0:T(8,128)S(1)}, f32[256,512]{1,0:T(8,128)S(1)}) custom-call(bf16[2,512,1024]{2,1,0:T(8,128)(2,1)S(1)} %interp.1.left_ref, bf16[2,4096,1024]{2,1,0:T(8,128)(2,1)} %steer_ref.11), custom_call_target="tpu_custom_call" | custom-call | flops 1073741824 | bytes 3145728 | tf_op jit(solution)/shard_map/image/pallas_call | solution.py:182
  56.1 0.1 collective-permute-start.17
  56.2 0.7 add_multiply_fusion.4
  57.0 2.5 %collective-permute-start.16 = (f16[128,512]{1,0:T(8,128)(2,1)S(1)}, f16[128,512]{1,0:T(8,128)(2,1)S(1)}, u32[]{:S(2)}, u32[]{:S(2)}) collective-permute-start(f16[128,512]{1,0:T(8,128)(2,1)S(1)} %slice_convert_fusion.5), channel_id=1, source_target_pairs={{0,4},{2,6},{4,0},{6,2},{8,12},{10,14},{12,8},{14,10},{1,5},{3,7},... | collective-permute-start | bytes 393224 | tf_op jit(solution)/shard_map/ppermute | solution.py:412
  59.5 1.6 %collective-permute-start.21 = (f32[32,1024]{1,0:T(8,128)S(1)}, f32[32,1024]{1,0:T(8,128)S(1)}, u32[]{:S(2)}, u32[]{:S(2)}) collective-permute-start(f32[32,1024]{1,0:T(8,128)S(1)} %get-tuple-element.88), channel_id=1, source_target_pairs={{0,1},{1,0},{2,3},{3,2},{4,5},{5,4},{6,7},{7,6},{8,9},{9,8},{10,11... | collective-permute-start | bytes 393224 | tf_op jit(solution)/shard_map/ppermute | solution.py:524
  61.2 0.4 collective-permute-start.15
  61.7 1.6 %collective-permute-start.22 = (f32[32,1024]{1,0:T(8,128)S(1)}, f32[32,1024]{1,0:T(8,128)S(1)}, u32[]{:S(2)}, u32[]{:S(2)}) collective-permute-start(f32[32,1024]{1,0:T(8,128)S(1)} %get-tuple-element.86), channel_id=1, source_target_pairs={{0,1},{1,0},{2,3},{3,2},{4,5},{5,4},{6,7},{7,6},{8,9},{9,8},{10,11... | collective-permute-start | bytes 393224 | tf_op jit(solution)/shard_map/ppermute | solution.py:524
  63.2 0.7 add_multiply_fusion.3
  64.1 2.5 %collective-permute-start.19 = (f16[128,512]{1,0:T(8,128)(2,1)S(1)}, f16[128,512]{1,0:T(8,128)(2,1)S(1)}, u32[]{:S(2)}, u32[]{:S(2)}) collective-permute-start(f16[128,512]{1,0:T(8,128)(2,1)S(1)} %slice_convert_fusion.3), channel_id=1, source_target_pairs={{0,4},{2,6},{4,0},{6,2},{8,12},{10,14},{12,8},{14,10},{1,5},{3,7},... | collective-permute-start | bytes 393224 | tf_op jit(solution)/shard_map/ppermute | solution.py:412
  66.7 0.1 collective-permute-start.18
  66.8 5.0 %collective-permute-done.15 = f16[64,1024]{1,0:T(8,128)(2,1)S(1)} collective-permute-done((f16[64,1024]{1,0:T(8,128)(2,1)S(1)}, f16[64,1024]{1,0:T(8,128)(2,1)S(1)}, u32[]{:S(2)}, u32[]{:S(2)}) %collective-permute-start.15) | collective-permute-done | bytes 131104 | tf_op jit(solution)/shard_map/ppermute | solution.py:412
  71.8 0.1 collective-permute-start.23
  71.9 0.4 collective-permute-done.19
  72.4 0.2 collective-permute-start.20
  72.5 0.7 collective-permute-done.18
  73.2 1.0 collective-permute-start.24
  74.2 3.8 %collective-permute-done.20 = f16[64,512]{1,0:T(8,128)(2,1)S(1)} collective-permute-done((f16[64,512]{1,0:T(8,128)(2,1)S(1)}, f16[64,512]{1,0:T(8,128)(2,1)S(1)}, u32[]{:S(2)}, u32[]{:S(2)}) %collective-permute-start.20) | collective-permute-done | bytes 65568 | tf_op jit(solution)/shard_map/ppermute | solution.py:412
  78.1 1.3 %collective-permute-start.25 = (f32[32,512]{1,0:T(8,128)S(1)}, f32[32,512]{1,0:T(8,128)S(1)}, u32[]{:S(2)}, u32[]{:S(2)}) collective-permute-start(f32[32,512]{1,0:T(8,128)S(1)} %get-tuple-element.90), channel_id=1, source_target_pairs={{0,1},{1,0},{2,3},{3,2},{4,5},{5,4},{6,7},{7,6},{8,9},{9,8},{10,11... | collective-permute-start | bytes 196616 | tf_op jit(solution)/shard_map/ppermute | solution.py:524
  79.4 3.0 %collective-permute-done.25 = f32[32,512]{1,0:T(8,128)S(1)} collective-permute-done((f32[32,512]{1,0:T(8,128)S(1)}, f32[32,512]{1,0:T(8,128)S(1)}, u32[]{:S(2)}, u32[]{:S(2)}) %collective-permute-start.25) | collective-permute-done | bytes 65568 | tf_op jit(solution)/shard_map/ppermute | solution.py:524
  82.5 2.5 %gradient.1 = (f32[2,1024,128]{2,1,0:T(8,128)S(1)}, f32[2,64,128]{2,1,0:T(8,128)S(1)}) custom-call(s32[2]{0:T(128)S(1)} %and_select_fusion.5.tile_ref, s32[16]{0:T(128)S(1)} %copy-done.10, s32[16]{0:T(128)S(1)} %copy-done.11, f32[2,16]{1,0:T(2,128)S(1)} %pad_maximum_fusion.1.turn_ref, f32[8,128]{1,0:T(8,128)S(1)} %get-tuple-element.48.down_ref, ...), custom_call_target="tpu_custom_call" | custom-call | flops 314572800 | bytes 2097152 | tf_op jit(solution)/shard_map/gradient/pallas_call | solution.py:289
  85.0 1.3 %collective-permute-start.27 = (f32[2,64,128]{2,1,0:T(8,128)S(1)}, f32[2,64,128]{2,1,0:T(8,128)S(1)}, u32[]{:S(2)}, u32[]{:S(2)}) collective-permute-start(f32[2,64,128]{2,1,0:T(8,128)S(1)} %get-tuple-element.76), channel_id=1, source_target_pairs={{0,1},{1,0},{2,3},{3,2},{4,5},{5,4},{6,7},{7,6},{8,9},{9,8},{10,11... | collective-permute-start | bytes 196616 | tf_op jit(solution)/shard_map/ppermute | solution.py:412
  86.3 0.9 collective-permute-start.26
  87.2 2.2 %collective-permute-done.27 = f32[2,64,128]{2,1,0:T(8,128)S(1)} collective-permute-done((f32[2,64,128]{2,1,0:T(8,128)S(1)}, f32[2,64,128]{2,1,0:T(8,128)S(1)}, u32[]{:S(2)}, u32[]{:S(2)}) %collective-permute-start.27) | collective-permute-done | bytes 65568 | tf_op jit(solution)/shard_map/ppermute | solution.py:412
  89.5 1.1 %collective-permute-done.28 = f32[2,64,128]{2,1,0:T(8,128)S(1)} collective-permute-done((f32[2,64,128]{2,1,0:T(8,128)S(1)}, f32[2,64,128]{2,1,0:T(8,128)S(1)}, u32[]{:S(2)}, u32[]{:S(2)}) %collective-permute-start.28) | collective-permute-done | bytes 65568 | tf_op jit(solution)/shard_map/ppermute | solution.py:426
  90.6 0.1 collective-permute-start.30
  90.7 1.8 %collective-permute-start.31 = (f32[2,64,128]{2,1,0:T(8,128)S(1)}, f32[2,64,128]{2,1,0:T(8,128)S(1)}, u32[]{:S(2)}, u32[]{:S(2)}) collective-permute-start(f32[2,64,128]{2,1,0:T(8,128)S(1)} %add_add_fusion.1), channel_id=1, source_target_pairs={{0,12},{2,14},{4,8},{6,10},{8,4},{10,6},{12,0},{14,2},{1,13},{3,15... | collective-permute-start | bytes 196616 | tf_op jit(solution)/shard_map/ppermute | solution.py:412
  92.5 1.7 %collective-permute-start.29 = (f32[2,64,128]{2,1,0:T(8,128)S(1)}, f32[2,64,128]{2,1,0:T(8,128)S(1)}, u32[]{:S(2)}, u32[]{:S(2)}) collective-permute-start(f32[2,64,128]{2,1,0:T(8,128)S(1)} %add_add_fusion.1), channel_id=1, source_target_pairs={{0,4},{2,6},{4,0},{6,2},{8,12},{10,14},{12,8},{14,10},{1,5},{3,7},... | collective-permute-start | bytes 196616 | tf_op jit(solution)/shard_map/ppermute | solution.py:412
  94.2 1.6 %spectrum.1.bins_ref = f32[1024,256]{1,0:T(8,128)S(1)} custom-call(bf16[128,384]{1,0:T(8,128)(2,1)S(1)} %copy-done.2, bf16[768,256]{1,0:T(8,128)(2,1)S(1)} %copy-done, f32[2,64,128]{2,1,0:T(8,128)S(1)} %copy-done.3, f32[2,1024,128]{2,1,0:T(8,128)S(1)} %get-tuple-element.77.grid_ref), custom_call_target="tpu_custom_call" | custom-call | flops 314572800 | bytes 2097152 | tf_op jit(solution)/shard_map/spectrum/pallas_call | solution.py:316
  95.8 2.3 %collective-permute-done.30 = f32[2,64,128]{2,1,0:T(8,128)S(1)} collective-permute-done((f32[2,64,128]{2,1,0:T(8,128)S(1)}, f32[2,64,128]{2,1,0:T(8,128)S(1)}, u32[]{:S(2)}, u32[]{:S(2)}) %collective-permute-start.30) | collective-permute-done | bytes 65568 | tf_op jit(solution)/shard_map/ppermute | solution.py:412
  98.1 1.3 %collective-permute-done.29 = f32[2,64,128]{2,1,0:T(8,128)S(1)} collective-permute-done((f32[2,64,128]{2,1,0:T(8,128)S(1)}, f32[2,64,128]{2,1,0:T(8,128)S(1)}, u32[]{:S(2)}, u32[]{:S(2)}) %collective-permute-start.29) | collective-permute-done | bytes 65568 | tf_op jit(solution)/shard_map/ppermute | solution.py:412
  99.4 4.1 %focus.1 = (f32[2,16,8192]{2,1,0:T(8,128)}, f32[64,128]{1,0:T(8,128)}) custom-call(bf16[128,384]{1,0:T(8,128)(2,1)S(1)} %copy-done.5, bf16[768,256]{1,0:T(8,128)(2,1)S(1)} %copy-done.1, f32[2,64,128]{2,1,0:T(8,128)S(1)} %copy-done.6, bf16[64,192]{1,0:T(8,128)(2,1)S(1)} %copy-done.7, bf16[384,256]{1,0:T(8,128)(2,1)S(1)} %copy-done.4, ...), custom_call_target="tpu_custom_call" | custom-call | flops 314572800 | bytes 2097152 | tf_op jit(solution)/shard_map/focus/pallas_call | solution.py:393
  (80 shorter events, 0.9 us)
Async XLA Ops:
  0.6 17.5 %collective-permute-start.1 = (bf16[2,1024,128]{2,1,0:T(8,128)(2,1)}, bf16[2,1024,128]{2,1,0:T(8,128)(2,1)S(1)}, u32[]{:S(2)}, u32[]{:S(2)}) collective-permute-start(bf16[2,1024,128]{2,1,0:T(8,128)(2,1)} %echo_ref.1), channel_id=1, source_target_pairs={{0,1},{1,0},{2,3},{3,2},{4,5},{5,4},{6,7},{7,6},{8,9},{9,8},{10,11... | collective-permute-start | bytes 1572872 | tf_op jit(solution)/shard_map/ppermute | solution.py:412
  3.6 14.5 %copy-start.12 = (bf16[2,1024,128]{2,1,0:T(8,128)(2,1)S(1)}, bf16[2,1024,128]{2,1,0:T(8,128)(2,1)}, u32[]{:S(2)}) copy-start(bf16[2,1024,128]{2,1,0:T(8,128)(2,1)} %echo_ref.1) | copy-start | bytes 1572868
  11.5 1.5 %collective-permute-start = (f32[3,8,128]{2,1,0:T(8,128)}, f32[3,8,128]{2,1,0:T(8,128)S(1)}, u32[]{:S(2)}, u32[]{:S(2)}) collective-permute-start(f32[3,8,128]{2,1,0:T(8,128)} %largest.1), channel_id=1, source_target_pairs={{0,2},{2,0},{4,6},{6,4},{8,10},{10,8},{12,14},{14,12},{1,3},{3,1},... | collective-permute-start | bytes 36872 | tf_op jit(solution)/shard_map/ppermute | solution.py:412
  13.7 4.6 %copy-start.8 = (f32[16,4]{0,1:T(4,128)S(1)}, f32[16,4]{0,1:T(4,128)}, u32[]{:S(2)}) copy-start(f32[16,4]{0,1:T(4,128)} %param.17) | copy-start | bytes 772
  13.7 4.6 %copy-start.9 = (s32[16]{0:T(128)S(1)}, s32[16]{0:T(128)}, u32[]{:S(2)}) copy-start(s32[16]{0:T(128)} %offsets_ref.1) | copy-start | bytes 196
  13.7 8.5 %collective-permute-start.2 = (f32[3,8,128]{2,1,0:T(8,128)S(1)}, f32[3,8,128]{2,1,0:T(8,128)S(1)}, u32[]{:S(2)}, u32[]{:S(2)}) collective-permute-start(f32[3,8,128]{2,1,0:T(8,128)S(1)} %max.27), channel_id=1, source_target_pairs={{0,4},{2,6},{4,0},{6,2},{8,12},{10,14},{12,8},{14,10},{1,5},{3,7},... | collective-permute-start | bytes 36872 | tf_op jit(solution)/shard_map/ppermute | solution.py:412
  15.3 6.9 %collective-permute-start.3 = (f32[3,8,128]{2,1,0:T(8,128)S(1)}, f32[3,8,128]{2,1,0:T(8,128)S(1)}, u32[]{:S(2)}, u32[]{:S(2)}) collective-permute-start(f32[3,8,128]{2,1,0:T(8,128)S(1)} %max.27), channel_id=1, source_target_pairs={{0,8},{2,10},{4,12},{6,14},{8,0},{10,2},{12,4},{14,6},{1,9},{3,11}... | collective-permute-start | bytes 36872 | tf_op jit(solution)/shard_map/ppermute | solution.py:412
  17.9 5.5 %collective-permute-start.4 = (f32[3,8,128]{2,1,0:T(8,128)S(1)}, f32[3,8,128]{2,1,0:T(8,128)S(1)}, u32[]{:S(2)}, u32[]{:S(2)}) collective-permute-start(f32[3,8,128]{2,1,0:T(8,128)S(1)} %max.27), channel_id=1, source_target_pairs={{0,12},{2,14},{4,8},{6,10},{8,4},{10,6},{12,0},{14,2},{1,13},{3,15... | collective-permute-start | bytes 36872 | tf_op jit(solution)/shard_map/ppermute | solution.py:412
  23.4 4.4 %copy-start.10 = (s32[16]{0:T(128)S(1)}, s32[16]{0:T(128)}, u32[]{:S(2)}) copy-start(s32[16]{0:T(128)} %centers_ref.1) | copy-start | bytes 196
  27.7 5.9 %collective-permute-start.6 = (f32[256,1024]{1,0:T(8,128)S(1)}, f32[256,1024]{1,0:T(8,128)S(1)}, u32[]{:S(2)}, u32[]{:S(2)}) collective-permute-start(f32[256,1024]{1,0:T(8,128)S(1)} %get-tuple-element.50), channel_id=1, source_target_pairs={{0,2},{2,0},{4,6},{6,4},{8,10},{10,8},{12,14},{14,12},{1,3},{3,1},... | collective-permute-start | bytes 3145736 | tf_op jit(solution)/shard_map/ppermute | solution.py:412
  27.9 5.2 %collective-permute-start.5 = (f32[3,8,128]{2,1,0:T(8,128)S(1)}, f32[3,8,128]{2,1,0:T(8,128)S(1)}, u32[]{:S(2)}, u32[]{:S(2)}) collective-permute-start(f32[3,8,128]{2,1,0:T(8,128)S(1)} %maximum_maximum_fusion), channel_id=1, source_target_pairs={{0,1},{1,0},{2,3},{3,2},{4,5},{5,4},{6,7},{7,6},{8,9},{9,8},{10,11... | collective-permute-start | bytes 36872 | tf_op jit(solution)/shard_map/ppermute | solution.py:412
  32.8 6.8 %collective-permute-start.8 = (f32[256,1024]{1,0:T(8,128)S(1)}, f32[256,1024]{1,0:T(8,128)S(1)}, u32[]{:S(2)}, u32[]{:S(2)}) collective-permute-start(f32[256,1024]{1,0:T(8,128)S(1)} %get-tuple-element.46), channel_id=1, source_target_pairs={{0,2},{2,0},{4,6},{6,4},{8,10},{10,8},{12,14},{14,12},{1,3},{3,1},... | collective-permute-start | bytes 3145736 | tf_op jit(solution)/shard_map/ppermute | solution.py:412
  34.6 8.6 %collective-permute-start.7 = (f16[128,1024]{1,0:T(8,128)(2,1)S(1)}, f16[128,1024]{1,0:T(8,128)(2,1)S(1)}, u32[]{:S(2)}, u32[]{:S(2)}) collective-permute-start(f16[128,1024]{1,0:T(8,128)(2,1)S(1)} %slice_convert_fusion.2), channel_id=1, source_target_pairs={{0,4},{2,6},{4,0},{6,2},{8,12},{10,14},{12,8},{14,10},{1,5},{3,7},... | collective-permute-start | bytes 786440 | tf_op jit(solution)/shard_map/ppermute | solution.py:412
  39.2 8.4 %collective-permute-start.11 = (f32[256,1024]{1,0:T(8,128)S(1)}, f32[256,1024]{1,0:T(8,128)S(1)}, u32[]{:S(2)}, u32[]{:S(2)}) collective-permute-start(f32[256,1024]{1,0:T(8,128)S(1)} %get-tuple-element.54), channel_id=1, source_target_pairs={{0,2},{2,0},{4,6},{6,4},{8,10},{10,8},{12,14},{14,12},{1,3},{3,1},... | collective-permute-start | bytes 3145736 | tf_op jit(solution)/shard_map/ppermute | solution.py:412
  40.5 11.9 %collective-permute-start.10 = (f16[128,1024]{1,0:T(8,128)(2,1)S(1)}, f16[128,1024]{1,0:T(8,128)(2,1)S(1)}, u32[]{:S(2)}, u32[]{:S(2)}) collective-permute-start(f16[128,1024]{1,0:T(8,128)(2,1)S(1)} %slice_convert_fusion.1), channel_id=1, source_target_pairs={{0,4},{2,6},{4,0},{6,2},{8,12},{10,14},{12,8},{14,10},{1,5},{3,7},... | collective-permute-start | bytes 786440 | tf_op jit(solution)/shard_map/ppermute | solution.py:412
  43.3 9.9 %collective-permute-start.9 = (f16[64,1024]{1,0:T(8,128)(2,1)S(1)}, f16[64,1024]{1,0:T(8,128)(2,1)S(1)}, u32[]{:S(2)}, u32[]{:S(2)}) collective-permute-start(f16[64,1024]{1,0:T(8,128)(2,1)S(1)} %slice_convert_fusion.7), channel_id=1, source_target_pairs={{0,8},{2,10},{4,12},{6,14},{8,0},{10,2},{12,4},{14,6},{1,9},{3,11}... | collective-permute-start | bytes 393224 | tf_op jit(solution)/shard_map/ppermute | solution.py:412
  47.5 8.7 %collective-permute-start.14 = (f32[256,512]{1,0:T(8,128)S(1)}, f32[256,512]{1,0:T(8,128)S(1)}, u32[]{:S(2)}, u32[]{:S(2)}) collective-permute-start(f32[256,512]{1,0:T(8,128)S(1)} %get-tuple-element.59), channel_id=1, source_target_pairs={{0,2},{2,0},{4,6},{6,4},{8,10},{10,8},{12,14},{14,12},{1,3},{3,1},... | collective-permute-start | bytes 1572872 | tf_op jit(solution)/shard_map/ppermute | solution.py:412
  48.5 12.6 %collective-permute-start.13 = (f16[128,1024]{1,0:T(8,128)(2,1)S(1)}, f16[128,1024]{1,0:T(8,128)(2,1)S(1)}, u32[]{:S(2)}, u32[]{:S(2)}) collective-permute-start(f16[128,1024]{1,0:T(8,128)(2,1)S(1)} %slice_convert_fusion), channel_id=1, source_target_pairs={{0,4},{2,6},{4,0},{6,2},{8,12},{10,14},{12,8},{14,10},{1,5},{3,7},... | collective-permute-start | bytes 786440 | tf_op jit(solution)/shard_map/ppermute | solution.py:412
  52.4 9.2 %collective-permute-start.12 = (f16[64,1024]{1,0:T(8,128)(2,1)S(1)}, f16[64,1024]{1,0:T(8,128)(2,1)S(1)}, u32[]{:S(2)}, u32[]{:S(2)}) collective-permute-start(f16[64,1024]{1,0:T(8,128)(2,1)S(1)} %slice_convert_fusion.6), channel_id=1, source_target_pairs={{0,8},{2,10},{4,12},{6,14},{8,0},{10,2},{12,4},{14,6},{1,9},{3,11}... | collective-permute-start | bytes 393224 | tf_op jit(solution)/shard_map/ppermute | solution.py:412
  56.1 7.1 %collective-permute-start.17 = (f32[256,512]{1,0:T(8,128)S(1)}, f32[256,512]{1,0:T(8,128)S(1)}, u32[]{:S(2)}, u32[]{:S(2)}) collective-permute-start(f32[256,512]{1,0:T(8,128)S(1)} %get-tuple-element.65), channel_id=1, source_target_pairs={{0,2},{2,0},{4,6},{6,4},{8,10},{10,8},{12,14},{14,12},{1,3},{3,1},... | collective-permute-start | bytes 1572872 | tf_op jit(solution)/shard_map/ppermute | solution.py:412
  57.0 9.6 %collective-permute-start.16 = (f16[128,512]{1,0:T(8,128)(2,1)S(1)}, f16[128,512]{1,0:T(8,128)(2,1)S(1)}, u32[]{:S(2)}, u32[]{:S(2)}) collective-permute-start(f16[128,512]{1,0:T(8,128)(2,1)S(1)} %slice_convert_fusion.5), channel_id=1, source_target_pairs={{0,4},{2,6},{4,0},{6,2},{8,12},{10,14},{12,8},{14,10},{1,5},{3,7},... | collective-permute-start | bytes 393224 | tf_op jit(solution)/shard_map/ppermute | solution.py:412
  59.5 19.8 %collective-permute-start.21 = (f32[32,1024]{1,0:T(8,128)S(1)}, f32[32,1024]{1,0:T(8,128)S(1)}, u32[]{:S(2)}, u32[]{:S(2)}) collective-permute-start(f32[32,1024]{1,0:T(8,128)S(1)} %get-tuple-element.88), channel_id=1, source_target_pairs={{0,1},{1,0},{2,3},{3,2},{4,5},{5,4},{6,7},{7,6},{8,9},{9,8},{10,11... | collective-permute-start | bytes 393224 | tf_op jit(solution)/shard_map/ppermute | solution.py:524
  61.2 10.6 %collective-permute-start.15 = (f16[64,1024]{1,0:T(8,128)(2,1)S(1)}, f16[64,1024]{1,0:T(8,128)(2,1)S(1)}, u32[]{:S(2)}, u32[]{:S(2)}) collective-permute-start(f16[64,1024]{1,0:T(8,128)(2,1)S(1)} %slice_convert_fusion.4), channel_id=1, source_target_pairs={{0,8},{2,10},{4,12},{6,14},{8,0},{10,2},{12,4},{14,6},{1,9},{3,11}... | collective-permute-start | bytes 393224 | tf_op jit(solution)/shard_map/ppermute | solution.py:412
  61.7 17.6 %collective-permute-start.22 = (f32[32,1024]{1,0:T(8,128)S(1)}, f32[32,1024]{1,0:T(8,128)S(1)}, u32[]{:S(2)}, u32[]{:S(2)}) collective-permute-start(f32[32,1024]{1,0:T(8,128)S(1)} %get-tuple-element.86), channel_id=1, source_target_pairs={{0,1},{1,0},{2,3},{3,2},{4,5},{5,4},{6,7},{7,6},{8,9},{9,8},{10,11... | collective-permute-start | bytes 393224 | tf_op jit(solution)/shard_map/ppermute | solution.py:524
  64.0 18.4 %copy-start = (bf16[768,256]{1,0:T(8,128)(2,1)S(1)}, bf16[768,256]{1,0:T(8,128)(2,1)}, u32[]{:S(2)}) copy-start(bf16[768,256]{1,0:T(8,128)(2,1)} %constant.118.clone.over_lanes_ref) | copy-start | bytes 1179652
  64.0 18.4 %copy-start.2 = (bf16[128,384]{1,0:T(8,128)(2,1)S(1)}, bf16[128,384]{1,0:T(8,128)(2,1)}, u32[]{:S(2)}) copy-start(bf16[128,384]{1,0:T(8,128)(2,1)} %constant.117.clone.over_rows_ref) | copy-start | bytes 294916
  64.0 18.4 %copy-start.3 = (f32[2,64,128]{2,1,0:T(8,128)S(1)}, f32[2,64,128]{2,1,0:T(8,128)}, u32[]{:S(2)}) copy-start(f32[2,64,128]{2,1,0:T(8,128)} %constant.119.clone.twist_ref) | copy-start | bytes 196612
  64.1 18.3 %copy-start.11 = (s32[16]{0:T(128)S(1)}, s32[16]{0:T(128)}, u32[]{:S(2)}) copy-start(s32[16]{0:T(128)} %halves_ref.1) | copy-start | bytes 196
  64.1 8.2 %collective-permute-start.19 = (f16[128,512]{1,0:T(8,128)(2,1)S(1)}, f16[128,512]{1,0:T(8,128)(2,1)S(1)}, u32[]{:S(2)}, u32[]{:S(2)}) collective-permute-start(f16[128,512]{1,0:T(8,128)(2,1)S(1)} %slice_convert_fusion.3), channel_id=1, source_target_pairs={{0,4},{2,6},{4,0},{6,2},{8,12},{10,14},{12,8},{14,10},{1,5},{3,7},... | collective-permute-start | bytes 393224 | tf_op jit(solution)/shard_map/ppermute | solution.py:412
  66.7 6.5 %collective-permute-start.18 = (f16[64,512]{1,0:T(8,128)(2,1)S(1)}, f16[64,512]{1,0:T(8,128)(2,1)S(1)}, u32[]{:S(2)}, u32[]{:S(2)}) collective-permute-start(f16[64,512]{1,0:T(8,128)(2,1)S(1)} %slice_convert_fusion.9), channel_id=1, source_target_pairs={{0,8},{2,10},{4,12},{6,14},{8,0},{10,2},{12,4},{14,6},{1,9},{3,11}... | collective-permute-start | bytes 196616 | tf_op jit(solution)/shard_map/ppermute | solution.py:412
  71.8 7.5 %collective-permute-start.23 = (f32[32,1024]{1,0:T(8,128)S(1)}, f32[32,1024]{1,0:T(8,128)S(1)}, u32[]{:S(2)}, u32[]{:S(2)}) collective-permute-start(f32[32,1024]{1,0:T(8,128)S(1)} %get-tuple-element.84), channel_id=1, source_target_pairs={{0,1},{1,0},{2,3},{3,2},{4,5},{5,4},{6,7},{7,6},{8,9},{9,8},{10,11... | collective-permute-start | bytes 393224 | tf_op jit(solution)/shard_map/ppermute | solution.py:524
  72.4 5.7 %collective-permute-start.20 = (f16[64,512]{1,0:T(8,128)(2,1)S(1)}, f16[64,512]{1,0:T(8,128)(2,1)S(1)}, u32[]{:S(2)}, u32[]{:S(2)}) collective-permute-start(f16[64,512]{1,0:T(8,128)(2,1)S(1)} %slice_convert_fusion.8), channel_id=1, source_target_pairs={{0,8},{2,10},{4,12},{6,14},{8,0},{10,2},{12,4},{14,6},{1,9},{3,11}... | collective-permute-start | bytes 196616 | tf_op jit(solution)/shard_map/ppermute | solution.py:412
  73.2 6.1 %collective-permute-start.24 = (f32[32,512]{1,0:T(8,128)S(1)}, f32[32,512]{1,0:T(8,128)S(1)}, u32[]{:S(2)}, u32[]{:S(2)}) collective-permute-start(f32[32,512]{1,0:T(8,128)S(1)} %get-tuple-element.92), channel_id=1, source_target_pairs={{0,1},{1,0},{2,3},{3,2},{4,5},{5,4},{6,7},{7,6},{8,9},{9,8},{10,11... | collective-permute-start | bytes 196616 | tf_op jit(solution)/shard_map/ppermute | solution.py:524
  78.1 4.3 %collective-permute-start.25 = (f32[32,512]{1,0:T(8,128)S(1)}, f32[32,512]{1,0:T(8,128)S(1)}, u32[]{:S(2)}, u32[]{:S(2)}) collective-permute-start(f32[32,512]{1,0:T(8,128)S(1)} %get-tuple-element.90), channel_id=1, source_target_pairs={{0,1},{1,0},{2,3},{3,2},{4,5},{5,4},{6,7},{7,6},{8,9},{9,8},{10,11... | collective-permute-start | bytes 196616 | tf_op jit(solution)/shard_map/ppermute | solution.py:524
  82.4 17.0 %copy-start.1 = (bf16[768,256]{1,0:T(8,128)(2,1)S(1)}, bf16[768,256]{1,0:T(8,128)(2,1)}, u32[]{:S(2)}) copy-start(bf16[768,256]{1,0:T(8,128)(2,1)} %constant.121.clone.over_lanes_ref) | copy-start | bytes 1179652
  82.4 17.0 %copy-start.4 = (bf16[384,256]{1,0:T(8,128)(2,1)S(1)}, bf16[384,256]{1,0:T(8,128)(2,1)}, u32[]{:S(2)}) copy-start(bf16[384,256]{1,0:T(8,128)(2,1)} %constant.124.clone.across_ref) | copy-start | bytes 589828
  82.4 17.0 %copy-start.5 = (bf16[128,384]{1,0:T(8,128)(2,1)S(1)}, bf16[128,384]{1,0:T(8,128)(2,1)}, u32[]{:S(2)}) copy-start(bf16[128,384]{1,0:T(8,128)(2,1)} %constant.120.clone.over_rows_ref) | copy-start | bytes 294916
  82.4 17.0 %copy-start.6 = (f32[2,64,128]{2,1,0:T(8,128)S(1)}, f32[2,64,128]{2,1,0:T(8,128)}, u32[]{:S(2)}) copy-start(f32[2,64,128]{2,1,0:T(8,128)} %constant.122.clone.twist_ref) | copy-start | bytes 196612
  82.5 16.9 %copy-start.7 = (bf16[64,192]{1,0:T(8,128)(2,1)S(1)}, bf16[64,192]{1,0:T(8,128)(2,1)}, u32[]{:S(2)}) copy-start(bf16[64,192]{1,0:T(8,128)(2,1)} %constant.123.clone.below_ref) | copy-start | bytes 73732
  85.0 4.4 %collective-permute-start.27 = (f32[2,64,128]{2,1,0:T(8,128)S(1)}, f32[2,64,128]{2,1,0:T(8,128)S(1)}, u32[]{:S(2)}, u32[]{:S(2)}) collective-permute-start(f32[2,64,128]{2,1,0:T(8,128)S(1)} %get-tuple-element.76), channel_id=1, source_target_pairs={{0,1},{1,0},{2,3},{3,2},{4,5},{5,4},{6,7},{7,6},{8,9},{9,8},{10,11... | collective-permute-start | bytes 196616 | tf_op jit(solution)/shard_map/ppermute | solution.py:412
  86.3 4.3 %collective-permute-start.28 = (f32[2,64,128]{2,1,0:T(8,128)S(1)}, f32[2,64,128]{2,1,0:T(8,128)S(1)}, u32[]{:S(2)}, u32[]{:S(2)}) collective-permute-start(f32[2,64,128]{2,1,0:T(8,128)S(1)} %get-tuple-element.76), channel_id=1, source_target_pairs={{0,3},{1,2},{2,1},{3,0},{4,7},{5,6},{6,5},{7,4},{8,11},{9,10},{10,... | collective-permute-start | bytes 196616 | tf_op jit(solution)/shard_map/ppermute | solution.py:426
  86.3 4.3 %collective-permute-start.26 = (f32[2,64,128]{2,1,0:T(8,128)S(1)}, f32[2,64,128]{2,1,0:T(8,128)S(1)}, u32[]{:S(2)}, u32[]{:S(2)}) collective-permute-start(f32[2,64,128]{2,1,0:T(8,128)S(1)} %get-tuple-element.76), channel_id=1, source_target_pairs={{0,2},{2,0},{4,6},{6,4},{8,10},{10,8},{12,14},{14,12},{1,3},{3,1},... | collective-permute-start | bytes 196616 | tf_op jit(solution)/shard_map/ppermute | solution.py:412
  90.6 7.4 %collective-permute-start.30 = (f32[2,64,128]{2,1,0:T(8,128)S(1)}, f32[2,64,128]{2,1,0:T(8,128)S(1)}, u32[]{:S(2)}, u32[]{:S(2)}) collective-permute-start(f32[2,64,128]{2,1,0:T(8,128)S(1)} %add_add_fusion.1), channel_id=1, source_target_pairs={{0,8},{2,10},{4,12},{6,14},{8,0},{10,2},{12,4},{14,6},{1,9},{3,11}... | collective-permute-start | bytes 196616 | tf_op jit(solution)/shard_map/ppermute | solution.py:412
  90.7 7.4 %collective-permute-start.31 = (f32[2,64,128]{2,1,0:T(8,128)S(1)}, f32[2,64,128]{2,1,0:T(8,128)S(1)}, u32[]{:S(2)}, u32[]{:S(2)}) collective-permute-start(f32[2,64,128]{2,1,0:T(8,128)S(1)} %add_add_fusion.1), channel_id=1, source_target_pairs={{0,12},{2,14},{4,8},{6,10},{8,4},{10,6},{12,0},{14,2},{1,13},{3,15... | collective-permute-start | bytes 196616 | tf_op jit(solution)/shard_map/ppermute | solution.py:412
  92.5 6.9 %collective-permute-start.29 = (f32[2,64,128]{2,1,0:T(8,128)S(1)}, f32[2,64,128]{2,1,0:T(8,128)S(1)}, u32[]{:S(2)}, u32[]{:S(2)}) collective-permute-start(f32[2,64,128]{2,1,0:T(8,128)S(1)} %add_add_fusion.1), channel_id=1, source_target_pairs={{0,4},{2,6},{4,0},{6,2},{8,12},{10,14},{12,8},{14,10},{1,5},{3,7},... | collective-permute-start | bytes 196616 | tf_op jit(solution)/shard_map/ppermute | solution.py:412
